TPU v7x, 32 devices: a whole 2x2x4 slice. The times are simulated.
32 devices in a mesh: dp: 2 (over core), expert: 4 (over z), tensor: 4 (over y, x).
Axes of the slice: x: 2, y: 2, z: 4, core: 2. Of those that a mesh axis runs over, the one named last changes fastest.
Arguments:
- layer_input: float32 [16384, 768], P(('dp', 'expert')), may hold values from -6 to 6
- cotangent: bfloat16 [16384, 768], P(('dp', 'expert')), may hold values from -6 to 6
- norm1_gain: bfloat16 [768], replicated, may hold values from 0.099609375 to 1.8984375
- w_query: bfloat16 [768, 768], P(None, 'tensor'), may hold values from -0.21875 to 0.21875
- w_key: bfloat16 [768, 768], P(None, 'tensor'), may hold values from -0.21875 to 0.21875
- w_value: bfloat16 [768, 768], P(None, 'tensor'), may hold values from -0.21875 to 0.21875
- w_output: bfloat16 [768, 768], P('tensor'), may hold values from -2.5 to 2.5
- bias_table: bfloat16 [32, 12], P(None, 'tensor'), may hold values from -6 to 6
- bucket: int32 [2047], replicated, may hold values from 0 to 31
- norm2_gain: bfloat16 [768], replicated, may hold values from 0.099609375 to 1.8984375
- router: bfloat16 [768, 4], replicated, may hold values from -0.15625 to 0.15625
- expert_index: int32 [16384, 1], P(('dp', 'expert')), may hold values from 0 to 3; in each aligned block of 512 rows (0 to 511, 512 to 1023, ...) at most 256 rows name the same one
- w_in: bfloat16 [4, 768, 3072], P('expert', None, 'tensor'), may hold values from -0.21875 to 0.21875
- w_out: bfloat16 [4, 3072, 768], P('expert', 'tensor'), may hold values from -0.4375 to 0.4375
Outputs:
- output: float32 [16384, 768], P(('dp', 'expert', 'tensor'))
- input_grad: float32 [16384, 768], P(('dp', 'expert', 'tensor'))
- grad_query: float32 [768, 768], P(None, 'tensor')
- grad_key: float32 [768, 768], P(None, 'tensor')
- grad_value: float32 [768, 768], P(None, 'tensor')
- grad_output_proj: float32 [768, 768], P('tensor')
- grad_bias_table: float32 [32, 12], P(None, 'tensor')
- grad_norm1: float32 [768], replicated
- grad_norm2: float32 [768], replicated
- grad_router: float32 [768, 4], replicated
- grad_w_in: float32 [4, 768, 3072], P('expert', None, 'tensor')
- grad_w_out: float32 [4, 3072, 768], P('expert', 'tensor')
Inputs may be any that keep to these rules, and one draw needn't show every extreme that they name: `expert_index`: in each aligned block of 512 rows (the rows of one device) no expert is named by more than 256 rows.
All inputs are finite; a program needn't handle non-finite values.
Results may differ from a plain program's by a relative error of at most 0.015.
Values may be sent and summed in bfloat16 or wider, within the bound.
No kernel may reach another device: no remote copies, remote signals or barrier semaphores. Data moves between devices by JAX's collectives and lax.ppermute only.
A program may use at most 320 MiB of HBM per device.

v0:
```python
import functools
import jax
import jax.numpy as jnp
from jax import lax
from jax.sharding import PartitionSpec as P
from jax.experimental import pallas as pl
from jax.experimental.pallas import tpu as pltpu

HEAD_DIM = 64
NUM_BUCKETS = 32
EPSILON = 1e-06
HIGHEST = lax.Precision.HIGHEST
CHUNK = 512
BAND = 128


def dot_nt(a, b):
    return lax.dot_general(a, b, (((1,), (1,)), ((), ())), preferred_element_type=jnp.float32)


def dot_nn(a, b):
    return lax.dot_general(a, b, (((1,), (0,)), ((), ())), preferred_element_type=jnp.float32)


def dot_tn(a, b):
    return lax.dot_general(a, b, (((0,), (0,)), ((), ())), preferred_element_type=jnp.float32)


def fill_band(band, vector):
    span = vector.shape[1]
    rows = jnp.broadcast_to(vector, (8, span))
    rows = pltpu.roll(rows, span - (BAND - 1), 1)
    index = lax.broadcasted_iota(jnp.int32, (8, span), 0)
    for step in (1, 2, 4):
        rows = jnp.where((index & step) != 0, pltpu.roll(rows, step, 1), rows)
    band[0:8, :] = rows
    step = 8
    while step < BAND:
        band[step : 2 * step, :] = pltpu.roll(band[0:step, :], step, 1)
        step *= 2


def fold_band(band):
    span = band.shape[1]
    step = BAND // 2
    while step >= 8:
        band[0:step, :] += pltpu.roll(band[step : 2 * step, :], span - step, 1)
        step //= 2
    rows = band[0:8, :]
    index = lax.broadcasted_iota(jnp.int32, (8, span), 0)
    for step in (1, 2, 4):
        rows = jnp.where((index & step) != 0, pltpu.roll(rows, span - step, 1), rows)
    total = jnp.sum(rows, axis=0, keepdims=True)
    return pltpu.roll(total, BAND - 1, 1)


def attend_kernel(q_ref, k_ref, v_ref, vec_ref, out_ref, log_ref, band):
    seq = k_ref.shape[3]
    own = out_ref.shape[3]

    @pl.when(pl.program_id(1) == 0)
    def _():
        fill_band(band, vec_ref[0])

    keys = k_ref[0, 0].T
    values = v_ref[0, 0]
    for start in range(0, seq, CHUNK):
        queries = q_ref[0, 0, :, start : start + CHUNK] * jnp.bfloat16(HEAD_DIM ** -0.5)
        raw = dot_nn(keys, queries)
        parts = []
        for low in range(0, seq, BAND):
            at = start - low + seq - BAND
            parts.append(raw[low : low + BAND] + band[:, at : at + CHUNK])
        peak = functools.reduce(jnp.maximum, parts)
        peak = jnp.max(peak, axis=0, keepdims=True)
        parts = [jnp.exp(part - peak) for part in parts]
        total = jnp.sum(functools.reduce(jnp.add, parts), axis=0, keepdims=True)
        weights = jnp.concatenate([part.astype(jnp.bfloat16) for part in parts], axis=0)
        mixed = dot_nn(values, weights) / total
        out_ref[start // own, 0, :, start % own : start % own + CHUNK] = mixed.astype(jnp.bfloat16)
        log_ref[0, 0, :, start : start + CHUNK] = peak + jnp.log(total)


def attend(projected, vectors, own):
    heads, seq = vectors.shape[0], vectors.shape[2] // 2
    seqs = projected.shape[1] // seq
    blocks = seq // own
    part = lambda p: pl.BlockSpec((1, 1, HEAD_DIM, seq), lambda h, s, p=p: (p, h, 0, s))
    proj = projected.reshape(3, heads, HEAD_DIM, seqs * seq)
    return pl.pallas_call(
        attend_kernel,
        grid=(heads, seqs),
        in_specs=[part(0), part(1), part(2), pl.BlockSpec((1, 1, 2 * seq), lambda h, s: (h, 0, 0))],
        out_specs=[
            pl.BlockSpec((blocks, 1, HEAD_DIM, own), lambda h, s: (s, h, 0, 0)),
            pl.BlockSpec((1, 1, 1, seq), lambda h, s: (h, s, 0, 0)),
        ],
        out_shape=[
            jax.ShapeDtypeStruct((seqs * blocks, heads, HEAD_DIM, own), jnp.bfloat16),
            jax.ShapeDtypeStruct((heads, seqs, 1, seq), jnp.float32),
        ],
        scratch_shapes=[pltpu.VMEM((BAND, 2 * seq), jnp.float32)],
        compiler_params=pltpu.CompilerParams(vmem_limit_bytes=48 * 2**20),
        cost_estimate=pl.CostEstimate(
            flops=4 * heads * seqs * seq * seq * HEAD_DIM * 4,
            bytes_accessed=4 * heads * seqs * seq * HEAD_DIM * 2,
            transcendentals=heads * seqs * seq * seq,
        ),
    )(proj, proj, proj, vectors)


def attend_back_kernel(q_ref, k_ref, v_ref, o_ref, g_ref, log_ref, vec_ref, out_ref, diag_ref, band, fold, dk, dv):
    seq = k_ref.shape[3]
    own = out_ref.shape[4]
    scale = HEAD_DIM ** -0.5

    @pl.when(pl.program_id(1) == 0)
    def _():
        fill_band(band, vec_ref[0])
        fold[...] = jnp.zeros_like(fold)

    keys_t = k_ref[0, 0]
    keys = keys_t.T
    values = v_ref[0, 0].T
    for start in range(0, seq, CHUNK):
        block, inner = start // own, start % own
        queries = q_ref[0, 0, :, start : start + CHUNK] * jnp.bfloat16(scale)
        grads = g_ref[block, 0, :, inner : inner + CHUNK]
        mixed = o_ref[block, 0, :, inner : inner + CHUNK]
        delta = jnp.sum(grads.astype(jnp.float32) * mixed.astype(jnp.float32), axis=0, keepdims=True)
        logs = log_ref[0, 0, :, start : start + CHUNK]
        raw = dot_nn(keys, queries)
        grad_weights = dot_nn(values, grads)
        low_weights, low_scores = [], []
        for low in range(0, seq, BAND):
            at = start - low + seq - BAND
            weights = jnp.exp(raw[low : low + BAND] + band[:, at : at + CHUNK] - logs)
            scores = weights * (grad_weights[low : low + BAND] - delta)
            fold[:, at : at + CHUNK] += scores
            low_weights.append(weights.astype(jnp.bfloat16))
            low_scores.append(scores.astype(jnp.bfloat16))
        weights = jnp.concatenate(low_weights, axis=0)
        scores = jnp.concatenate(low_scores, axis=0)
        grad_q = dot_nn(keys_t, scores) * scale
        out_ref[block, 0, 0, :, inner : inner + CHUNK] = grad_q.astype(jnp.bfloat16)
        if start == 0:
            dk[...] = dot_nt(queries, scores)
            dv[...] = dot_nt(grads, weights)
        else:
            dk[...] += dot_nt(queries, scores)
            dv[...] += dot_nt(grads, weights)
    for block in range(seq // own):
        out_ref[block, 1, 0] = dk[:, block * own : (block + 1) * own].astype(jnp.bfloat16)
        out_ref[block, 2, 0] = dv[:, block * own : (block + 1) * own].astype(jnp.bfloat16)

    @pl.when(pl.program_id(1) == pl.num_programs(1) - 1)
    def _():
        diag_ref[0] = fold_band(fold)


def attend_back(projected, vectors, mixed, grads, logs):
    heads, seq = vectors.shape[0], vectors.shape[2] // 2
    seqs = projected.shape[1] // seq
    own = mixed.shape[3]
    blocks = seq // own
    part = lambda p: pl.BlockSpec((1, 1, HEAD_DIM, seq), lambda h, s, p=p: (p, h, 0, s))
    side = pl.BlockSpec((blocks, 1, HEAD_DIM, own), lambda h, s: (s, h, 0, 0))
    vec = pl.BlockSpec((1, 1, 2 * seq), lambda h, s: (h, 0, 0))
    proj = projected.reshape(3, heads, HEAD_DIM, seqs * seq)
    return pl.pallas_call(
        attend_back_kernel,
        grid=(heads, seqs),
        in_specs=[part(0), part(1), part(2), side, side,
                  pl.BlockSpec((1, 1, 1, seq), lambda h, s: (h, s, 0, 0)), vec],
        out_specs=[
            pl.BlockSpec((blocks, 3, 1, HEAD_DIM, own), lambda h, s: (s, 0, h, 0, 0)),
            vec,
        ],
        out_shape=[
            jax.ShapeDtypeStruct((seqs * blocks, 3, heads, HEAD_DIM, own), jnp.bfloat16),
            jax.ShapeDtypeStruct((heads, 1, 2 * seq), jnp.float32),
        ],
        scratch_shapes=[
            pltpu.VMEM((BAND, 2 * seq), jnp.float32),
            pltpu.VMEM((BAND, 2 * seq), jnp.float32),
            pltpu.VMEM((HEAD_DIM, seq), jnp.float32),
            pltpu.VMEM((HEAD_DIM, seq), jnp.float32),
        ],
        compiler_params=pltpu.CompilerParams(vmem_limit_bytes=48 * 2**20),
        cost_estimate=pl.CostEstimate(
            flops=10 * heads * seqs * seq * seq * HEAD_DIM * 4,
            bytes_accessed=8 * heads * seqs * seq * HEAD_DIM * 2,
            transcendentals=heads * seqs * seq * seq,
        ),
    )(proj, proj, proj, mixed, grads, logs, vectors)


def gelu_parts(values):
    root = 0.7978845608028654
    square = values * values
    bend = jnp.tanh(root * values * (1.0 + 0.044715 * square))
    half = 0.5 * (1.0 + bend)
    slope = half + 0.5 * values * (1.0 - bend * bend) * (root * (1.0 + 3.0 * 0.044715 * square))
    return values * half, slope


def expert_kernel(x_ref, g_ref, gate_ref, in_ref, out_ref, act_ref, pre_ref, low_ref, res_ref, back_ref, gg_ref, res_sum, back_sum):
    step = pl.program_id(0)
    rows = x_ref.shape[0]
    tile = min(rows, 256)

    @pl.when(step == 0)
    def _():
        low_ref[...] = (gate_ref[...] * g_ref[...].astype(jnp.float32)).astype(jnp.bfloat16)
        res_sum[...] = jnp.zeros_like(res_sum)
        back_sum[...] = jnp.zeros_like(back_sum)

    first = in_ref[0]
    second = out_ref[0]
    for start in range(0, rows, tile):
        span = pl.ds(start, tile)
        active, slope = gelu_parts(dot_nn(x_ref[span, :], first))
        active = active.astype(jnp.bfloat16)
        act_ref[0, span, :] = active
        res_sum[span, :] += dot_nn(active, second)
        pre = (dot_nt(low_ref[span, :], second) * slope).astype(jnp.bfloat16)
        pre_ref[0, span, :] = pre
        back_sum[span, :] += dot_nt(pre, first)

    @pl.when(step == pl.num_programs(0) - 1)
    def _():
        res_ref[...] = res_sum[...].astype(jnp.bfloat16)
        back_ref[...] = back_sum[...].astype(jnp.bfloat16)
        gg_ref[...] = jnp.sum(res_sum[...] * g_ref[...].astype(jnp.float32), axis=1, keepdims=True)


def expert_apply(rows, grads, gates, first, second):
    count, width = rows.shape
    steps, _, hidden = first.shape
    whole = pl.BlockSpec((count, width), lambda i: (0, 0))
    column = pl.BlockSpec((count, 1), lambda i: (0, 0))
    kept = pl.BlockSpec((1, count, hidden), lambda i: (i, 0, 0))
    return pl.pallas_call(
        expert_kernel,
        grid=(steps,),
        in_specs=[
            whole,
            whole,
            column,
            pl.BlockSpec((1, width, hidden), lambda i: (i, 0, 0)),
            pl.BlockSpec((1, hidden, width), lambda i: (i, 0, 0)),
        ],
        out_specs=[kept, kept, whole, whole, whole, column],
        out_shape=[
            jax.ShapeDtypeStruct((steps, count, hidden), jnp.bfloat16),
            jax.ShapeDtypeStruct((steps, count, hidden), jnp.bfloat16),
            jax.ShapeDtypeStruct((count, width), jnp.bfloat16),
            jax.ShapeDtypeStruct((count, width), jnp.bfloat16),
            jax.ShapeDtypeStruct((count, width), jnp.bfloat16),
            jax.ShapeDtypeStruct((count, 1), jnp.float32),
        ],
        scratch_shapes=[
            pltpu.VMEM((count, width), jnp.float32),
            pltpu.VMEM((count, width), jnp.float32),
        ],
        compiler_params=pltpu.CompilerParams(vmem_limit_bytes=50 * 2**20),
        cost_estimate=pl.CostEstimate(
            flops=8 * count * width * hidden * steps,
            bytes_accessed=4 * (count + width) * hidden * steps,
            transcendentals=count * hidden * steps,
        ),
    )(rows, grads, gates, first, second)


def weight_kernel(x_ref, low_ref, act_ref, pre_ref, out_ref, x_turned, low_turned):
    @pl.when(pl.program_id(0) == 0)
    def _():
        x_turned[...] = x_ref[...].T
        low_turned[...] = low_ref[...].T

    out_ref[0, 0] = dot_nn(x_turned[...], pre_ref[0]).astype(jnp.bfloat16)
    out_ref[0, 1] = dot_nn(low_turned[...], act_ref[0]).astype(jnp.bfloat16)


def expert_weights(rows, low, act, pre):
    count, width = rows.shape
    steps, _, hidden = act.shape
    whole = pl.BlockSpec((count, width), lambda i: (0, 0))
    kept = pl.BlockSpec((1, count, hidden), lambda i: (i, 0, 0))
    return pl.pallas_call(
        weight_kernel,
        grid=(steps,),
        in_specs=[whole, whole, kept, kept],
        out_specs=pl.BlockSpec((1, 2, width, hidden), lambda i: (i, 0, 0, 0)),
        out_shape=jax.ShapeDtypeStruct((steps, 2, width, hidden), jnp.bfloat16),
        scratch_shapes=[
            pltpu.VMEM((width, count), jnp.bfloat16),
            pltpu.VMEM((width, count), jnp.bfloat16),
        ],
        compiler_params=pltpu.CompilerParams(vmem_limit_bytes=50 * 2**20),
        cost_estimate=pl.CostEstimate(
            flops=4 * count * width * hidden * steps,
            bytes_accessed=4 * (count + width) * hidden * steps,
            transcendentals=0,
        ),
    )(rows, low, act, pre)


def inverse_rms(rows):
    return lax.rsqrt(jnp.mean(rows * rows, axis=-1, keepdims=True) + EPSILON)


def norm_backward(grad_normed, gain, normed_hat, inv_scale):
    scaled = grad_normed * gain
    return inv_scale * (scaled - normed_hat * jnp.mean(scaled * normed_hat, axis=-1, keepdims=True))


def swap(array, axis, offset):
    count = lax.axis_size(axis)
    return lax.ppermute(array, axis, [(i, i ^ offset) for i in range(count)])


def trade(array, axis):
    return lax.all_to_all(array, axis, 0, 0, tiled=True)


def spread(array, axis):
    return trade(jnp.broadcast_to(array[None], (lax.axis_size(axis),) + array.shape), axis)


def split_low(values):
    high = values.astype(jnp.bfloat16)
    return high, (values - high.astype(jnp.float32)).astype(jnp.bfloat16)


def sum_copies(partial):
    rows, columns = partial.shape
    experts = lax.axis_size("expert")
    rank = lax.axis_index("dp")
    half = rows // 2
    mine = lax.dynamic_slice_in_dim(partial, rank * half, half, 0)
    other = lax.dynamic_slice_in_dim(partial, (1 - rank) * half, half, 0).astype(jnp.bfloat16)
    mine = (mine + swap(other, "dp", 1).astype(jnp.float32)).astype(jnp.bfloat16)
    shares = trade(mine.reshape(experts, half // experts, columns), "expert")
    share = jnp.sum(shares.astype(jnp.float32), axis=0).astype(jnp.bfloat16)
    mine = spread(share, "expert").reshape(half, columns)
    other = swap(mine, "dp", 1)
    first = rank == 0
    return jnp.concatenate(
        [jnp.where(first, mine, other), jnp.where(first, other, mine)], axis=0
    ).astype(jnp.float32)


def on_device(
    layer_input,
    cotangent,
    norm1_gain,
    w_query,
    w_key,
    w_value,
    w_output,
    bias_table,
    bucket,
    norm2_gain,
    router,
    expert_index,
    w_in,
    w_out,
):
    group_rows, width = layer_input.shape
    tensor_count = lax.axis_size("tensor")
    tensor_rank = lax.axis_index("tensor")
    dp_rank = lax.axis_index("dp")
    own_rows = group_rows // tensor_count
    own_start = tensor_rank * own_rows
    local_heads = bias_table.shape[1]
    inner = local_heads * HEAD_DIM
    experts = router.shape[1]
    capacity = 2 * own_rows // experts
    slots = experts * capacity

    hidden = w_in.shape[2]
    half = hidden // 2
    first_mine = lax.dynamic_slice_in_dim(w_in[0], dp_rank * half, half, 1)
    first_other = lax.dynamic_slice_in_dim(w_in[0], (1 - dp_rank) * half, half, 1)
    second_mine = lax.dynamic_slice_in_dim(w_out[0], dp_rank * half, half, 0)
    second_other = lax.dynamic_slice_in_dim(w_out[0], (1 - dp_rank) * half, half, 0)
    w_joined = jnp.concatenate([w_query, w_key, w_value], axis=1)
    w_joined_t = w_joined.T
    output_full = spread(w_output, "tensor").reshape(tensor_count * inner, width)

    routes = lax.dynamic_slice_in_dim(expert_index[:, 0], own_start, own_rows, 0)
    own_hot = routes[:, None] == jnp.arange(experts, dtype=jnp.int32)[None, :]
    row_ids = jnp.arange(own_rows, dtype=jnp.int32)
    earlier = (row_ids[None, :] < row_ids[:, None]).astype(jnp.bfloat16)
    before = jnp.dot(earlier, own_hot.astype(jnp.bfloat16), preferred_element_type=jnp.float32)
    own_hot = own_hot.astype(jnp.float32)
    slot = jnp.sum(before * own_hot, axis=-1).astype(jnp.int32)
    flat = routes * capacity + slot
    place_hot = (jnp.arange(slots, dtype=jnp.int32)[:, None] == flat[None, :]).astype(jnp.bfloat16)
    cot_low = lax.dynamic_slice_in_dim(cotangent, own_start, own_rows, 0)
    cot_own = cot_low.astype(jnp.float32)
    grad_send = jnp.dot(place_hot, cot_low, preferred_element_type=jnp.float32).astype(jnp.bfloat16)
    grad_in = trade(grad_send.reshape(experts, capacity, width), "expert").reshape(slots, width)

    gain_one = norm1_gain.astype(jnp.float32)
    inv_one = inverse_rms(layer_input)
    hat_one = layer_input * inv_one
    normed_one = (hat_one * gain_one).astype(jnp.bfloat16)
    projected = dot_nt(w_joined_t, normed_one).astype(jnp.bfloat16)
    turned = jnp.concatenate([bucket[::-1], jnp.full((1,), -1, jnp.int32)])
    bucket_hot = jnp.arange(NUM_BUCKETS, dtype=jnp.int32)[:, None] == turned[None, :]
    vectors = dot_tn(bias_table, bucket_hot.astype(jnp.bfloat16))[:, None, :]
    mixed, logs = attend(projected, vectors, own_rows)
    mixed_own = trade(mixed.reshape(tensor_count, inner, own_rows), "tensor").reshape(
        tensor_count * inner, own_rows
    )

    input_own = lax.dynamic_slice_in_dim(layer_input, own_start, own_rows, 0)
    residual = input_own + dot_tn(mixed_own, output_full)
    gain_two = norm2_gain.astype(jnp.float32)
    inv_two = inverse_rms(residual)
    hat_two = residual * inv_two
    normed_two = hat_two * gain_two
    router_wide = router.astype(jnp.float32)
    router_probs = jax.nn.softmax(jnp.dot(normed_two, router_wide, precision=HIGHEST), axis=-1)
    gate_full = jnp.sum(router_probs * own_hot, axis=-1)
    gate_low = gate_full.astype(jnp.bfloat16)
    send_rows = dot_nn(place_hot, normed_two.astype(jnp.bfloat16)).astype(jnp.bfloat16)
    send_gates = dot_nn(place_hot, gate_low[:, None]).astype(jnp.bfloat16)
    gate_rows = jnp.pad(send_gates.reshape(experts, 1, capacity), ((0, 0), (0, 7), (0, width - capacity)))
    sent = jnp.concatenate([send_rows.reshape(experts, capacity, width), gate_rows], axis=1)
    arrived = trade(sent, "expert")
    rows_in = arrived[:, :capacity].reshape(slots, width)
    gates_in = arrived[:, capacity, :capacity].reshape(slots, 1).astype(jnp.float32)

    first_parts, second_parts = [first_mine], [second_mine]
    for offset in range(1, tensor_count):
        first_parts.append(swap(first_mine, "tensor", offset))
        second_parts.append(swap(second_mine, "tensor", offset))
    first_rest = [first_other] + [swap(part, "dp", 1) for part in first_parts[1:]]
    second_rest = [second_other] + [swap(part, "dp", 1) for part in second_parts[1:]]
    first_all = jnp.stack(first_parts + first_rest)
    second_all = jnp.stack(second_parts + second_rest)

    act, pre, low_grads, result, back, grad_gates = expert_apply(
        rows_in, grad_in, gates_in, first_all, second_all
    )
    gate_high, gate_rest = split_low(grad_gates[:, 0])
    gate_pair = jnp.stack(
        [gate_high.reshape(experts, capacity), gate_rest.reshape(experts, capacity)], axis=1
    )
    gate_pair = jnp.pad(gate_pair, ((0, 0), (0, 6), (0, width - capacity)))
    back_sent = jnp.concatenate([back.reshape(experts, capacity, width), gate_pair], axis=1)
    back_got = trade(back_sent, "expert")
    weight_parts = expert_weights(rows_in, low_grads, act, pre)

    grad_normed_two = dot_tn(place_hot, back_got[:, :capacity].reshape(slots, width))
    pair_got = jnp.swapaxes(back_got[:, capacity : capacity + 2, :capacity], 1, 2).reshape(slots, 2)
    grad_gate = jnp.sum(dot_tn(place_hot, pair_got), axis=-1)
    grad_logits = router_probs * (own_hot - gate_full[:, None]) * grad_gate[:, None]
    grad_router = jnp.einsum("td,te->de", normed_two, grad_logits, precision=HIGHEST)
    grad_normed_two = grad_normed_two + jnp.einsum(
        "te,de->td", grad_logits, router_wide, precision=HIGHEST
    )
    grad_norm_two = jnp.sum(grad_normed_two * hat_two, axis=0)
    grad_residual = cot_own + norm_backward(grad_normed_two, gain_two, hat_two, inv_two)
    grad_low = grad_residual.astype(jnp.bfloat16)
    grad_heads = dot_nt(output_full, grad_low).astype(jnp.bfloat16)
    heads_got = trade(grad_heads.reshape(tensor_count, inner, own_rows), "tensor")

    result, heads_got = lax.optimization_barrier((result, heads_got))
    returned = trade(result.reshape(experts, capacity, width), "expert").reshape(slots, width)
    output = residual + gate_low.astype(jnp.float32)[:, None] * dot_tn(place_hot, returned)

    head_shape = (tensor_count, local_heads, HEAD_DIM, own_rows)
    grad_projected, diagonals = attend_back(
        projected, vectors, mixed, heads_got.reshape(head_shape), logs
    )
    grad_projected = grad_projected.reshape(tensor_count, 3 * inner, own_rows)
    joined_full = spread(w_joined_t, "tensor").reshape(tensor_count * 3 * inner, width)
    grad_got = trade(grad_projected, "tensor").reshape(tensor_count * 3 * inner, own_rows)
    grad_normed_one = dot_tn(grad_got, joined_full)
    hat_own = lax.dynamic_slice_in_dim(hat_one, own_start, own_rows, 0)
    inv_own = lax.dynamic_slice_in_dim(inv_one, own_start, own_rows, 0)
    input_grad = grad_residual + norm_backward(grad_normed_one, gain_one, hat_own, inv_own)

    grad_wo = dot_nn(mixed_own, grad_low).astype(jnp.bfloat16)
    grad_wo = trade(grad_wo.reshape(tensor_count, inner, width), "tensor")
    grad_wo = sum_copies(jnp.sum(grad_wo.astype(jnp.float32), axis=0))

    grad_joined = jnp.einsum(
        "bcn,bnd->dc",
        grad_projected,
        normed_one.reshape(tensor_count, own_rows, width),
        preferred_element_type=jnp.float32,
    )
    norm_one = jnp.sum(grad_joined * w_joined.astype(jnp.float32), axis=1) / gain_one
    norm_one = norm_one + sum(swap(norm_one, "tensor", k) for k in range(1, tensor_count))
    grad_table = jnp.einsum(
        "br,hr->bh", bucket_hot.astype(jnp.float32), diagonals[:, 0], precision=HIGHEST
    ).reshape(-1)
    table_size = grad_table.shape[0]
    extra = jnp.stack(
        [norm_one, jnp.pad(grad_table, (0, width - table_size))], axis=1
    )
    extra_high, extra_low = split_low(extra)
    extra = jnp.concatenate([extra_high, extra_low], axis=1).astype(jnp.float32)
    used = 3 * inner
    joined = jnp.concatenate(
        [grad_joined, extra, jnp.zeros((width, -(used + 4) % 128), jnp.float32)], axis=1
    )
    joined = sum_copies(joined)
    grad_norm_one = joined[:, used] + joined[:, used + 2]
    grad_table = (joined[:table_size, used + 1] + joined[:table_size, used + 3]).reshape(
        NUM_BUCKETS, local_heads
    )
    grad_norm_two, grad_router = lax.psum(
        (grad_norm_two, grad_router), ("dp", "expert", "tensor")
    )

    mine, other = weight_parts[:tensor_count], weight_parts[tensor_count:]
    mine = mine.astype(jnp.float32) + swap(other, "dp", 1).astype(jnp.float32)
    mine = mine.astype(jnp.bfloat16)
    total = mine[0].astype(jnp.float32)
    for offset in range(1, tensor_count):
        total = total + swap(mine[offset], "tensor", offset).astype(jnp.float32)
    total = total.astype(jnp.bfloat16)
    rest = swap(total, "dp", 1)
    first = dp_rank == 0
    both = jnp.concatenate(
        [jnp.where(first, total, rest), jnp.where(first, rest, total)], axis=2
    ).astype(jnp.float32)
    return (
        output,
        input_grad,
        joined[:, :inner],
        joined[:, inner : 2 * inner],
        joined[:, 2 * inner : used],
        grad_wo,
        grad_table,
        grad_norm_one,
        grad_norm_two,
        grad_router,
        both[0][None],
        both[1].T[None],
    )


def solution(mesh):
    return jax.shard_map(
        on_device,
        mesh=mesh,
        in_specs=(
            P(("dp", "expert"), None),
            P(("dp", "expert"), None),
            P(),
            P(None, "tensor"),
            P(None, "tensor"),
            P(None, "tensor"),
            P("tensor", None),
            P(None, "tensor"),
            P(),
            P(),
            P(),
            P(("dp", "expert"), None),
            P("expert", None, "tensor"),
            P("expert", "tensor", None),
        ),
        out_specs=(
            P(("dp", "expert", "tensor"), None),
            P(("dp", "expert", "tensor"), None),
            P(None, "tensor"),
            P(None, "tensor"),
            P(None, "tensor"),
            P("tensor", None),
            P(None, "tensor"),
            P(),
            P(),
            P(),
            P("expert", None, "tensor"),
            P("expert", "tensor", None),
        ),
        check_vma=False,
    )
```

profile of v0, /device:TPU:0, one launch (start us, length us, event | category | flops | bytes accessed | tf_op | source)
XLA Modules:
  0.0 553.0 jit_solution(10179240078591736734)
XLA Ops:
  4.5 6.2 %multiply_convert_fusion = (bf16[2048,768]{1,0:T(8,128)(2,1)S(1)}, f32[2048,768]{1,0:T(8,128)}) fusion(f32[768]{0:T(1024)S(1)} %convert_element_type.193, f32[2048,768]{1,0:T(8,128)} %param.14, f32[2048]{0:T(1024)S(1)} %add_rsqrt_fusion), kind=kLoop, calls=%fused_computation.1 | loop fusion | flops 4718592 | bytes 15739904 | tf_op jit(solution)/shard_map/convert_element_type | solution.py:409
  12.9 14.4 %shard_map.229 = (bf16[4,3,64,512]{3,2,1,0:T(8,128)(2,1)S(1)}, f32[3,2,1,1024]{3,2,1,0:T(1,128)S(1)}) custom-call(bf16[3,3,64,2048]{3,2,1,0:T(8,128)(2,1)S(1)} %bitcast.113, bf16[3,3,64,2048]{3,2,1,0:T(8,128)(2,1)S(1)} %bitcast.114, bf16[3,3,64,2048]{3,2,1,0:T(8,128)(2,1)S(1)} %bitcast.115, f32[3,1,2048]{2,1,0:T(1,128)S(1)} %broadcast_in_dim.14.vec_ref), custom_call_target="tpu_custom_call" | custom-call | flops 6442450944 | bytes 3145728 | tf_op jit(solution)/shard_map/pallas_call | solution.py:90
  27.3 16.3 %all_to_all.70 = bf16[4,192,512]{2,1,0:T(8,128)(2,1)S(1)} all-to-all(bf16[4,192,512]{2,1,0:T(8,128)(2,1)S(1)} %bitcast.111), channel_id=1, replica_groups=mesh['dp'=2,'expert'=4,'tensor'=4] {'tensor'}, dimensions={0} | all-to-all | bytes 1572864 | tf_op jit(solution)/shard_map/all_to_all | solution.py:324
  49.5 13.5 %all-to-all-done.1 = bf16[4,192,768]{2,1,0:T(8,128)(2,1)} async-done(((bf16[4,192,768]{2,1,0:T(8,128)(2,1)}), bf16[4,192,768]{2,1,0:T(8,128)(2,1)}, u32[]{:S(2)}, u32[]{:S(2)}) %all-to-all-start.1) | async-done | bytes 1179680 | tf_op jit(solution)/shard_map/all_to_all | solution.py:324
  72.8 4.9 all-to-all-start.2
  89.8 6.7 %collective-permute-done.6 = bf16[384,768]{1,0:T(8,128)(2,1)} collective-permute-done((bf16[384,768]{1,0:T(8,128)(2,1)}, bf16[384,768]{1,0:T(8,128)(2,1)}, u32[]{:S(2)}, u32[]{:S(2)}) %collective-permute-start.6) | collective-permute-done | bytes 589856 | tf_op jit(solution)/shard_map/ppermute | solution.py:320
  99.9 10.7 %collective-permute-done.7 = bf16[384,768]{1,0:T(8,128)(2,1)} collective-permute-done((bf16[384,768]{1,0:T(8,128)(2,1)}, bf16[384,768]{1,0:T(8,128)(2,1)}, u32[]{:S(2)}, u32[]{:S(2)}) %collective-permute-start.7) | collective-permute-done | bytes 589856 | tf_op jit(solution)/shard_map/ppermute | solution.py:320
  115.9 5.3 all-to-all-start.3
  123.8 8.2 %collective-permute-done.1 = bf16[768,384]{1,0:T(8,128)(2,1)S(1)} collective-permute-done((bf16[768,384]{1,0:T(8,128)(2,1)}, bf16[768,384]{1,0:T(8,128)(2,1)S(1)}, u32[]{:S(2)}, u32[]{:S(2)}) %collective-permute-start.1) | collective-permute-done | bytes 589856 | tf_op jit(solution)/shard_map/ppermute | solution.py:320
  147.3 11.1 %all-to-all-done.3 = bf16[4,256,768]{2,1,0:T(8,128)(2,1)} async-done(((bf16[4,256,768]{2,1,0:T(8,128)(2,1)}), bf16[4,256,768]{2,1,0:T(8,128)(2,1)}, u32[]{:S(2)}, u32[]{:S(2)}) %all-to-all-start.3) | async-done | bytes 1572896 | tf_op jit(solution)/shard_map/all_to_all | solution.py:324
  158.4 39.5 %shard_map.230 = (bf16[8,1024,384]{2,1,0:T(8,128)(2,1)}, bf16[8,1024,384]{2,1,0:T(8,128)(2,1)}, bf16[1024,768]{1,0:T(8,128)(2,1)S(1)}, bf16[1024,768]{1,0:T(8,12...) custom-call(bf16[1024,768]{1,0:T(8,128)(2,1)} %bitcast.109, bf16[1024,768]{1,0:T(8,128)(2,1)} %bitcast.9.g_ref, ...), custom_call_target="tpu_custom_call" | custom-call | flops 19327352832 | bytes 22020096 | tf_op jit(solution)/shard_map/pallas_call | solution.py:243
  200.9 40.0 %all_to_all.71 = bf16[4,264,768]{2,1,0:T(8,128)(2,1)S(1)} all-to-all(bf16[4,264,768]{2,1,0:T(8,128)(2,1)S(1)} %fusion.14), channel_id=1, replica_groups=mesh['dp'=2,'expert'=4,'tensor'=4] {'expert'}, dimensions={0} | all-to-all | bytes 3244032 | tf_op jit(solution)/shard_map/all_to_all | solution.py:324
  248.6 4.4 all-to-all-start.11
  256.3 10.8 %all-to-all-done.11 = bf16[4,192,768]{2,1,0:T(8,128)(2,1)} async-done(((bf16[4,192,768]{2,1,0:T(8,128)(2,1)}), bf16[4,192,768]{2,1,0:T(8,128)(2,1)}, u32[]{:S(2)}, u32[]{:S(2)}) %all-to-all-start.11) | async-done | bytes 1179680 | tf_op jit(solution)/shard_map/all_to_all | solution.py:324
  276.3 4.8 all-to-all-done.5
  285.8 17.8 %shard_map.232 = bf16[8,2,768,384]{3,2,1,0:T(8,128)(2,1)} custom-call(bf16[1024,768]{1,0:T(8,128)(2,1)S(1)} %bitcast.110, bf16[1024,768]{1,0:T(8,128)(2,1)S(1)} %copy-done.5, bf16[8,1024,384]{2,1,0:T(8,128)(2,1)} %get-tuple-element.34.act_ref, bf16[8,1024,384]{2,1,0:T(8,128)(2,1)} %get-tuple-element.35.pre_ref), custom_call_target="tpu_custom_call" | custom-call | flops 9663676416 | bytes 22020096 | tf_op jit(solution)/shard_map/pallas_call | solution.py:290
  303.6 5.1 slice.86
  310.7 4.7 all-to-all-start.8
  315.4 24.3 %shard_map.231 = (bf16[4,3,3,64,512]{4,3,2,1,0:T(8,128)(2,1)}, f32[3,1,2048]{2,1,0:T(1,128)S(1)}) custom-call(bf16[3,3,64,2048]{3,2,1,0:T(8,128)(2,1)} %bitcast.116, bf16[3,3,64,2048]{3,2,1,0:T(8,128)(2,1)} %bitcast.117, bf16[3,3,64,2048]{3,2,1,0:T(8,128)(2,1)} %bitcast.118, bf16[4,3,64,512]{3,2,1,0:T(8,128)(2,1)S(1)} %get-tuple-element.24.o_ref, ...), custom_call_target="tpu_custom_call" | custom-call | flops 16106127360 | bytes 6291456 | tf_op jit(solution)/shard_map/pallas_call | solution.py:170
  339.7 4.9 multiply_reduce_fusion.1
  348.5 8.4 %collective-permute-done.12 = f32[768]{0:T(1024)S(1)} collective-permute-done((f32[768]{0:T(1024)S(1)}, f32[768]{0:T(1024)S(1)}, u32[]{:S(2)}, u32[]{:S(2)}) %collective-permute-start.12) | collective-permute-done | bytes 3104 | tf_op jit(solution)/shard_map/ppermute | solution.py:320
  360.4 5.1 all-to-all-start.13
  366.8 5.3 all-to-all-done.13
  372.1 16.3 %all_to_all.72 = bf16[4,96,640]{2,1,0:T(8,128)(2,1)S(1)} all-to-all(bf16[4,96,640]{2,1,0:T(8,128)(2,1)S(1)} %bitcast.124), channel_id=1, replica_groups=mesh['dp'=2,'expert'=4,'tensor'=4] {'expert'}, dimensions={0} | all-to-all | bytes 983040 | tf_op jit(solution)/shard_map/all_to_all | solution.py:324
  388.4 4.5 all-to-all-start.7
  393.0 26.9 %all-to-all-done.7 = bf16[4,576,512]{2,1,0:T(8,128)(2,1)} async-done(((bf16[4,576,512]{2,1,0:T(8,128)(2,1)}), bf16[4,576,512]{2,1,0:T(8,128)(2,1)}, u32[]{:S(2)}, u32[]{:S(2)}) %all-to-all-start.7) | async-done | bytes 2359328 | tf_op jit(solution)/shard_map/all_to_all | solution.py:324
  425.4 40.0 %all-reduce.3 = (f32[768]{0:T(1024)}, f32[768,4]{0,1:T(4,128)}) all-reduce(f32[768]{0:T(1024)S(1)} %get-tuple-element.96, f32[768,4]{0,1:T(4,128)S(1)} %fusion.16), channel_id=1, replica_groups=mesh['dp'=2,'expert'=4,'tensor'=4] {'dp','expert','tensor'}, use_global_device_ids=true, to_apply=%region_14.15 | all-reduce | flops 3840 | bytes 30720 | tf_op jit(solution)/shard_map/psum | solution.py:518
  466.3 4.6 all-to-all-start.6
  470.9 4.9 add_convert_fusion
  480.6 5.4 multiply_reduce_fusion.3
  489.0 16.4 %collective-permute-done.20 = bf16[2,768,384]{2,1,0:T(8,128)(2,1)S(1)} collective-permute-done((bf16[2,768,384]{2,1,0:T(8,128)(2,1)S(1)}, bf16[2,768,384]{2,1,0:T(8,128)(2,1)S(1)}, u32[]{:S(2)}, u32[]{:S(2)}) %collective-permute-start.20) | collective-permute-done | bytes 1179680 | tf_op jit(solution)/shard_map/ppermute | solution.py:320
  505.4 25.7 %collective-permute-done.21 = bf16[2,768,384]{2,1,0:T(8,128)(2,1)S(1)} collective-permute-done((bf16[2,768,384]{2,1,0:T(8,128)(2,1)S(1)}, bf16[2,768,384]{2,1,0:T(8,128)(2,1)S(1)}, u32[]{:S(2)}, u32[]{:S(2)}) %collective-permute-start.21) | collective-permute-done | bytes 1179680 | tf_op jit(solution)/shard_map/ppermute | solution.py:320
  (233 shorter events, 134.2 us)
Async XLA Ops:
  44.8 18.1 %all-to-all-start.1 = ((bf16[4,192,768]{2,1,0:T(8,128)(2,1)}), bf16[4,192,768]{2,1,0:T(8,128)(2,1)}, u32[]{:S(2)}, u32[]{:S(2)}) async-start(bf16[4,192,768]{2,1,0:T(8,128)(2,1)} %broadcast_in_dim.15), calls=%async_computation.1 | async-start | bytes 2359296 | tf_op jit(solution)/shard_map/all_to_all | solution.py:324
  72.8 43.1 %all-to-all-start.2 = ((bf16[4,264,768]{2,1,0:T(8,128)(2,1)}), bf16[4,264,768]{2,1,0:T(8,128)(2,1)}, u32[]{:S(2)}, u32[]{:S(2)}) async-start(bf16[4,264,768]{2,1,0:T(8,128)(2,1)} %fusion.13), calls=%async_computation.2 | async-start | bytes 3244032 | tf_op jit(solution)/shard_map/all_to_all | solution.py:324
  79.9 16.6 %collective-permute-start.6 = (bf16[384,768]{1,0:T(8,128)(2,1)}, bf16[384,768]{1,0:T(8,128)(2,1)}, u32[]{:S(2)}, u32[]{:S(2)}) collective-permute-start(bf16[384,768]{1,0:T(8,128)(2,1)} %get-tuple-element.118), channel_id=1, source_target_pairs={{0,1},{1,0},{2,3},{3,2},{4,5},{5,4},{6,7},{7,6},{8,9},{9,8},{10,11... | collective-permute-start | bytes 1769480 | tf_op jit(solution)/shard_map/ppermute | solution.py:320
  81.4 29.2 %collective-permute-start.7 = (bf16[384,768]{1,0:T(8,128)(2,1)}, bf16[384,768]{1,0:T(8,128)(2,1)}, u32[]{:S(2)}, u32[]{:S(2)}) collective-permute-start(bf16[384,768]{1,0:T(8,128)(2,1)} %get-tuple-element.118), channel_id=1, source_target_pairs={{0,2},{1,3},{2,0},{3,1},{4,6},{5,7},{6,4},{7,5},{8,10},{9,11},{10,... | collective-permute-start | bytes 1769480 | tf_op jit(solution)/shard_map/ppermute | solution.py:320
  81.9 30.6 %collective-permute-start.8 = (bf16[384,768]{1,0:T(8,128)(2,1)}, bf16[384,768]{1,0:T(8,128)(2,1)}, u32[]{:S(2)}, u32[]{:S(2)}) collective-permute-start(bf16[384,768]{1,0:T(8,128)(2,1)} %get-tuple-element.118), channel_id=1, source_target_pairs={{0,3},{1,2},{2,1},{3,0},{4,7},{5,6},{6,5},{7,4},{8,11},{9,10},{10,... | collective-permute-start | bytes 1769480 | tf_op jit(solution)/shard_map/ppermute | solution.py:320
  84.5 37.3 %collective-permute-start = (bf16[768,384]{1,0:T(8,128)(2,1)}, bf16[768,384]{1,0:T(8,128)(2,1)}, u32[]{:S(2)}, u32[]{:S(2)}) collective-permute-start(bf16[768,384]{1,0:T(8,128)(2,1)} %get-tuple-element.120), channel_id=1, source_target_pairs={{0,1},{1,0},{2,3},{3,2},{4,5},{5,4},{6,7},{7,6},{8,9},{9,8},{10,11... | collective-permute-start | bytes 1769480 | tf_op jit(solution)/shard_map/ppermute | solution.py:320
  86.0 46.1 %collective-permute-start.1 = (bf16[768,384]{1,0:T(8,128)(2,1)}, bf16[768,384]{1,0:T(8,128)(2,1)S(1)}, u32[]{:S(2)}, u32[]{:S(2)}) collective-permute-start(bf16[768,384]{1,0:T(8,128)(2,1)} %get-tuple-element.120), channel_id=1, source_target_pairs={{0,2},{1,3},{2,0},{3,1},{4,6},{5,7},{6,4},{7,5},{8,10},{9,11},{10,... | collective-permute-start | bytes 1769480 | tf_op jit(solution)/shard_map/ppermute | solution.py:320
  96.5 36.4 %collective-permute-start.2 = (bf16[768,384]{1,0:T(8,128)(2,1)}, bf16[768,384]{1,0:T(8,128)(2,1)}, u32[]{:S(2)}, u32[]{:S(2)}) collective-permute-start(bf16[768,384]{1,0:T(8,128)(2,1)} %get-tuple-element.120), channel_id=1, source_target_pairs={{0,3},{1,2},{2,1},{3,0},{4,7},{5,6},{6,5},{7,4},{8,11},{9,10},{10,... | collective-permute-start | bytes 1769480 | tf_op jit(solution)/shard_map/ppermute | solution.py:320
  110.6 25.7 %collective-permute-start.9 = (bf16[384,768]{1,0:T(8,128)(2,1)}, bf16[384,768]{1,0:T(8,128)(2,1)}, u32[]{:S(2)}, u32[]{:S(2)}) collective-permute-start(bf16[384,768]{1,0:T(8,128)(2,1)} %collective-permute-done.6), channel_id=1, source_target_pairs={{0,16},{16,0},{1,17},{17,1},{2,18},{18,2},{3,19},{19,3},{4,20},{20... | collective-permute-start | bytes 1769480 | tf_op jit(solution)/shard_map/ppermute | solution.py:320
  112.5 25.7 %collective-permute-start.10 = (bf16[384,768]{1,0:T(8,128)(2,1)}, bf16[384,768]{1,0:T(8,128)(2,1)}, u32[]{:S(2)}, u32[]{:S(2)}) collective-permute-start(bf16[384,768]{1,0:T(8,128)(2,1)} %collective-permute-done.7), channel_id=1, source_target_pairs={{0,16},{16,0},{1,17},{17,1},{2,18},{18,2},{3,19},{19,3},{4,20},{20... | collective-permute-start | bytes 1769480 | tf_op jit(solution)/shard_map/ppermute | solution.py:320
  115.9 42.5 %all-to-all-start.3 = ((bf16[4,256,768]{2,1,0:T(8,128)(2,1)}), bf16[4,256,768]{2,1,0:T(8,128)(2,1)}, u32[]{:S(2)}, u32[]{:S(2)}) async-start(bf16[4,256,768]{2,1,0:T(8,128)(2,1)} %bitcast.126), calls=%async_computation.3 | async-start | bytes 3145728 | tf_op jit(solution)/shard_map/all_to_all | solution.py:324
  121.8 18.3 %collective-permute-start.11 = (bf16[384,768]{1,0:T(8,128)(2,1)}, bf16[384,768]{1,0:T(8,128)(2,1)S(1)}, u32[]{:S(2)}, u32[]{:S(2)}) collective-permute-start(bf16[384,768]{1,0:T(8,128)(2,1)} %collective-permute-done.8), channel_id=1, source_target_pairs={{0,16},{16,0},{1,17},{17,1},{2,18},{18,2},{3,19},{19,3},{4,20},{20... | collective-permute-start | bytes 1769480 | tf_op jit(solution)/shard_map/ppermute | solution.py:320
  132.0 9.0 %collective-permute-start.3 = (bf16[768,384]{1,0:T(8,128)(2,1)}, bf16[768,384]{1,0:T(8,128)(2,1)S(1)}, u32[]{:S(2)}, u32[]{:S(2)}) collective-permute-start(bf16[768,384]{1,0:T(8,128)(2,1)} %collective-permute-done), channel_id=1, source_target_pairs={{0,16},{16,0},{1,17},{17,1},{2,18},{18,2},{3,19},{19,3},{4,20},{20... | collective-permute-start | bytes 1769480 | tf_op jit(solution)/shard_map/ppermute | solution.py:320
  132.9 9.0 %collective-permute-start.4 = (bf16[768,384]{1,0:T(8,128)(2,1)S(1)}, bf16[768,384]{1,0:T(8,128)(2,1)S(1)}, u32[]{:S(2)}, u32[]{:S(2)}) collective-permute-start(bf16[768,384]{1,0:T(8,128)(2,1)S(1)} %collective-permute-done.1), channel_id=1, source_target_pairs={{0,16},{16,0},{1,17},{17,1},{2,18},{18,2},{3,19},{19,3},{4,20},{20... | collective-permute-start | bytes 1769480 | tf_op jit(solution)/shard_map/ppermute | solution.py:320
  248.6 18.5 %all-to-all-start.11 = ((bf16[4,192,768]{2,1,0:T(8,128)(2,1)}), bf16[4,192,768]{2,1,0:T(8,128)(2,1)}, u32[]{:S(2)}, u32[]{:S(2)}) async-start(bf16[4,192,768]{2,1,0:T(8,128)(2,1)} %bitcast.119), calls=%async_computation.11 | async-start | bytes 2359296 | tf_op jit(solution)/shard_map/all_to_all | solution.py:324
  267.0 14.1 %all-to-all-start.5 = ((bf16[4,192,512]{2,1,0:T(8,128)(2,1)}), bf16[4,192,512]{2,1,0:T(8,128)(2,1)S(1)}, u32[]{:S(2)}, u32[]{:S(2)}) async-start(bf16[4,192,512]{2,1,0:T(8,128)(2,1)} %bitcast.121), calls=%async_computation.5 | async-start | bytes 1572864 | tf_op jit(solution)/shard_map/all_to_all | solution.py:324
  281.1 27.6 %all-to-all-start.12 = ((bf16[4,24,768]{2,1,0:T(8,128)(2,1)}), bf16[4,24,768]{2,1,0:T(8,128)(2,1)S(1)}, u32[]{:S(2)}, u32[]{:S(2)}) async-start(bf16[4,24,768]{2,1,0:T(8,128)(2,1)} %bitcast.44), calls=%async_computation.12 | async-start | bytes 294912 | tf_op jit(solution)/shard_map/all_to_all | solution.py:324
  308.7 162.2 %collective-permute-start.19 = (bf16[4,2,768,384]{3,2,1,0:T(8,128)(2,1)}, bf16[4,2,768,384]{3,2,1,0:T(8,128)(2,1)}, u32[]{:S(2)}, u32[]{:S(2)}) collective-permute-start(bf16[4,2,768,384]{3,2,1,0:T(8,128)(2,1)} %slice.86), channel_id=1, source_target_pairs={{0,16},{16,0},{1,17},{17,1},{2,18},{18,2},{3,19},{19,3},{4,20},{20... | collective-permute-start | bytes 14155784 | tf_op jit(solution)/shard_map/ppermute | solution.py:320
  310.7 49.0 %all-to-all-start.8 = ((bf16[4,576,768]{2,1,0:T(8,128)(2,1)}), bf16[4,576,768]{2,1,0:T(8,128)(2,1)}, u32[]{:S(2)}, u32[]{:S(2)}) async-start(bf16[4,576,768]{2,1,0:T(8,128)(2,1)} %broadcast_in_dim.16), calls=%async_computation.8 | async-start | bytes 7077888 | tf_op jit(solution)/shard_map/all_to_all | solution.py:324
  344.6 12.3 %collective-permute-start.12 = (f32[768]{0:T(1024)S(1)}, f32[768]{0:T(1024)S(1)}, u32[]{:S(2)}, u32[]{:S(2)}) collective-permute-start(f32[768]{0:T(1024)S(1)} %convert_divide_fusion), channel_id=1, source_target_pairs={{0,1},{1,0},{2,3},{3,2},{4,5},{5,4},{6,7},{7,6},{8,9},{9,8},{10,11... | collective-permute-start | bytes 9224 | tf_op jit(solution)/shard_map/ppermute | solution.py:320
  346.5 10.3 %collective-permute-start.13 = (f32[768]{0:T(1024)S(1)}, f32[768]{0:T(1024)S(1)}, u32[]{:S(2)}, u32[]{:S(2)}) collective-permute-start(f32[768]{0:T(1024)S(1)} %convert_divide_fusion), channel_id=1, source_target_pairs={{0,2},{1,3},{2,0},{3,1},{4,6},{5,7},{6,4},{7,5},{8,10},{9,11},{10,... | collective-permute-start | bytes 9224 | tf_op jit(solution)/shard_map/ppermute | solution.py:320
  348.0 9.7 %collective-permute-start.14 = (f32[768]{0:T(1024)S(1)}, f32[768]{0:T(1024)S(1)}, u32[]{:S(2)}, u32[]{:S(2)}) collective-permute-start(f32[768]{0:T(1024)S(1)} %convert_divide_fusion), channel_id=1, source_target_pairs={{0,3},{1,2},{2,1},{3,0},{4,7},{5,6},{6,5},{7,4},{8,11},{9,10},{10,... | collective-permute-start | bytes 9224 | tf_op jit(solution)/shard_map/ppermute | solution.py:320
  360.4 11.7 %all-to-all-start.13 = ((bf16[4,24,768]{2,1,0:T(8,128)(2,1)}), bf16[4,24,768]{2,1,0:T(8,128)(2,1)S(1)}, u32[]{:S(2)}, u32[]{:S(2)}) async-start(bf16[4,24,768]{2,1,0:T(8,128)(2,1)} %broadcast_in_dim.19), calls=%async_computation.13 | async-start | bytes 294912 | tf_op jit(solution)/shard_map/all_to_all | solution.py:324
  388.4 31.5 %all-to-all-start.7 = ((bf16[4,576,512]{2,1,0:T(8,128)(2,1)}), bf16[4,576,512]{2,1,0:T(8,128)(2,1)}, u32[]{:S(2)}, u32[]{:S(2)}) async-start(bf16[4,576,512]{2,1,0:T(8,128)(2,1)} %bitcast.35), calls=%async_computation.7 | async-start | bytes 4718592 | tf_op jit(solution)/shard_map/all_to_all | solution.py:324
  420.7 45.6 %all-to-all-start.10 = ((bf16[4,96,640]{2,1,0:T(8,128)(2,1)}), bf16[4,96,640]{2,1,0:T(8,128)(2,1)S(1)}, u32[]{:S(2)}, u32[]{:S(2)}) async-start(bf16[4,96,640]{2,1,0:T(8,128)(2,1)} %broadcast_in_dim.18), calls=%async_computation.10 | async-start | bytes 983040 | tf_op jit(solution)/shard_map/all_to_all | solution.py:324
  424.3 41.1 %collective-permute-start.18 = (bf16[96,768]{1,0:T(8,128)(2,1)S(1)}, bf16[96,768]{1,0:T(8,128)(2,1)S(1)}, u32[]{:S(2)}, u32[]{:S(2)}) collective-permute-start(bf16[96,768]{1,0:T(8,128)(2,1)S(1)} %bitcast.131), channel_id=1, source_target_pairs={{0,16},{16,0},{1,17},{17,1},{2,18},{18,2},{3,19},{19,3},{4,20},{20... | collective-permute-start | bytes 442376 | tf_op jit(solution)/shard_map/ppermute | solution.py:320
  466.3 66.4 %all-to-all-start.6 = ((bf16[4,256,768]{2,1,0:T(8,128)(2,1)}), bf16[4,256,768]{2,1,0:T(8,128)(2,1)}, u32[]{:S(2)}, u32[]{:S(2)}) async-start(bf16[4,256,768]{2,1,0:T(8,128)(2,1)} %bitcast.125), calls=%async_computation.6 | async-start | bytes 3145728 | tf_op jit(solution)/shard_map/all_to_all | solution.py:324
  476.2 29.2 %collective-permute-start.20 = (bf16[2,768,384]{2,1,0:T(8,128)(2,1)S(1)}, bf16[2,768,384]{2,1,0:T(8,128)(2,1)S(1)}, u32[]{:S(2)}, u32[]{:S(2)}) collective-permute-start(bf16[2,768,384]{2,1,0:T(8,128)(2,1)S(1)} %get-tuple-element.110), channel_id=1, source_target_pairs={{0,1},{1,0},{2,3},{3,2},{4,5},{5,4},{6,7},{7,6},{8,9},{9,8},{10,11... | collective-permute-start | bytes 3538952 | tf_op jit(solution)/shard_map/ppermute | solution.py:320
  478.6 52.5 %collective-permute-start.21 = (bf16[2,768,384]{2,1,0:T(8,128)(2,1)S(1)}, bf16[2,768,384]{2,1,0:T(8,128)(2,1)S(1)}, u32[]{:S(2)}, u32[]{:S(2)}) collective-permute-start(bf16[2,768,384]{2,1,0:T(8,128)(2,1)S(1)} %get-tuple-element.112), channel_id=1, source_target_pairs={{0,2},{1,3},{2,0},{3,1},{4,6},{5,7},{6,4},{7,5},{8,10},{9,11},{10,... | collective-permute-start | bytes 3538952 | tf_op jit(solution)/shard_map/ppermute | solution.py:320
  480.6 50.4 %collective-permute-start.22 = (bf16[2,768,384]{2,1,0:T(8,128)(2,1)S(1)}, bf16[2,768,384]{2,1,0:T(8,128)(2,1)S(1)}, u32[]{:S(2)}, u32[]{:S(2)}) collective-permute-start(bf16[2,768,384]{2,1,0:T(8,128)(2,1)S(1)} %get-tuple-element.111), channel_id=1, source_target_pairs={{0,3},{1,2},{2,1},{3,0},{4,7},{5,6},{6,5},{7,4},{8,11},{9,10},{10,... | collective-permute-start | bytes 3538952 | tf_op jit(solution)/shard_map/ppermute | solution.py:320
  488.9 47.6 %collective-permute-start.16 = (bf16[384,640]{1,0:T(8,128)(2,1)S(1)}, bf16[384,640]{1,0:T(8,128)(2,1)}, u32[]{:S(2)}, u32[]{:S(2)}) collective-permute-start(bf16[384,640]{1,0:T(8,128)(2,1)S(1)} %bitcast.123), channel_id=1, source_target_pairs={{0,16},{16,0},{1,17},{17,1},{2,18},{18,2},{3,19},{19,3},{4,20},{20... | collective-permute-start | bytes 1474568 | tf_op jit(solution)/shard_map/ppermute | solution.py:320
  532.7 14.0 %collective-permute-start.23 = (bf16[2,768,384]{2,1,0:T(8,128)(2,1)}, bf16[2,768,384]{2,1,0:T(8,128)(2,1)}, u32[]{:S(2)}, u32[]{:S(2)}) collective-permute-start(bf16[2,768,384]{2,1,0:T(8,128)(2,1)} %fusion.4), channel_id=1, source_target_pairs={{0,16},{16,0},{1,17},{17,1},{2,18},{18,2},{3,19},{19,3},{4,20},{20... | collective-permute-start | bytes 3538952 | tf_op jit(solution)/shard_map/ppermute | solution.py:320
  (38 other events, 806.7 us)
where the time goes:
time: 564 us; the launch traced here: 553 us
  waiting for transfers between devices  151 us (27%)
  blocking collectives  113 us (20%)
  Pallas kernels  96.1 us (17%)
  starting transfers between devices  64.3 us (11%)
  local copies, waits for them, and re-layouts  55 us (10%)
  other arithmetic  37.4 us (7%)
  matrix products  34.4 us (6%)
    ppermute x24, waiting for transfers between devices, swap(): return lax.ppermute(array, axis, [(i, i ^ offset) for i in range(count)])  79 us
    all_to_all x3, blocking collectives, trade(): return lax.all_to_all(array, axis, 0, 0, tiled=True)  72.6 us
    all_to_all x11, waiting for transfers between devices, trade(): return lax.all_to_all(array, axis, 0, 0, tiled=True)  72.3 us
    all_to_all x11, starting transfers between devices, trade(): return lax.all_to_all(array, axis, 0, 0, tiled=True)  48.4 us
    psum x1, blocking collectives, on_device(): lax.psum((grad_norm_two, grad_router), ('dp', 'expert', 'tensor'))  40 us
    pallas_call x1, Pallas kernels, expert_apply(): pl.pallas_call(expert_kernel, grid=(steps,), in_specs=[whole, whole, colu...  39.5 us
    unnamed x92, local copies, waits for them, and re-layouts  31 us
    pallas_call x1, Pallas kernels, attend_back(): pl.pallas_call(attend_back_kernel, grid=(heads, seqs), in_specs=[part(0),...  24.3 us
  transfers between devices with their start and end apart: 35, of which 15 were waited for; matrix products, arithmetic and copies ran while one was open for 15% of the time, Pallas kernels for 8%

commit v1 on v0

v1 whole, which is shorter than its diff:
```python
import functools
import jax
import jax.numpy as jnp
from jax import lax
from jax.sharding import PartitionSpec as P
from jax.experimental import pallas as pl
from jax.experimental.pallas import tpu as pltpu

HEAD_DIM = 64
NUM_BUCKETS = 32
EPSILON = 1e-06
HIGHEST = lax.Precision.HIGHEST
CHUNK = 512


def cost(work):
    return pl.CostEstimate(flops=work, bytes_accessed=work // 1024, transcendentals=0)

BAND = 128


def dot_nt(a, b):
    return lax.dot_general(a, b, (((1,), (1,)), ((), ())), preferred_element_type=jnp.float32)


def dot_nn(a, b):
    return lax.dot_general(a, b, (((1,), (0,)), ((), ())), preferred_element_type=jnp.float32)


def dot_tn(a, b):
    return lax.dot_general(a, b, (((0,), (0,)), ((), ())), preferred_element_type=jnp.float32)


def fill_band(band, vector):
    span = vector.shape[1]
    rows = jnp.broadcast_to(vector, (8, span))
    rows = pltpu.roll(rows, span - (BAND - 1), 1)
    index = lax.broadcasted_iota(jnp.int32, (8, span), 0)
    for step in (1, 2, 4):
        rows = jnp.where((index & step) != 0, pltpu.roll(rows, step, 1), rows)
    band[0:8, :] = rows
    step = 8
    while step < BAND:
        band[step : 2 * step, :] = pltpu.roll(band[0:step, :], step, 1)
        step *= 2


def fold_band(band):
    span = band.shape[1]
    step = BAND // 2
    while step >= 8:
        band[0:step, :] += pltpu.roll(band[step : 2 * step, :], span - step, 1)
        step //= 2
    rows = band[0:8, :]
    index = lax.broadcasted_iota(jnp.int32, (8, span), 0)
    for step in (1, 2, 4):
        rows = jnp.where((index & step) != 0, pltpu.roll(rows, span - step, 1), rows)
    total = jnp.sum(rows, axis=0, keepdims=True)
    return pltpu.roll(total, BAND - 1, 1)


def attend_kernel(q_ref, k_ref, v_ref, vec_ref, out_ref, log_ref, band):
    seq = k_ref.shape[3]
    own = out_ref.shape[3]

    @pl.when(pl.program_id(1) == 0)
    def _():
        fill_band(band, vec_ref[0])

    keys = k_ref[0, 0].T
    values = v_ref[0, 0]
    for start in range(0, seq, CHUNK):
        queries = q_ref[0, 0, :, start : start + CHUNK] * jnp.bfloat16(HEAD_DIM ** -0.5)
        raw = dot_nn(keys, queries)
        parts = []
        for low in range(0, seq, BAND):
            at = start - low + seq - BAND
            parts.append(raw[low : low + BAND] + band[:, at : at + CHUNK])
        peak = functools.reduce(jnp.maximum, parts)
        peak = jnp.max(peak, axis=0, keepdims=True)
        parts = [jnp.exp(part - peak) for part in parts]
        total = jnp.sum(functools.reduce(jnp.add, parts), axis=0, keepdims=True)
        weights = jnp.concatenate([part.astype(jnp.bfloat16) for part in parts], axis=0)
        mixed = dot_nn(values, weights) / total
        out_ref[start // own, 0, :, start % own : start % own + CHUNK] = mixed.astype(jnp.bfloat16)
        log_ref[0, 0, :, start : start + CHUNK] = peak + jnp.log(total)


def attend(projected, vectors, own):
    heads, seq = vectors.shape[0], vectors.shape[2] // 2
    seqs = projected.shape[1] // seq
    blocks = seq // own
    part = lambda p: pl.BlockSpec((1, 1, HEAD_DIM, seq), lambda h, s, p=p: (p, h, 0, s))
    proj = projected.reshape(3, heads, HEAD_DIM, seqs * seq)
    return pl.pallas_call(
        attend_kernel,
        grid=(heads, seqs),
        in_specs=[part(0), part(1), part(2), pl.BlockSpec((1, 1, 2 * seq), lambda h, s: (h, 0, 0))],
        out_specs=[
            pl.BlockSpec((blocks, 1, HEAD_DIM, own), lambda h, s: (s, h, 0, 0)),
            pl.BlockSpec((1, 1, 1, seq), lambda h, s: (h, s, 0, 0)),
        ],
        out_shape=[
            jax.ShapeDtypeStruct((seqs * blocks, heads, HEAD_DIM, own), jnp.bfloat16),
            jax.ShapeDtypeStruct((heads, seqs, 1, seq), jnp.float32),
        ],
        scratch_shapes=[pltpu.VMEM((BAND, 2 * seq), jnp.float32)],
        compiler_params=pltpu.CompilerParams(vmem_limit_bytes=48 * 2**20),
        cost_estimate=cost(16 * heads * seqs * seq * seq * HEAD_DIM),
    )(proj, proj, proj, vectors)


def attend_back_kernel(q_ref, k_ref, v_ref, o_ref, g_ref, log_ref, vec_ref, out_ref, diag_ref, band, fold, dk, dv):
    seq = k_ref.shape[3]
    own = out_ref.shape[4]
    scale = HEAD_DIM ** -0.5

    @pl.when(pl.program_id(1) == 0)
    def _():
        fill_band(band, vec_ref[0])
        fold[...] = jnp.zeros_like(fold)

    keys_t = k_ref[0, 0]
    keys = keys_t.T
    values = v_ref[0, 0].T
    for start in range(0, seq, CHUNK):
        block, inner = start // own, start % own
        queries = q_ref[0, 0, :, start : start + CHUNK] * jnp.bfloat16(scale)
        grads = g_ref[block, 0, :, inner : inner + CHUNK]
        mixed = o_ref[block, 0, :, inner : inner + CHUNK]
        delta = jnp.sum(grads.astype(jnp.float32) * mixed.astype(jnp.float32), axis=0, keepdims=True)
        logs = log_ref[0, 0, :, start : start + CHUNK]
        raw = dot_nn(keys, queries)
        grad_weights = dot_nn(values, grads)
        low_weights, low_scores = [], []
        for low in range(0, seq, BAND):
            at = start - low + seq - BAND
            weights = jnp.exp(raw[low : low + BAND] + band[:, at : at + CHUNK] - logs)
            scores = weights * (grad_weights[low : low + BAND] - delta)
            fold[:, at : at + CHUNK] += scores
            low_weights.append(weights.astype(jnp.bfloat16))
            low_scores.append(scores.astype(jnp.bfloat16))
        weights = jnp.concatenate(low_weights, axis=0)
        scores = jnp.concatenate(low_scores, axis=0)
        grad_q = dot_nn(keys_t, scores) * scale
        out_ref[block, 0, 0, :, inner : inner + CHUNK] = grad_q.astype(jnp.bfloat16)
        if start == 0:
            dk[...] = dot_nt(queries, scores)
            dv[...] = dot_nt(grads, weights)
        else:
            dk[...] += dot_nt(queries, scores)
            dv[...] += dot_nt(grads, weights)
    for block in range(seq // own):
        out_ref[block, 1, 0] = dk[:, block * own : (block + 1) * own].astype(jnp.bfloat16)
        out_ref[block, 2, 0] = dv[:, block * own : (block + 1) * own].astype(jnp.bfloat16)

    @pl.when(pl.program_id(1) == pl.num_programs(1) - 1)
    def _():
        diag_ref[0] = fold_band(fold)


def attend_back(projected, vectors, mixed, grads, logs):
    heads, seq = vectors.shape[0], vectors.shape[2] // 2
    seqs = projected.shape[1] // seq
    own = mixed.shape[3]
    blocks = seq // own
    part = lambda p: pl.BlockSpec((1, 1, HEAD_DIM, seq), lambda h, s, p=p: (p, h, 0, s))
    side = pl.BlockSpec((blocks, 1, HEAD_DIM, own), lambda h, s: (s, h, 0, 0))
    vec = pl.BlockSpec((1, 1, 2 * seq), lambda h, s: (h, 0, 0))
    proj = projected.reshape(3, heads, HEAD_DIM, seqs * seq)
    return pl.pallas_call(
        attend_back_kernel,
        grid=(heads, seqs),
        in_specs=[part(0), part(1), part(2), side, side,
                  pl.BlockSpec((1, 1, 1, seq), lambda h, s: (h, s, 0, 0)), vec],
        out_specs=[
            pl.BlockSpec((blocks, 3, 1, HEAD_DIM, own), lambda h, s: (s, 0, h, 0, 0)),
            vec,
        ],
        out_shape=[
            jax.ShapeDtypeStruct((seqs * blocks, 3, heads, HEAD_DIM, own), jnp.bfloat16),
            jax.ShapeDtypeStruct((heads, 1, 2 * seq), jnp.float32),
        ],
        scratch_shapes=[
            pltpu.VMEM((BAND, 2 * seq), jnp.float32),
            pltpu.VMEM((BAND, 2 * seq), jnp.float32),
            pltpu.VMEM((HEAD_DIM, seq), jnp.float32),
            pltpu.VMEM((HEAD_DIM, seq), jnp.float32),
        ],
        compiler_params=pltpu.CompilerParams(vmem_limit_bytes=48 * 2**20),
        cost_estimate=cost(32 * heads * seqs * seq * seq * HEAD_DIM),
    )(proj, proj, proj, mixed, grads, logs, vectors)


def place_kernel(capacity, flat_ref, rows_ref, place_ref, *piece_refs):
    flat = flat_ref[...]
    for k, ref in enumerate(piece_refs):
        index = lax.broadcasted_iota(jnp.int32, (capacity, flat.shape[1]), 0) + k * capacity
        hot = (index == flat).astype(jnp.bfloat16)
        place_ref[k * capacity : (k + 1) * capacity, :] = hot
        ref[...] = dot_nn(hot, rows_ref[...]).astype(jnp.bfloat16)


def place_rows(flat, rows, pieces, capacity):
    count, width = rows.shape
    outs = pl.pallas_call(
        functools.partial(place_kernel, capacity),
        out_shape=[jax.ShapeDtypeStruct((pieces * capacity, count), jnp.bfloat16)]
        + [jax.ShapeDtypeStruct((capacity, width), jnp.bfloat16)] * pieces,
        compiler_params=pltpu.CompilerParams(vmem_limit_bytes=48 * 2**20),
        cost_estimate=cost(2 * pieces * capacity * count * width),
    )(flat[None, :], rows)
    return outs[0], list(outs[1:])


def project_kernel(x_ref, gain_ref, weight_ref, out_ref, normed_ref):
    rows = x_ref[...]
    scale = lax.rsqrt(jnp.mean(rows * rows, axis=-1, keepdims=True) + EPSILON)
    normed = (rows * scale * gain_ref[...]).astype(jnp.bfloat16)
    normed_ref[...] = normed
    out_ref[...] = dot_nt(weight_ref[...], normed).astype(jnp.bfloat16)


def project(rows, gain, weights, tile):
    count, width = rows.shape
    columns = weights.shape[0]
    return pl.pallas_call(
        project_kernel,
        grid=(count // tile,),
        in_specs=[
            pl.BlockSpec((tile, width), lambda i: (i, 0)),
            pl.BlockSpec((1, width), lambda i: (0, 0)),
            pl.BlockSpec((columns, width), lambda i: (0, 0)),
        ],
        out_specs=[
            pl.BlockSpec((columns, tile), lambda i: (0, i)),
            pl.BlockSpec((tile, width), lambda i: (i, 0)),
        ],
        out_shape=[
            jax.ShapeDtypeStruct((columns, count), jnp.bfloat16),
            jax.ShapeDtypeStruct((count, width), jnp.bfloat16),
        ],
        compiler_params=pltpu.CompilerParams(vmem_limit_bytes=48 * 2**20),
        cost_estimate=cost(4 * count * width * columns),
    )(rows, gain, weights)


def gelu_parts(values):
    root = 0.7978845608028654
    square = values * values
    bend = jnp.tanh(root * values * (1.0 + 0.044715 * square))
    half = 0.5 + 0.5 * bend
    slope = half + half * (1.0 - bend) * values * (root + (3.0 * 0.044715 * root) * square)
    return values * half, slope


def expert_kernel(places, arrays, pieces, *refs):
    row_refs, grad_refs, refs = refs[:pieces], refs[pieces : 2 * pieces], refs[2 * pieces :]
    first_refs, second_refs, refs = refs[:arrays], refs[arrays : 2 * arrays], refs[2 * arrays :]
    parts = len(places)
    act_ref, pre_ref, xt_ref, lt_ref = refs[:4]
    res_refs, back_refs = refs[4 : 4 + pieces], refs[4 + pieces : 4 + 2 * pieces]
    rows, low, res_sum, back_sum, firsts, seconds, sems = refs[4 + 2 * pieces :]
    step = pl.program_id(0)
    capacity = grad_refs[0].shape[0]
    width = grad_refs[0].shape[1]
    count = pieces * capacity
    tile = min(count, 256)

    def fetch(j):
        (one, at), (two, there) = places[j]
        return (
            pltpu.make_async_copy(first_refs[one].at[at], firsts.at[j % 2], sems.at[0, j % 2]),
            pltpu.make_async_copy(second_refs[two].at[there], seconds.at[j % 2], sems.at[1, j % 2]),
        )

    @pl.when(step == 0)
    def _():
        for copy in fetch(0):
            copy.start()
        for e in range(pieces):
            span = pl.ds(e * capacity, capacity)
            rows[span, :] = row_refs[e][:capacity, :]
            gates = row_refs[e][capacity : capacity + 8, :capacity].astype(jnp.float32).T[:, 0:1]
            low[span, :] = (gates * grad_refs[e][...].astype(jnp.float32)).astype(jnp.bfloat16)
        res_sum[...] = jnp.zeros_like(res_sum)
        back_sum[...] = jnp.zeros_like(back_sum)

    for j in range(parts):

        @pl.when(step == j)
        def _(j=j):
            if j + 1 < parts:
                for copy in fetch(j + 1):
                    copy.start()
            for copy in fetch(j):
                copy.wait()

    @pl.when(step == 0)
    def _():
        xt_ref[...] = rows[...].T
        lt_ref[...] = low[...].T

    first = firsts[step % 2]
    second = seconds[step % 2]
    for start in range(0, count, tile):
        span = pl.ds(start, tile)
        active, slope = gelu_parts(dot_nn(rows[span, :], first))
        active = active.astype(jnp.bfloat16)
        act_ref[0, span, :] = active
        res_sum[span, :] += dot_nn(active, second)
        pre = (dot_nt(low[span, :], second) * slope).astype(jnp.bfloat16)
        pre_ref[0, span, :] = pre
        back_sum[span, :] += dot_nt(pre, first)

    @pl.when(step == parts - 1)
    def _():
        for e in range(pieces):
            span = pl.ds(e * capacity, capacity)
            res_refs[e][...] = res_sum[span, :].astype(jnp.bfloat16)
            back_refs[e][:capacity, :] = back_sum[span, :].astype(jnp.bfloat16)
            sums = jnp.sum(
                res_sum[span, :] * grad_refs[e][...].astype(jnp.float32), axis=1, keepdims=True
            )
            sums = jnp.broadcast_to(sums, (capacity, 128)).T[0:8, :]
            high = sums.astype(jnp.bfloat16).astype(jnp.float32)
            index = lax.broadcasted_iota(jnp.int32, sums.shape, 0)
            pair = jnp.where(index == 0, high, jnp.where(index == 1, sums - high, 0.0))
            back_refs[e][capacity : capacity + 8, :] = jnp.zeros((8, width), jnp.bfloat16)
            back_refs[e][capacity : capacity + 8, :capacity] = pair.astype(jnp.bfloat16)


PLACES = (
    ((0, 0), (0, 0)),
    ((1, 0), (1, 0)),
    ((2, 0), (4, 0)),
    ((3, 0), (5, 0)),
    ((4, 0), (2, 0)),
    ((4, 1), (4, 1)),
    ((5, 0), (3, 0)),
    ((5, 1), (5, 1)),
)
MINE = ((0, 4, 2, 5), (0, 2, 4, 5))
OTHER = ((1, 6, 3, 7), (1, 3, 6, 7))


def expert_apply(arrived, grads, firsts, seconds):
    pieces = len(grads)
    capacity, width = grads[0].shape
    count = pieces * capacity
    hidden = firsts[0].shape[2]
    parts, arrays = len(PLACES), len(firsts)
    sent = pl.BlockSpec(arrived[0].shape, lambda i: (0, 0))
    whole = pl.BlockSpec((capacity, width), lambda i: (0, 0))
    kept = pl.BlockSpec((1, count, hidden), lambda i: (i, 0, 0))
    turned = pl.BlockSpec((width, count), lambda i: (0, 0))
    outs = pl.pallas_call(
        functools.partial(expert_kernel, PLACES, arrays, pieces),
        grid=(parts,),
        in_specs=[sent] * pieces + [whole] * pieces + [pl.BlockSpec(memory_space=pl.ANY)] * (2 * arrays),
        out_specs=[kept, kept, turned, turned] + [whole] * pieces + [sent] * pieces,
        out_shape=[
            jax.ShapeDtypeStruct((parts, count, hidden), jnp.bfloat16),
            jax.ShapeDtypeStruct((parts, count, hidden), jnp.bfloat16),
            jax.ShapeDtypeStruct((width, count), jnp.bfloat16),
            jax.ShapeDtypeStruct((width, count), jnp.bfloat16),
        ]
        + [jax.ShapeDtypeStruct((capacity, width), jnp.bfloat16)] * pieces
        + [jax.ShapeDtypeStruct(arrived[0].shape, jnp.bfloat16)] * pieces,
        scratch_shapes=[
            pltpu.VMEM((count, width), jnp.bfloat16),
            pltpu.VMEM((count, width), jnp.bfloat16),
            pltpu.VMEM((count, width), jnp.float32),
            pltpu.VMEM((count, width), jnp.float32),
            pltpu.VMEM((2, width, hidden), jnp.bfloat16),
            pltpu.VMEM((2, hidden, width), jnp.bfloat16),
            pltpu.SemaphoreType.DMA((2, 2)),
        ],
        compiler_params=pltpu.CompilerParams(vmem_limit_bytes=52 * 2**20),
        cost_estimate=cost(12 * count * width * hidden * parts),
    )(*arrived, *grads, *firsts, *seconds)
    return list(outs[:4]), list(outs[4 : 4 + pieces]), list(outs[4 + pieces :])


def weight_kernel(groups, added, *refs):
    for out, (left, right) in enumerate(((2, 1), (3, 0))):
        total = 0.0
        for g in range(groups):
            total = total + dot_nn(refs[4 * g + left][...], refs[4 * g + right][0])
        if added:
            total = total + refs[4 * groups + out][0].astype(jnp.float32)
        refs[4 * groups + 2 * added + out][0] = total.astype(jnp.bfloat16)


def expert_weights(groups, chosen, added=()):
    steps, hidden = len(chosen[0]), groups[0][0].shape[2]
    width = groups[0][2].shape[0]
    count = sum(group[2].shape[1] for group in groups)
    specs, arrays = [], []

    def pick(i, which):
        return sum(jnp.where(i == j, at, 0) for j, at in enumerate(chosen[which]))

    for act, pre, xt, lt in groups:
        block = (1,) + act.shape[1:]
        whole = pl.BlockSpec(xt.shape, lambda i: (0, 0))
        specs += [
            pl.BlockSpec(block, lambda i: (pick(i, 1), 0, 0)),
            pl.BlockSpec(block, lambda i: (pick(i, 0), 0, 0)),
            whole,
            whole,
        ]
        arrays += [act, pre, xt, lt]
    part = pl.BlockSpec((1, width, hidden), lambda i: (i, 0, 0))
    return pl.pallas_call(
        functools.partial(weight_kernel, len(groups), len(added) // 2),
        grid=(steps,),
        in_specs=specs + [part] * len(added),
        out_specs=[part, part],
        out_shape=[jax.ShapeDtypeStruct((steps, width, hidden), jnp.bfloat16)] * 2,
        compiler_params=pltpu.CompilerParams(vmem_limit_bytes=50 * 2**20),
        cost_estimate=cost(6 * count * width * hidden * steps),
    )(*arrays, *added)


def inverse_rms(rows):
    return lax.rsqrt(jnp.mean(rows * rows, axis=-1, keepdims=True) + EPSILON)


def norm_backward(grad_normed, gain, normed_hat, inv_scale):
    scaled = grad_normed * gain
    return inv_scale * (scaled - normed_hat * jnp.mean(scaled * normed_hat, axis=-1, keepdims=True))


def swap(array, axis, offset):
    count = lax.axis_size(axis)
    return lax.ppermute(array, axis, [(i, i ^ offset) for i in range(count)])


def trade(array, axis):
    return lax.all_to_all(array, axis, 0, 0, tiled=True)


def spread(array, axis):
    return trade(jnp.broadcast_to(array[None], (lax.axis_size(axis),) + array.shape), axis)


def sum_copies(partial):
    experts = lax.axis_size("expert")
    rank = lax.axis_index("dp")
    kept = partial.shape[0]
    partial = jnp.pad(partial, ((0, -kept % (2 * experts)), (0, 0)))
    rows, columns = partial.shape
    half = rows // 2
    mine = lax.dynamic_slice_in_dim(partial, rank * half, half, 0)
    other = lax.dynamic_slice_in_dim(partial, (1 - rank) * half, half, 0).astype(jnp.bfloat16)
    mine = (mine + swap(other, "dp", 1).astype(jnp.float32)).astype(jnp.bfloat16)
    shares = trade(mine.reshape(experts, half // experts, columns), "expert")
    share = jnp.sum(shares.astype(jnp.float32), axis=0).astype(jnp.bfloat16)
    mine = spread(share, "expert").reshape(half, columns)
    other = swap(mine, "dp", 1)
    first = rank == 0
    return jnp.concatenate(
        [jnp.where(first, mine, other), jnp.where(first, other, mine)], axis=0
    )[:kept].astype(jnp.float32)


def on_device(
    layer_input,
    cotangent,
    norm1_gain,
    w_query,
    w_key,
    w_value,
    w_output,
    bias_table,
    bucket,
    norm2_gain,
    router,
    expert_index,
    w_in,
    w_out,
):
    group_rows, width = layer_input.shape
    tensor_count = lax.axis_size("tensor")
    tensor_rank = lax.axis_index("tensor")
    dp_rank = lax.axis_index("dp")
    own_rows = group_rows // tensor_count
    own_start = tensor_rank * own_rows
    local_heads = bias_table.shape[1]
    inner = local_heads * HEAD_DIM
    experts = router.shape[1]
    capacity = 2 * own_rows // experts
    slots = experts * capacity

    half = w_in.shape[2] // 2
    first_mine = lax.dynamic_slice_in_dim(w_in[0], dp_rank * half, half, 1)
    first_other = lax.dynamic_slice_in_dim(w_in[0], (1 - dp_rank) * half, half, 1)
    second_mine = lax.dynamic_slice_in_dim(w_out[0], dp_rank * half, half, 0)
    second_other = lax.dynamic_slice_in_dim(w_out[0], (1 - dp_rank) * half, half, 0)
    w_joined = jnp.concatenate([w_query.T, w_key.T, w_value.T], axis=0)
    output_full = spread(w_output, "tensor")

    routes = lax.dynamic_slice_in_dim(expert_index[:, 0], own_start, own_rows, 0)
    own_hot = routes[:, None] == jnp.arange(experts, dtype=jnp.int32)[None, :]
    row_ids = jnp.arange(own_rows, dtype=jnp.int32)
    earlier = (row_ids[None, :] < row_ids[:, None]).astype(jnp.bfloat16)
    before = jnp.dot(earlier, own_hot.astype(jnp.bfloat16), preferred_element_type=jnp.float32)
    own_hot = own_hot.astype(jnp.float32)
    slot = jnp.sum(before * own_hot, axis=-1).astype(jnp.int32)
    flat = (routes ^ lax.axis_index("expert")) * capacity + slot
    cot_low = lax.dynamic_slice_in_dim(cotangent, own_start, own_rows, 0)
    cot_own = cot_low.astype(jnp.float32)
    place_hot, grad_in = place_rows(flat, cot_low, experts, capacity)
    near = experts // 2
    far = near + experts // 4
    grad_in = [grad_in[0]] + [swap(grad_in[k], "expert", k) for k in range(1, far)] + grad_in[far:]

    gain_one = norm1_gain.astype(jnp.float32)
    projected, normed_one = project(layer_input, gain_one[None, :], w_joined, own_rows)
    high_bit = tensor_count // 2
    first_near = swap(first_mine, "tensor", 1)
    second_near = swap(second_mine, "tensor", high_bit)
    turned = jnp.concatenate([bucket[::-1], jnp.full((1,), -1, jnp.int32)])
    bucket_hot = jnp.arange(NUM_BUCKETS, dtype=jnp.int32)[:, None] == turned[None, :]
    vectors = dot_tn(bias_table, bucket_hot.astype(jnp.bfloat16))[:, None, :]
    mixed, logs = attend(projected, vectors, own_rows)
    mixed, output_full, first_near, second_near, grad_in[1:far] = lax.optimization_barrier(
        (mixed, output_full, first_near, second_near, grad_in[1:far])
    )
    output_full = output_full.reshape(tensor_count * inner, width)
    first_far = swap(jnp.stack([first_mine, first_near]), "tensor", high_bit)
    second_far = swap(jnp.stack([second_mine, second_near]), "tensor", 1)
    grad_in[far:] = [swap(grad_in[k], "expert", k) for k in range(far, experts)]
    mixed_own = trade(mixed.reshape(tensor_count, inner, own_rows), "tensor").reshape(
        tensor_count * inner, own_rows
    )

    input_own = lax.dynamic_slice_in_dim(layer_input, own_start, own_rows, 0)
    residual = input_own + dot_tn(mixed_own, output_full)
    gain_two = norm2_gain.astype(jnp.float32)
    inv_two = inverse_rms(residual)
    hat_two = residual * inv_two
    normed_two = hat_two * gain_two
    router_wide = router.astype(jnp.float32)
    router_probs = jax.nn.softmax(jnp.dot(normed_two, router_wide, precision=HIGHEST), axis=-1)
    gate_full = jnp.sum(router_probs * own_hot, axis=-1)
    gate_low = gate_full.astype(jnp.bfloat16)
    send_rows = dot_nn(place_hot, normed_two.astype(jnp.bfloat16)).astype(jnp.bfloat16)
    send_gates = dot_nn(place_hot, gate_low[:, None]).astype(jnp.bfloat16)
    gate_rows = jnp.pad(send_gates.reshape(experts, 1, capacity), ((0, 0), (0, 7), (0, width - capacity)))
    sent = jnp.concatenate([send_rows.reshape(experts, capacity, width), gate_rows], axis=1)
    sent, grad_in[far:] = lax.optimization_barrier((sent, grad_in[far:]))
    arrived = [sent[0]] + [swap(sent[k], "expert", k) for k in range(1, experts)]

    arrived[1:near], first_far, second_far = lax.optimization_barrier(
        (arrived[1:near], first_far, second_far)
    )
    first_parts = [first_mine[None], first_other[None]]
    second_parts = [second_mine[None], second_other[None]]
    for first, second in ((first_near[None], second_near[None]), (first_far, second_far)):
        first_parts += [first, swap(first, "dp", 1)]
        second_parts += [second, swap(second, "dp", 1)]
    arrived[:near], first_parts, second_parts, joined = lax.optimization_barrier(
        (arrived[:near], first_parts, second_parts, w_joined)
    )
    joined_parts = [w_joined] + [swap(joined, "tensor", k) for k in range(1, tensor_count - 1)]
    groups, results, back_got = [], [], []
    for low, high in ((0, near), (near, far), (far, experts)):
        pieces = arrived[low:high]
        if low == near:
            results, pieces, joined, joined_parts = lax.optimization_barrier(
                (results, pieces, joined, joined_parts)
            )
            joined_parts.append(swap(joined, "tensor", tensor_count - 1))
        if low == far:
            results, pieces, joined_parts = lax.optimization_barrier((results, pieces, joined_parts))
        kept, res, back = expert_apply(pieces, grad_in[low:high], first_parts, second_parts)
        groups.append(kept)
        results += res
        back_got += [
            back[k - low] if k == 0 else swap(back[k - low], "expert", k) for k in range(low, high)
        ]
    others = expert_weights(groups, OTHER)
    first_sum, second_sum = expert_weights(groups, MINE, [swap(part, "dp", 1) for part in others])
    first_sum, second_sum, back_got = lax.optimization_barrier((first_sum, second_sum, back_got))
    first_got = swap(first_sum[2:], "tensor", 1)
    second_got = swap(second_sum[2:], "tensor", high_bit)

    grad_normed_two = dot_tn(place_hot, jnp.concatenate([back[:capacity] for back in back_got]))
    pair_got = jnp.concatenate([back[capacity : capacity + 2, :capacity].T for back in back_got])
    grad_gate = jnp.sum(dot_tn(place_hot, pair_got), axis=-1)
    grad_logits = router_probs * (own_hot - gate_full[:, None]) * grad_gate[:, None]
    grad_router = jnp.einsum("td,te->ed", normed_two, grad_logits, precision=HIGHEST)
    grad_normed_two = grad_normed_two + jnp.einsum(
        "te,de->td", grad_logits, router_wide, precision=HIGHEST
    )
    grad_norm_two = jnp.sum(grad_normed_two * hat_two, axis=0)
    grad_residual = cot_own + norm_backward(grad_normed_two, gain_two, hat_two, inv_two)
    grad_low = grad_residual.astype(jnp.bfloat16)
    grad_heads = dot_nt(output_full, grad_low).astype(jnp.bfloat16)
    heads_got = trade(grad_heads.reshape(tensor_count, inner, own_rows), "tensor")
    grad_wo = dot_nn(mixed_own, grad_low).astype(jnp.bfloat16).reshape(tensor_count, inner, width)
    shared = jnp.concatenate([grad_router, grad_norm_two[None]], axis=0).astype(jnp.bfloat16)
    shared = jnp.pad(shared, ((0, -shared.shape[0] % 8), (0, 0)))
    shared = jnp.broadcast_to(shared[None], (tensor_count,) + shared.shape)
    grad_wo = trade(jnp.concatenate([grad_wo, shared], axis=1), "tensor")
    _, *results = lax.optimization_barrier((grad_low, *results))
    returned = [results[0]] + [swap(results[k], "expert", k) for k in range(1, experts)]

    heads_got, first_got, second_got = lax.optimization_barrier((heads_got, first_got, second_got))
    first_pair = (first_sum[:2].astype(jnp.float32) + first_got.astype(jnp.float32)).astype(jnp.bfloat16)
    second_pair = (second_sum[:2].astype(jnp.float32) + second_got.astype(jnp.float32)).astype(
        jnp.bfloat16
    )
    first_got = swap(first_pair[1], "tensor", high_bit)
    second_got = swap(second_pair[1], "tensor", 1)

    head_shape = (tensor_count, local_heads, HEAD_DIM, own_rows)
    grad_projected, diagonals = attend_back(
        projected, vectors, mixed, heads_got.reshape(head_shape), logs
    )
    grad_projected = grad_projected.reshape(tensor_count, 3 * inner, own_rows)
    grad_projected, first_got, second_got, returned, grad_wo = lax.optimization_barrier(
        (grad_projected, first_got, second_got, returned, grad_wo)
    )

    pairs = ((first_pair, first_got), (second_pair, second_got))
    total = jnp.stack([pair[0].astype(jnp.float32) + got.astype(jnp.float32) for pair, got in pairs])
    total = total.astype(jnp.bfloat16)
    rest = swap(total, "dp", 1)
    first = dp_rank == 0
    both = jnp.concatenate(
        [jnp.where(first, total, rest), jnp.where(first, rest, total)], axis=2
    ).astype(jnp.float32)
    output = residual + gate_low.astype(jnp.float32)[:, None] * dot_tn(
        place_hot, jnp.concatenate(returned)
    )

    grad_normed_one = dot_tn(
        lax.dynamic_index_in_dim(grad_projected, tensor_rank, 0, keepdims=False), w_joined
    )
    for k in range(1, tensor_count):
        sent = lax.dynamic_index_in_dim(grad_projected, tensor_rank ^ k, 0, keepdims=False)
        grad_normed_one = grad_normed_one + dot_tn(swap(sent, "tensor", k), joined_parts[k])
    inv_own = inverse_rms(input_own)
    input_grad = grad_residual + norm_backward(grad_normed_one, gain_one, input_own * inv_own, inv_own)

    grad_joined = jnp.einsum(
        "bcn,bnd->cd",
        grad_projected,
        normed_one.reshape(tensor_count, own_rows, width),
        preferred_element_type=jnp.float32,
    )
    norm_one = jnp.sum(grad_joined * w_joined.astype(jnp.float32), axis=0) / gain_one
    grad_table = jnp.einsum(
        "br,hr->hb", bucket_hot.astype(jnp.float32), diagonals[:, 0], precision=HIGHEST
    ).reshape(-1)
    table_size = grad_table.shape[0]
    used = 3 * inner
    joined = sum_copies(
        jnp.concatenate(
            [
                grad_joined,
                jnp.sum(grad_wo.astype(jnp.float32), axis=0),
                norm_one[None],
                jnp.pad(grad_table, (0, width - table_size))[None],
            ],
            axis=0,
        )
    )
    shared = joined[used + inner :]
    norm_one = shared[-2]
    norm_one = norm_one + sum(swap(norm_one, "tensor", k) for k in range(1, tensor_count))
    return (
        output,
        input_grad,
        joined[:inner].T,
        joined[inner : 2 * inner].T,
        joined[2 * inner : used].T,
        joined[used : used + inner],
        shared[-1, :table_size].reshape(local_heads, NUM_BUCKETS).T,
        norm_one,
        shared[experts],
        shared[:experts].T,
        both[0][None],
        both[1].T[None],
    )


def solution(mesh):
    return jax.shard_map(
        on_device,
        mesh=mesh,
        in_specs=(
            P(("dp", "expert"), None),
            P(("dp", "expert"), None),
            P(),
            P(None, "tensor"),
            P(None, "tensor"),
            P(None, "tensor"),
            P("tensor", None),
            P(None, "tensor"),
            P(),
            P(),
            P(),
            P(("dp", "expert"), None),
            P("expert", None, "tensor"),
            P("expert", "tensor", None),
        ),
        out_specs=(
            P(("dp", "expert", "tensor"), None),
            P(("dp", "expert", "tensor"), None),
            P(None, "tensor"),
            P(None, "tensor"),
            P(None, "tensor"),
            P("tensor", None),
            P(None, "tensor"),
            P(),
            P(),
            P(),
            P("expert", None, "tensor"),
            P("expert", "tensor", None),
        ),
        check_vma=False,
    )
```

time: 564 us -> 374 us (0.66)
  blocking collectives: 113 us -> 0 us
  waiting for transfers between devices: 151 us -> 69 us
  local copies, waits for them, and re-layouts: 55 us -> 27.7 us
  Pallas kernels: 96.1 us -> 118 us
  starting transfers between devices: 64.3 us -> 81.5 us
  other arithmetic: 37.4 us -> 30.7 us
    all_to_all x3 -> x0, blocking collectives: 72.6 us -> none  [trade(): return lax.all_to_all(array, axis, 0, 0, tiled=True)]
    ppermute x24 -> x38, waiting for transfers between devices: 79 us -> 37.1 us  [swap(): return lax.ppermute(array, axis, [(i, i ^ offset) for i in range(count)])]
    all_to_all x11 -> x6, waiting for transfers between devices: 72.3 us -> 31.9 us  [trade(): return lax.all_to_all(array, axis, 0, 0, tiled=True)]
    psum x1 -> x0, blocking collectives: 40 us -> none  [on_device(): lax.psum((grad_norm_two, grad_router), ('dp', 'expert', 'tensor'))]
    ppermute x24 -> x38, starting transfers between devices: 16 us -> 49 us  [swap(): return lax.ppermute(array, axis, [(i, i ^ offset) for i in range(count)])]
    unnamed x92 -> x133, local copies, waits for them, and re-layouts: 31 us -> 8.46 us
    pallas_call x2 -> x7, Pallas kernels: 57.3 us -> 79.6 us  [the longest x3 51.4 us: expert_apply(): pl.pallas_call(functools.partial(expert_kernel, PLACES, arrays, pieces),...]
    all_to_all x11 -> x6, starting transfers between devices: 48.4 us -> 32.4 us  [trade(): return lax.all_to_all(array, axis, 0, 0, tiled=True)]
  transfers between devices with their start and end apart: 35 -> 44, of which waited for: 15 -> 12; matrix products, arithmetic and copies ran while one was open for 15% -> 21% of each run, Pallas kernels for 8% -> 26%
where the time goes in v1:
time: 374 us; the launch traced here: 368 us
  Pallas kernels  118 us (32%)
  starting transfers between devices  81.5 us (22%)
  waiting for transfers between devices  69 us (18%)
  matrix products  38.2 us (10%)
  other arithmetic  30.7 us (8%)
  local copies, waits for them, and re-layouts  27.7 us (7%)
    pallas_call x3, Pallas kernels, expert_apply(): pl.pallas_call(functools.partial(expert_kernel, PLACES, arrays, pieces),...  51.4 us
    ppermute x38, starting transfers between devices, swap(): return lax.ppermute(array, axis, [(i, i ^ offset) for i in range(count)])  49 us
    ppermute x38, waiting for transfers between devices, swap(): return lax.ppermute(array, axis, [(i, i ^ offset) for i in range(count)])  37.1 us
    all_to_all x6, starting transfers between devices, trade(): return lax.all_to_all(array, axis, 0, 0, tiled=True)  32.4 us
    all_to_all x6, waiting for transfers between devices, trade(): return lax.all_to_all(array, axis, 0, 0, tiled=True)  31.9 us
    pallas_call x1, Pallas kernels, attend_back(): pl.pallas_call(attend_back_kernel, grid=(heads, seqs), in_specs=[part(0),...  23.6 us
    dot_general x9, matrix products, dot_tn(): lax.dot_general(a, b, (((0,), (0,)), ((), ())), preferred_element_type=jn...  20.1 us
    pallas_call x2, Pallas kernels, expert_weights(): pl.pallas_call(functools.partial(weight_kernel, len(groups), len(added) /...  19.9 us
  transfers between devices with their start and end apart: 44, of which 12 were waited for; matrix products, arithmetic and copies ran while one was open for 21% of the time, Pallas kernels for 26%

profile of v1, /device:TPU:0, one launch (start us, length us, event | category | flops | bytes accessed | tf_op | source)
XLA Modules:
  0.0 367.7 jit_solution(5051387210300055066)
XLA Ops:
  2.8 5.2 %all-to-all-start = ((bf16[4,192,768]{2,1,0:T(8,128)(2,1)}), bf16[4,192,768]{2,1,0:T(8,128)(2,1)}, u32[]{:S(2)}, u32[]{:S(2)}) async-start(bf16[4,192,768]{2,1,0:T(8,128)(2,1)} %broadcast_in_dim.21), calls=%async_computation | async-start | bytes 2359296 | tf_op jit(solution)/shard_map/all_to_all | solution.py:441
  19.8 2.6 collective-permute-start.3
  24.0 6.6 %shard_map.229 = (bf16[576,2048]{1,0:T(8,128)(2,1)S(1)}, bf16[2048,768]{1,0:T(8,128)(2,1)}) custom-call(f32[2048,768]{1,0:T(8,128)} %x_ref.1, f32[1,768]{1,0:T(1,128)S(1)} %broadcast_in_dim.19.gain_ref, bf16[576,768]{1,0:T(8,128)(2,1)S(1)} %pad_maximum_fusion.5.weight_ref), custom_call_target="tpu_custom_call" | custom-call | flops 3623878656 | bytes 3538944 | tf_op jit(solution)/shard_map/pallas_call | solution.py:227
  30.7 15.1 %shard_map.230 = (bf16[4,3,64,512]{3,2,1,0:T(8,128)(2,1)}, f32[3,2,1,1024]{3,2,1,0:T(1,128)S(1)}) custom-call(bf16[3,3,64,2048]{3,2,1,0:T(8,128)(2,1)S(1)} %bitcast.117, bf16[3,3,64,2048]{3,2,1,0:T(8,128)(2,1)S(1)} %bitcast.118, bf16[3,3,64,2048]{3,2,1,0:T(8,128)(2,1)S(1)} %bitcast.119, f32[3,1,2048]{2,1,0:T(1,128)S(1)} %broadcast_in_dim.20.vec_ref), custom_call_target="tpu_custom_call" | custom-call | flops 6442450944 | bytes 6291456 | tf_op jit(solution)/shard_map/pallas_call | solution.py:95
  45.8 4.4 %all-to-all-start.1 = ((bf16[4,192,512]{2,1,0:T(8,128)(2,1)}), bf16[4,192,512]{2,1,0:T(8,128)(2,1)}, u32[]{:S(2)}, u32[]{:S(2)}) async-start(bf16[4,192,512]{2,1,0:T(8,128)(2,1)} %bitcast.10), calls=%async_computation.1 | async-start | bytes 1572864 | tf_op jit(solution)/shard_map/all_to_all | solution.py:441
  61.5 4.0 %multiply_reduce_fusion.5 = (f32[512]{0:T(512)S(1)}, f32[512,768]{1,0:T(8,128)}) fusion(bf16[4,192,512]{2,1,0:T(8,128)(2,1)} %all-to-all-done.1, bf16[4,192,768]{2,1,0:T(8,128)(2,1)} %all-to-all-done, f32[2048,768]{1,0:T(8,128)} %x_ref.1, s32[]{:T(128)S(6)} %select_n.56), kind=kOutput, calls=%fused_computation.40 | convolution fusion | flops 605158912 | bytes 5113860 | tf_op jit(solution)/shard_map/dot_general | solution.py:31
  73.4 6.9 %collective-permute-done.5.refs_1_ = bf16[264,768]{1,0:T(8,128)(2,1)S(1)} collective-permute-done((bf16[264,768]{1,0:T(8,128)(2,1)S(1)}, bf16[264,768]{1,0:T(8,128)(2,1)S(1)}, u32[]{:S(2)}, u32[]{:S(2)}) %collective-permute-start.5) | collective-permute-done | bytes 405536 | tf_op jit(solution)/shard_map/ppermute | solution.py:437
  80.3 4.9 %collective-permute-done.6.refs_8_.refs_6_ = bf16[2,768,384]{2,1,0:T(8,128)(2,1)} collective-permute-done((bf16[2,768,384]{2,1,0:T(8,128)(2,1)}, bf16[2,768,384]{2,1,0:T(8,128)(2,1)}, u32[]{:S(2)}, u32[]{:S(2)}) %collective-permute-start.6) | collective-permute-done | bytes 1179680 | tf_op jit(solution)/shard_map/ppermute | solution.py:437
  86.6 4.2 %collective-permute-done.8.refs_7_.refs_5_ = bf16[1,768,384]{2,1,0:T(8,128)(2,1)S(1)} collective-permute-done((bf16[1,768,384]{2,1,0:T(8,128)(2,1)}, bf16[1,768,384]{2,1,0:T(8,128)(2,1)S(1)}, u32[]{:S(2)}, u32[]{:S(2)}) %collective-permute-start.8) | collective-permute-done | bytes 589856 | tf_op jit(solution)/shard_map/ppermute | solution.py:437
  93.8 23.0 %shard_map.232 = (bf16[8,512,384]{2,1,0:T(8,128)(2,1)}, bf16[8,512,384]{2,1,0:T(8,128)(2,1)}, bf16[768,512]{1,0:T(8,128)(2,1)}, bf16[768,512]{1,0:T(8,128)(2,1)}...) custom-call(bf16[264,768]{1,0:T(8,128)(2,1)} %get-tuple-element.121., ...), custom_call_target="tpu_custom_call" | custom-call | flops 14495514624 | bytes 14155776 | tf_op jit(solution)/shard_map/pallas_call | solution.py:357
  121.2 14.0 %shard_map.233 = (bf16[8,256,384]{2,1,0:T(8,128)(2,1)}, bf16[8,256,384]{2,1,0:T(8,128)(2,1)}, bf16[768,256]{1,0:T(8,128)(2,1)S(1)}, bf16[768,256]{1,0:T(8,128)(2...) custom-call(bf16[264,768]{1,0:T(8,128)(2,1)} %copy-done.62, ...), custom_call_target="tpu_custom_call" | custom-call | flops 7247757312 | bytes 7077888 | tf_op jit(solution)/shard_map/pallas_call | solution.py:357
  135.3 5.1 %collective-permute-done.16 = bf16[576,768]{1,0:T(8,128)(2,1)S(1)} collective-permute-done((bf16[576,768]{1,0:T(8,128)(2,1)S(1)}, bf16[576,768]{1,0:T(8,128)(2,1)S(1)}, u32[]{:S(2)}, u32[]{:S(2)}) %collective-permute-start.16) | collective-permute-done | bytes 884768 | tf_op jit(solution)/shard_map/ppermute | solution.py:437
  140.4 14.4 %shard_map.234 = (bf16[8,256,384]{2,1,0:T(8,128)(2,1)}, bf16[8,256,384]{2,1,0:T(8,128)(2,1)}, bf16[768,256]{1,0:T(8,128)(2,1)S(1)}, bf16[768,256]{1,0:T(8,128)(2...) custom-call(bf16[264,768]{1,0:T(8,128)(2,1)} %copy-done.63, bf16[256,768]{1,0:T(8,128)(2,1)S(1)} %copy-done.5, ...), custom_call_target="tpu_custom_call" | custom-call | flops 7247757312 | bytes 7077888 | tf_op jit(solution)/shard_map/pallas_call | solution.py:357
  154.9 9.8 %shard_map.235 = (bf16[4,768,384]{2,1,0:T(8,128)(2,1)}, bf16[4,768,384]{2,1,0:T(8,128)(2,1)}) custom-call(bf16[8,512,384]{2,1,0:T(8,128)(2,1)} %get-tuple-element.137.refs_0_, bf16[8,512,384]{2,1,0:T(8,128)(2,1)} %get-tuple-element.138.refs_1_, bf16[768,512]{1,0:T(8,128)(2,1)S(1)} %copy-done.12, bf16[768,512]{1,0:T(8,128)(2,1)S(1)} %copy-done.13, ...), custom_call_target="tpu_custom_call" | custom-call | flops 7247757312 | bytes 7077888 | tf_op jit(solution)/shard_map/pallas_call | solution.py:415
  175.1 10.1 %shard_map.236 = (bf16[4,768,384]{2,1,0:T(8,128)(2,1)}, bf16[4,768,384]{2,1,0:T(8,128)(2,1)}) custom-call(bf16[8,512,384]{2,1,0:T(8,128)(2,1)} %get-tuple-element.137.refs_0_, bf16[8,512,384]{2,1,0:T(8,128)(2,1)} %get-tuple-element.138.refs_1_, bf16[768,512]{1,0:T(8,128)(2,1)S(1)} %copy-done.12, bf16[768,512]{1,0:T(8,128)(2,1)S(1)} %copy-done.14, ...), custom_call_target="tpu_custom_call" | custom-call | flops 7247757312 | bytes 7077888 | tf_op jit(solution)/shard_map/pallas_call | solution.py:415
  185.8 12.9 %collective-permute-done.20 = bf16[264,768]{1,0:T(8,128)(2,1)S(1)} collective-permute-done((bf16[264,768]{1,0:T(8,128)(2,1)S(1)}, bf16[264,768]{1,0:T(8,128)(2,1)S(1)}, u32[]{:S(2)}, u32[]{:S(2)}) %collective-permute-start.20) | collective-permute-done | bytes 405536 | tf_op jit(solution)/shard_map/ppermute | solution.py:437
  200.8 2.9 multiply_reduce_fusion.3
  211.1 3.3 convolution_convert_fusion.2
  214.4 3.5 all-to-all-start.2
  220.4 8.0 %collective-permute-start.26 = (bf16[256,768]{1,0:T(8,128)(2,1)}, bf16[256,768]{1,0:T(8,128)(2,1)}, u32[]{:S(2)}, u32[]{:S(2)}) collective-permute-start(bf16[256,768]{1,0:T(8,128)(2,1)} %get-tuple-element.186), channel_id=1, source_target_pairs={{0,4},{4,0},{8,12},{12,8},{1,5},{5,1},{9,13},{13,9},{2,6},{6,2},{1... | collective-permute-start | bytes 1179656 | tf_op jit(solution)/shard_map/ppermute | solution.py:437
  233.9 8.0 %all-to-all-done.2 = bf16[4,192,512]{2,1,0:T(8,128)(2,1)S(1)} async-done(((bf16[4,192,512]{2,1,0:T(8,128)(2,1)}), bf16[4,192,512]{2,1,0:T(8,128)(2,1)S(1)}, u32[]{:S(2)}, u32[]{:S(2)}) %all-to-all-start.2) | async-done | bytes 786464 | tf_op jit(solution)/shard_map/all_to_all | solution.py:441
  241.9 4.5 %all-to-all-start.3 = ((bf16[4,200,768]{2,1,0:T(8,128)(2,1)}), bf16[4,200,768]{2,1,0:T(8,128)(2,1)}, u32[]{:S(2)}, u32[]{:S(2)}) async-start(bf16[4,200,768]{2,1,0:T(8,128)(2,1)} %pad_maximum_fusion), calls=%async_computation.3 | async-start | bytes 2457600 | tf_op jit(solution)/shard_map/all_to_all | solution.py:441
  255.5 23.6 %shard_map.237 = (bf16[4,3,3,64,512]{4,3,2,1,0:T(8,128)(2,1)S(1)}, f32[3,1,2048]{2,1,0:T(1,128)S(1)}) custom-call(bf16[3,3,64,2048]{3,2,1,0:T(8,128)(2,1)} %bitcast.120, bf16[3,3,64,2048]{3,2,1,0:T(8,128)(2,1)} %bitcast.121, bf16[3,3,64,2048]{3,2,1,0:T(8,128)(2,1)} %bitcast.122, bf16[4,3,64,512]{3,2,1,0:T(8,128)(2,1)} %get-tuple-element.111.o_ref, ...), custom_call_target="tpu_custom_call" | custom-call | flops 12884901888 | bytes 12582912 | tf_op jit(solution)/shard_map/pallas_call | solution.py:171
  281.5 3.9 %multiply_reduce_fusion = (f32[768]{0:T(1024)S(1)}, f32[576,768]{1,0:T(8,128)S(1)}) fusion(bf16[192,768]{1,0:T(8,128)(2,1)S(1)} %bitcast.126, bf16[192,768]{1,0:T(8,128)(2,1)S(1)} %bitcast.129, bf16[192,768]{1,0:T(8,128)(2,1)S(1)} %bitcast.132, bf16[4,576,512]{2,1,0:T(8,128)(2,1)S(1)} %bitcast.114, bf16[4,512,768]{2,1,0:T(8,128)(2,1)} %bitcast.142), kind=kOutput, calls=%fused_computation.12 | convolution fusion | flops 1815477504 | bytes 8162304 | tf_op jit(solution)/shard_map/bcn,bnd->cd/dot_general | solution.py:649
  292.2 4.0 %multiply_add_fusion.1 = f32[512,768]{1,0:T(8,128)} fusion(f32[512,768]{1,0:T(8,128)} %get-tuple-element.258, bf16[1024,512]{1,0:T(8,128)(2,1)S(1)} %get-tuple-element.113, bf16[256,768]{1,0:T(8,128)(2,1)} %collective-permute-done.28, bf16[256,768]{1,0:T(8,128)(2,1)} %collective-permute-done.27, bf16[256,768]{1,0:T(8,128)(2,1)} %collective-permute-done.26, ...), kind=kOutput, calls=%fused_computation.36 | convolution fusion | flops 812384256 | bytes 5769216 | tf_op jit(solution)/shard_map/dot_general | solution.py:31
  298.1 2.9 collective-permute-start.31
  302.1 10.4 %all-to-all-start.4 = ((bf16[4,98,768]{2,1,0:T(8,128)(2,1)}), bf16[4,98,768]{2,1,0:T(8,128)(2,1)}, u32[]{:S(2)}, u32[]{:S(2)}) async-start(bf16[4,98,768]{2,1,0:T(8,128)(2,1)} %reshape.164), calls=%async_computation.4 | async-start | bytes 1277952 | tf_op jit(solution)/shard_map/all_to_all | solution.py:441
  316.6 2.9 multiply_reduce_fusion.1
  319.5 10.4 %all-to-all-done.4 = bf16[4,98,768]{2,1,0:T(8,128)(2,1)} async-done(((bf16[4,98,768]{2,1,0:T(8,128)(2,1)}), bf16[4,98,768]{2,1,0:T(8,128)(2,1)}, u32[]{:S(2)}, u32[]{:S(2)}) %all-to-all-start.4) | async-done | bytes 602144 | tf_op jit(solution)/shard_map/all_to_all | solution.py:441
  331.9 4.5 %all-to-all-start.5 = ((bf16[4,98,768]{2,1,0:T(8,128)(2,1)}), bf16[4,98,768]{2,1,0:T(8,128)(2,1)}, u32[]{:S(2)}, u32[]{:S(2)}) async-start(bf16[4,98,768]{2,1,0:T(8,128)(2,1)} %broadcast_in_dim.26), calls=%async_computation.5 | async-start | bytes 1277952 | tf_op jit(solution)/shard_map/all_to_all | solution.py:441
  336.4 4.0 %multiply_add_fusion = f32[512,768]{1,0:T(8,128)} fusion(f32[512,768]{1,0:T(8,128)S(1)} %get-tuple-element.231, f32[2048,768]{1,0:T(8,128)} %x_ref.1, s32[]{:T(128)S(6)} %select_n.56, f32[512]{0:T(512)S(1)} %broadcast_multiply_fusion, f32[512]{0:T(512)S(1)} %add_rsqrt_fusion, f32[512]{0:T(512)S(1)} %broadcast_multiply_fusion.1, ...), kind=kLoop, calls=%fused_computation.32 | loop fusion | flops 4718592 | bytes 8662020 | tf_op jit(solution)/shard_map/add | solution.py:647
  342.0 11.1 %all-to-all-done.5 = bf16[4,98,768]{2,1,0:T(8,128)(2,1)} async-done(((bf16[4,98,768]{2,1,0:T(8,128)(2,1)}), bf16[4,98,768]{2,1,0:T(8,128)(2,1)}, u32[]{:S(2)}, u32[]{:S(2)}) %all-to-all-start.5) | async-done | bytes 602144 | tf_op jit(solution)/shard_map/all_to_all | solution.py:441
  (294 shorter events, 114.6 us)
Async XLA Ops:
  2.8 43.0 %all-to-all-start = ((bf16[4,192,768]{2,1,0:T(8,128)(2,1)}), bf16[4,192,768]{2,1,0:T(8,128)(2,1)}, u32[]{:S(2)}, u32[]{:S(2)}) async-start(bf16[4,192,768]{2,1,0:T(8,128)(2,1)} %broadcast_in_dim.21), calls=%async_computation | async-start | bytes 2359296 | tf_op jit(solution)/shard_map/all_to_all | solution.py:441
  9.2 36.7 %collective-permute-start = (bf16[768,384]{1,0:T(8,128)(2,1)}, bf16[768,384]{1,0:T(8,128)(2,1)}, u32[]{:S(2)}, u32[]{:S(2)}) collective-permute-start(bf16[768,384]{1,0:T(8,128)(2,1)} %bitcast.5), channel_id=1, source_target_pairs={{0,1},{1,0},{2,3},{3,2},{4,5},{5,4},{6,7},{7,6},{8,9},{9,8},{10,11... | collective-permute-start | bytes 1769480 | tf_op jit(solution)/shard_map/ppermute | solution.py:437
  12.4 33.5 %collective-permute-start.1 = (bf16[384,768]{1,0:T(8,128)(2,1)}, bf16[384,768]{1,0:T(8,128)(2,1)}, u32[]{:S(2)}, u32[]{:S(2)}) collective-permute-start(bf16[384,768]{1,0:T(8,128)(2,1)} %bitcast.6), channel_id=1, source_target_pairs={{0,2},{1,3},{2,0},{3,1},{4,6},{5,7},{6,4},{7,5},{8,10},{9,11},{10,... | collective-permute-start | bytes 1769480 | tf_op jit(solution)/shard_map/ppermute | solution.py:437
  17.9 27.9 %collective-permute-start.2 = (bf16[256,768]{1,0:T(8,128)(2,1)}, bf16[256,768]{1,0:T(8,128)(2,1)S(1)}, u32[]{:S(2)}, u32[]{:S(2)}) collective-permute-start(bf16[256,768]{1,0:T(8,128)(2,1)} %get-tuple-element.109), channel_id=1, source_target_pairs={{0,4},{4,0},{8,12},{12,8},{1,5},{5,1},{9,13},{13,9},{2,6},{6,2},{1... | collective-permute-start | bytes 1179656 | tf_op jit(solution)/shard_map/ppermute | solution.py:437
  19.8 26.0 %collective-permute-start.3 = (bf16[256,768]{1,0:T(8,128)(2,1)S(1)}, bf16[256,768]{1,0:T(8,128)(2,1)S(1)}, u32[]{:S(2)}, u32[]{:S(2)}) collective-permute-start(bf16[256,768]{1,0:T(8,128)(2,1)S(1)} %get-tuple-element.110), channel_id=1, source_target_pairs={{0,8},{4,12},{8,0},{12,4},{1,9},{5,13},{9,1},{13,5},{2,10},{6,14},... | collective-permute-start | bytes 1179656 | tf_op jit(solution)/shard_map/ppermute | solution.py:437
  45.8 15.7 %all-to-all-start.1 = ((bf16[4,192,512]{2,1,0:T(8,128)(2,1)}), bf16[4,192,512]{2,1,0:T(8,128)(2,1)}, u32[]{:S(2)}, u32[]{:S(2)}) async-start(bf16[4,192,512]{2,1,0:T(8,128)(2,1)} %bitcast.10), calls=%async_computation.1 | async-start | bytes 1572864 | tf_op jit(solution)/shard_map/all_to_all | solution.py:441
  50.3 20.8 %collective-permute-start.4 = (bf16[256,768]{1,0:T(8,128)(2,1)}, bf16[256,768]{1,0:T(8,128)(2,1)S(1)}, u32[]{:S(2)}, u32[]{:S(2)}) collective-permute-start(bf16[256,768]{1,0:T(8,128)(2,1)} %copy-done.6), channel_id=1, source_target_pairs={{0,12},{4,8},{8,4},{12,0},{1,13},{5,9},{9,5},{13,1},{2,14},{6,10},... | collective-permute-start | bytes 1179656 | tf_op jit(solution)/shard_map/ppermute | solution.py:437
  53.2 32.0 %collective-permute-start.6 = (bf16[2,768,384]{2,1,0:T(8,128)(2,1)}, bf16[2,768,384]{2,1,0:T(8,128)(2,1)}, u32[]{:S(2)}, u32[]{:S(2)}) collective-permute-start(bf16[2,768,384]{2,1,0:T(8,128)(2,1)} %pad_maximum_fusion.2), channel_id=1, source_target_pairs={{0,2},{1,3},{2,0},{3,1},{4,6},{5,7},{6,4},{7,5},{8,10},{9,11},{10,... | collective-permute-start | bytes 3538952 | tf_op jit(solution)/shard_map/ppermute | solution.py:437
  57.6 27.6 %collective-permute-start.7 = (bf16[2,384,768]{2,1,0:T(8,128)(2,1)}, bf16[2,384,768]{2,1,0:T(8,128)(2,1)}, u32[]{:S(2)}, u32[]{:S(2)}) collective-permute-start(bf16[2,384,768]{2,1,0:T(8,128)(2,1)} %pad_maximum_fusion.3), channel_id=1, source_target_pairs={{0,1},{1,0},{2,3},{3,2},{4,5},{5,4},{6,7},{7,6},{8,9},{9,8},{10,11... | collective-permute-start | bytes 3538952 | tf_op jit(solution)/shard_map/ppermute | solution.py:437
  86.2 31.3 %collective-permute-start.12 = (bf16[264,768]{1,0:T(8,128)(2,1)S(1)}, bf16[264,768]{1,0:T(8,128)(2,1)S(1)}, u32[]{:S(2)}, u32[]{:S(2)}) collective-permute-start(bf16[264,768]{1,0:T(8,128)(2,1)S(1)} %get-tuple-element.248), channel_id=1, source_target_pairs={{0,8},{4,12},{8,0},{12,4},{1,9},{5,13},{9,1},{13,5},{2,10},{6,14},... | collective-permute-start | bytes 1216520 | tf_op jit(solution)/shard_map/ppermute | solution.py:437
  91.7 25.9 %collective-permute-start.13 = (bf16[576,768]{1,0:T(8,128)(2,1)S(1)}, bf16[576,768]{1,0:T(8,128)(2,1)S(1)}, u32[]{:S(2)}, u32[]{:S(2)}) collective-permute-start(bf16[576,768]{1,0:T(8,128)(2,1)S(1)} %pad_maximum_fusion.5.weight_ref), channel_id=1, source_target_pairs={{0,1},{1,0},{2,3},{3,2},{4,5},{5,4},{6,7},{7,6},{8,9},{9,8},{10,11... | collective-permute-start | bytes 2654216 | tf_op jit(solution)/shard_map/ppermute | solution.py:437
  93.2 24.4 %collective-permute-start.14 = (bf16[576,768]{1,0:T(8,128)(2,1)S(1)}, bf16[576,768]{1,0:T(8,128)(2,1)S(1)}, u32[]{:S(2)}, u32[]{:S(2)}) collective-permute-start(bf16[576,768]{1,0:T(8,128)(2,1)S(1)} %pad_maximum_fusion.5.weight_ref), channel_id=1, source_target_pairs={{0,2},{1,3},{2,0},{3,1},{4,6},{5,7},{6,4},{7,5},{8,10},{9,11},{10,... | collective-permute-start | bytes 2654216 | tf_op jit(solution)/shard_map/ppermute | solution.py:437
  118.3 22.0 %collective-permute-start.16 = (bf16[576,768]{1,0:T(8,128)(2,1)S(1)}, bf16[576,768]{1,0:T(8,128)(2,1)S(1)}, u32[]{:S(2)}, u32[]{:S(2)}) collective-permute-start(bf16[576,768]{1,0:T(8,128)(2,1)S(1)} %pad_maximum_fusion.5.weight_ref), channel_id=1, source_target_pairs={{0,3},{1,2},{2,1},{3,0},{4,7},{5,6},{6,5},{7,4},{8,11},{9,10},{10,... | collective-permute-start | bytes 2654216 | tf_op jit(solution)/shard_map/ppermute | solution.py:437
  119.8 15.5 %collective-permute-start.15 = (bf16[264,768]{1,0:T(8,128)(2,1)S(1)}, bf16[264,768]{1,0:T(8,128)(2,1)S(1)}, u32[]{:S(2)}, u32[]{:S(2)}) collective-permute-start(bf16[264,768]{1,0:T(8,128)(2,1)S(1)} %get-tuple-element.247), channel_id=1, source_target_pairs={{0,12},{4,8},{8,4},{12,0},{1,13},{5,9},{9,5},{13,1},{2,14},{6,10},... | collective-permute-start | bytes 1216520 | tf_op jit(solution)/shard_map/ppermute | solution.py:437
  167.0 18.7 %collective-permute-start.19 = (bf16[264,768]{1,0:T(8,128)(2,1)}, bf16[264,768]{1,0:T(8,128)(2,1)S(1)}, u32[]{:S(2)}, u32[]{:S(2)}) collective-permute-start(bf16[264,768]{1,0:T(8,128)(2,1)} %get-tuple-element.167), channel_id=1, source_target_pairs={{0,4},{4,0},{8,12},{12,8},{1,5},{5,1},{9,13},{13,9},{2,6},{6,2},{1... | collective-permute-start | bytes 1216520 | tf_op jit(solution)/shard_map/ppermute | solution.py:437
  168.1 30.6 %collective-permute-start.20 = (bf16[264,768]{1,0:T(8,128)(2,1)S(1)}, bf16[264,768]{1,0:T(8,128)(2,1)S(1)}, u32[]{:S(2)}, u32[]{:S(2)}) collective-permute-start(bf16[264,768]{1,0:T(8,128)(2,1)S(1)} %get-tuple-element.168), channel_id=1, source_target_pairs={{0,8},{4,12},{8,0},{12,4},{1,9},{5,13},{9,1},{13,5},{2,10},{6,14},... | collective-permute-start | bytes 1216520 | tf_op jit(solution)/shard_map/ppermute | solution.py:437
  169.1 29.6 %collective-permute-start.21 = (bf16[264,768]{1,0:T(8,128)(2,1)S(1)}, bf16[264,768]{1,0:T(8,128)(2,1)S(1)}, u32[]{:S(2)}, u32[]{:S(2)}) collective-permute-start(bf16[264,768]{1,0:T(8,128)(2,1)S(1)} %get-tuple-element.169), channel_id=1, source_target_pairs={{0,12},{4,8},{8,4},{12,0},{1,13},{5,9},{9,5},{13,1},{2,14},{6,10},... | collective-permute-start | bytes 1216520 | tf_op jit(solution)/shard_map/ppermute | solution.py:437
  204.9 41.5 %collective-permute-start.22 = (bf16[2,768,384]{2,1,0:T(8,128)(2,1)}, bf16[2,768,384]{2,1,0:T(8,128)(2,1)}, u32[]{:S(2)}, u32[]{:S(2)}) collective-permute-start(bf16[2,768,384]{2,1,0:T(8,128)(2,1)} %slice.110), channel_id=1, source_target_pairs={{0,1},{1,0},{2,3},{3,2},{4,5},{5,4},{6,7},{7,6},{8,9},{9,8},{10,11... | collective-permute-start | bytes 3538952 | tf_op jit(solution)/shard_map/ppermute | solution.py:437
  207.5 38.9 %collective-permute-start.23 = (bf16[2,768,384]{2,1,0:T(8,128)(2,1)}, bf16[2,768,384]{2,1,0:T(8,128)(2,1)}, u32[]{:S(2)}, u32[]{:S(2)}) collective-permute-start(bf16[2,768,384]{2,1,0:T(8,128)(2,1)} %slice.111), channel_id=1, source_target_pairs={{0,2},{1,3},{2,0},{3,1},{4,6},{5,7},{6,4},{7,5},{8,10},{9,11},{10,... | collective-permute-start | bytes 3538952 | tf_op jit(solution)/shard_map/ppermute | solution.py:437
  214.4 27.5 %all-to-all-start.2 = ((bf16[4,192,512]{2,1,0:T(8,128)(2,1)}), bf16[4,192,512]{2,1,0:T(8,128)(2,1)S(1)}, u32[]{:S(2)}, u32[]{:S(2)}) async-start(bf16[4,192,512]{2,1,0:T(8,128)(2,1)} %bitcast.25), calls=%async_computation.2 | async-start | bytes 1572864 | tf_op jit(solution)/shard_map/all_to_all | solution.py:441
  220.4 59.0 %collective-permute-start.26 = (bf16[256,768]{1,0:T(8,128)(2,1)}, bf16[256,768]{1,0:T(8,128)(2,1)}, u32[]{:S(2)}, u32[]{:S(2)}) collective-permute-start(bf16[256,768]{1,0:T(8,128)(2,1)} %get-tuple-element.186), channel_id=1, source_target_pairs={{0,4},{4,0},{8,12},{12,8},{1,5},{5,1},{9,13},{13,9},{2,6},{6,2},{1... | collective-permute-start | bytes 1179656 | tf_op jit(solution)/shard_map/ppermute | solution.py:437
  228.4 51.0 %collective-permute-start.27 = (bf16[256,768]{1,0:T(8,128)(2,1)}, bf16[256,768]{1,0:T(8,128)(2,1)}, u32[]{:S(2)}, u32[]{:S(2)}) collective-permute-start(bf16[256,768]{1,0:T(8,128)(2,1)} %get-tuple-element.187), channel_id=1, source_target_pairs={{0,8},{4,12},{8,0},{12,4},{1,9},{5,13},{9,1},{13,5},{2,10},{6,14},... | collective-permute-start | bytes 1179656 | tf_op jit(solution)/shard_map/ppermute | solution.py:437
  228.4 51.0 %collective-permute-start.28 = (bf16[256,768]{1,0:T(8,128)(2,1)}, bf16[256,768]{1,0:T(8,128)(2,1)}, u32[]{:S(2)}, u32[]{:S(2)}) collective-permute-start(bf16[256,768]{1,0:T(8,128)(2,1)} %get-tuple-element.188), channel_id=1, source_target_pairs={{0,12},{4,8},{8,4},{12,0},{1,13},{5,9},{9,5},{13,1},{2,14},{6,10},... | collective-permute-start | bytes 1179656 | tf_op jit(solution)/shard_map/ppermute | solution.py:437
  241.9 37.6 %all-to-all-start.3 = ((bf16[4,200,768]{2,1,0:T(8,128)(2,1)}), bf16[4,200,768]{2,1,0:T(8,128)(2,1)}, u32[]{:S(2)}, u32[]{:S(2)}) async-start(bf16[4,200,768]{2,1,0:T(8,128)(2,1)} %pad_maximum_fusion), calls=%async_computation.3 | async-start | bytes 2457600 | tf_op jit(solution)/shard_map/all_to_all | solution.py:441
  249.5 30.0 %collective-permute-start.24 = (bf16[768,384]{1,0:T(8,128)(2,1)}, bf16[768,384]{1,0:T(8,128)(2,1)}, u32[]{:S(2)}, u32[]{:S(2)}) collective-permute-start(bf16[768,384]{1,0:T(8,128)(2,1)} %slice_bitcast_fusion.7), channel_id=1, source_target_pairs={{0,2},{1,3},{2,0},{3,1},{4,6},{5,7},{6,4},{7,5},{8,10},{9,11},{10,... | collective-permute-start | bytes 1769480 | tf_op jit(solution)/shard_map/ppermute | solution.py:437
  254.0 25.4 %collective-permute-start.25 = (bf16[768,384]{1,0:T(8,128)(2,1)}, bf16[768,384]{1,0:T(8,128)(2,1)}, u32[]{:S(2)}, u32[]{:S(2)}) collective-permute-start(bf16[768,384]{1,0:T(8,128)(2,1)} %slice_bitcast_fusion.6), channel_id=1, source_target_pairs={{0,1},{1,0},{2,3},{3,2},{4,5},{5,4},{6,7},{7,6},{8,9},{9,8},{10,11... | collective-permute-start | bytes 1769480 | tf_op jit(solution)/shard_map/ppermute | solution.py:437
  280.8 31.7 %collective-permute-start.30 = (bf16[576,512]{1,0:T(8,128)(2,1)}, bf16[576,512]{1,0:T(8,128)(2,1)}, u32[]{:S(2)}, u32[]{:S(2)}) collective-permute-start(bf16[576,512]{1,0:T(8,128)(2,1)} %get-tuple-element.246), channel_id=1, source_target_pairs={{0,2},{1,3},{2,0},{3,1},{4,6},{5,7},{6,4},{7,5},{8,10},{9,11},{10,... | collective-permute-start | bytes 1769480 | tf_op jit(solution)/shard_map/ppermute | solution.py:437
  281.3 33.2 %collective-permute-start.29 = (bf16[576,512]{1,0:T(8,128)(2,1)}, bf16[576,512]{1,0:T(8,128)(2,1)}, u32[]{:S(2)}, u32[]{:S(2)}) collective-permute-start(bf16[576,512]{1,0:T(8,128)(2,1)} %get-tuple-element.244), channel_id=1, source_target_pairs={{0,1},{1,0},{2,3},{3,2},{4,5},{5,4},{6,7},{7,6},{8,9},{9,8},{10,11... | collective-permute-start | bytes 1769480 | tf_op jit(solution)/shard_map/ppermute | solution.py:437
  292.1 48.3 %collective-permute-start.37 = (bf16[2,768,384]{2,1,0:T(8,128)(2,1)}, bf16[2,768,384]{2,1,0:T(8,128)(2,1)}, u32[]{:S(2)}, u32[]{:S(2)}) collective-permute-start(bf16[2,768,384]{2,1,0:T(8,128)(2,1)} %pad_maximum_fusion.4), channel_id=1, source_target_pairs={{0,16},{16,0},{1,17},{17,1},{2,18},{18,2},{3,19},{19,3},{4,20},{20... | collective-permute-start | bytes 3538952 | tf_op jit(solution)/shard_map/ppermute | solution.py:437
  298.1 18.5 %collective-permute-start.31 = (bf16[576,512]{1,0:T(8,128)(2,1)}, bf16[576,512]{1,0:T(8,128)(2,1)}, u32[]{:S(2)}, u32[]{:S(2)}) collective-permute-start(bf16[576,512]{1,0:T(8,128)(2,1)} %get-tuple-element.245), channel_id=1, source_target_pairs={{0,3},{1,2},{2,1},{3,0},{4,7},{5,6},{6,5},{7,4},{8,11},{9,10},{10,... | collective-permute-start | bytes 1769480 | tf_op jit(solution)/shard_map/ppermute | solution.py:437
  302.1 27.7 %all-to-all-start.4 = ((bf16[4,98,768]{2,1,0:T(8,128)(2,1)}), bf16[4,98,768]{2,1,0:T(8,128)(2,1)}, u32[]{:S(2)}, u32[]{:S(2)}) async-start(bf16[4,98,768]{2,1,0:T(8,128)(2,1)} %reshape.164), calls=%async_computation.4 | async-start | bytes 1277952 | tf_op jit(solution)/shard_map/all_to_all | solution.py:441
  331.9 21.2 %all-to-all-start.5 = ((bf16[4,98,768]{2,1,0:T(8,128)(2,1)}), bf16[4,98,768]{2,1,0:T(8,128)(2,1)}, u32[]{:S(2)}, u32[]{:S(2)}) async-start(bf16[4,98,768]{2,1,0:T(8,128)(2,1)} %broadcast_in_dim.26), calls=%async_computation.5 | async-start | bytes 1277952 | tf_op jit(solution)/shard_map/all_to_all | solution.py:441
  (80 other events, 569.3 us)

commit v2 on v1

--- a/solution.py
+++ b/solution.py
@@ -192,25 +192,121 @@
     )(proj, proj, proj, mixed, grads, logs, vectors)
 
 
-def place_kernel(capacity, flat_ref, rows_ref, place_ref, *piece_refs):
-    flat = flat_ref[...]
+def dot_exact(a, b, axes):
+    return lax.dot_general(
+        a, b, ((axes[:1], axes[1:]), ((), ())), precision=HIGHEST, preferred_element_type=jnp.float32
+    )
+
+
+def place_kernel(capacity, row_ref, column_ref, rows_ref, place_ref, turned_ref, *piece_refs):
+    flat = row_ref[...]
+    column = column_ref[...]
     for k, ref in enumerate(piece_refs):
+        span = slice(k * capacity, (k + 1) * capacity)
         index = lax.broadcasted_iota(jnp.int32, (capacity, flat.shape[1]), 0) + k * capacity
         hot = (index == flat).astype(jnp.bfloat16)
-        place_ref[k * capacity : (k + 1) * capacity, :] = hot
+        place_ref[span, :] = hot
         ref[...] = dot_nn(hot, rows_ref[...]).astype(jnp.bfloat16)
+    index = lax.broadcasted_iota(jnp.int32, turned_ref.shape, 1)
+    turned_ref[...] = (index == column).astype(jnp.bfloat16)
 
 
 def place_rows(flat, rows, pieces, capacity):
     count, width = rows.shape
     outs = pl.pallas_call(
         functools.partial(place_kernel, capacity),
-        out_shape=[jax.ShapeDtypeStruct((pieces * capacity, count), jnp.bfloat16)]
+        out_shape=[
+            jax.ShapeDtypeStruct((pieces * capacity, count), jnp.bfloat16),
+            jax.ShapeDtypeStruct((count, pieces * capacity), jnp.bfloat16),
+        ]
         + [jax.ShapeDtypeStruct((capacity, width), jnp.bfloat16)] * pieces,
         compiler_params=pltpu.CompilerParams(vmem_limit_bytes=48 * 2**20),
         cost_estimate=cost(2 * pieces * capacity * count * width),
-    )(flat[None, :], rows)
-    return outs[0], list(outs[1:])
+    )(flat[None, :], flat[:, None], rows)
+    return outs[0], outs[1], list(outs[2:])
+
+
+def second_norm(rows, gain):
+    scale = lax.rsqrt(jnp.mean(rows * rows, axis=-1, keepdims=True) + EPSILON)
+    hat = rows * scale
+    return scale, hat, hat * gain
+
+
+def send_kernel(capacity, mixed_ref, weight_ref, rows_ref, gain_ref, router_ref, hot_ref, place_ref, *refs):
+    residual_ref, probs_ref, gate_ref = refs[:3]
+    residual = rows_ref[...] + dot_tn(mixed_ref[...], weight_ref[...])
+    residual_ref[...] = residual
+    _, _, normed = second_norm(residual, gain_ref[...])
+    logits = dot_exact(router_ref[...], normed, (1, 1))
+    logits = jnp.exp(logits - jnp.max(logits, axis=0, keepdims=True))
+    probs = logits / jnp.sum(logits, axis=0, keepdims=True)
+    probs_ref[...] = probs
+    gate = jnp.sum(probs * hot_ref[...], axis=0, keepdims=True)
+    gate_ref[...] = gate
+    low = normed.astype(jnp.bfloat16)
+    gates = jnp.broadcast_to(gate.astype(jnp.bfloat16), (8, gate.shape[1]))
+    for k, ref in enumerate(refs[3:]):
+        place = place_ref[k * capacity : (k + 1) * capacity, :]
+        ref[:capacity, :] = dot_nn(place, low).astype(jnp.bfloat16)
+        ref[capacity : capacity + 8, :] = jnp.zeros((8, ref.shape[1]), jnp.bfloat16)
+        ref[capacity : capacity + 8, :capacity] = dot_nt(gates, place).astype(jnp.bfloat16)
+
+
+def send_rows(mixed, weight, rows, gain, router, hot, place):
+    experts, count = hot.shape
+    width = rows.shape[1]
+    capacity = place.shape[0] // experts
+    outs = pl.pallas_call(
+        functools.partial(send_kernel, capacity),
+        out_shape=[
+            jax.ShapeDtypeStruct((count, width), jnp.float32),
+            jax.ShapeDtypeStruct((experts, count), jnp.float32),
+            jax.ShapeDtypeStruct((1, count), jnp.float32),
+        ]
+        + [jax.ShapeDtypeStruct((capacity + 8, width), jnp.bfloat16)] * experts,
+        compiler_params=pltpu.CompilerParams(vmem_limit_bytes=48 * 2**20),
+        cost_estimate=cost(6 * width * count * width),
+    )(mixed, weight, rows, gain, router, hot, place)
+    return outs[0], outs[1], outs[2], list(outs[3:])
+
+
+def receive_kernel(capacity, residual_ref, cot_ref, gain_ref, router_ref, hot_ref, probs_ref, gate_ref, place_ref, turned_ref, weight_ref, *refs):
+    backs, (grad_ref, low_ref, heads_ref, router_grad_ref, gain_grad_ref) = refs[:-5], refs[-5:]
+    scale, hat, normed = second_norm(residual_ref[...], gain_ref[...])
+    grad, pair = 0.0, 0.0
+    for k, ref in enumerate(backs):
+        span = slice(k * capacity, (k + 1) * capacity)
+        grad = grad + dot_nn(turned_ref[:, span], ref[:capacity, :])
+        pair = pair + dot_nn(ref[capacity : capacity + 8, :capacity], place_ref[span, :])
+    grad_gate = jnp.sum(pair, axis=0, keepdims=True)
+    grad_logits = probs_ref[...] * (hot_ref[...] - gate_ref[...]) * grad_gate
+    router_grad_ref[...] = dot_exact(grad_logits, normed, (1, 0))
+    grad = grad + dot_exact(grad_logits, router_ref[...], (0, 0))
+    gain_grad_ref[...] = jnp.sum(grad * hat, axis=0, keepdims=True)
+    scaled = grad * gain_ref[...]
+    grad = scale * (scaled - hat * jnp.mean(scaled * hat, axis=-1, keepdims=True))
+    grad = grad + cot_ref[...].astype(jnp.float32)
+    grad_ref[...] = grad
+    low = grad.astype(jnp.bfloat16)
+    low_ref[...] = low
+    heads_ref[...] = dot_nt(weight_ref[...], low).astype(jnp.bfloat16)
+
+
+def receive_rows(residual, cot, gain, router, hot, probs, gate, place, turned, weight, backs):
+    experts, count = hot.shape
+    width = residual.shape[1]
+    return pl.pallas_call(
+        functools.partial(receive_kernel, place.shape[0] // experts),
+        out_shape=[
+            jax.ShapeDtypeStruct((count, width), jnp.float32),
+            jax.ShapeDtypeStruct((count, width), jnp.bfloat16),
+            jax.ShapeDtypeStruct((weight.shape[0], count), jnp.bfloat16),
+            jax.ShapeDtypeStruct((experts, width), jnp.float32),
+            jax.ShapeDtypeStruct((1, width), jnp.float32),
+        ],
+        compiler_params=pltpu.CompilerParams(vmem_limit_bytes=48 * 2**20),
+        cost_estimate=cost(6 * width * count * width),
+    )(residual, cot, gain, router, hot, probs, gate, place, turned, weight, *backs)
 
 
 def project_kernel(x_ref, gain_ref, weight_ref, out_ref, normed_ref):
@@ -254,10 +350,9 @@
     return values * half, slope
 
 
-def expert_kernel(places, arrays, pieces, *refs):
+def expert_kernel(parts, pieces, *refs):
     row_refs, grad_refs, refs = refs[:pieces], refs[pieces : 2 * pieces], refs[2 * pieces :]
-    first_refs, second_refs, refs = refs[:arrays], refs[arrays : 2 * arrays], refs[2 * arrays :]
-    parts = len(places)
+    first_refs, second_refs, refs = refs[:parts], refs[parts : 2 * parts], refs[2 * parts :]
     act_ref, pre_ref, xt_ref, lt_ref = refs[:4]
     res_refs, back_refs = refs[4 : 4 + pieces], refs[4 + pieces : 4 + 2 * pieces]
     rows, low, res_sum, back_sum, firsts, seconds, sems = refs[4 + 2 * pieces :]
@@ -268,11 +363,12 @@
     tile = min(count, 256)
 
     def fetch(j):
-        (one, at), (two, there) = places[j]
-        return (
-            pltpu.make_async_copy(first_refs[one].at[at], firsts.at[j % 2], sems.at[0, j % 2]),
-            pltpu.make_async_copy(second_refs[two].at[there], seconds.at[j % 2], sems.at[1, j % 2]),
-        )
+        copies = []
+        for i in range(2):
+            to = (j % 2, i)
+            copies.append(pltpu.make_async_copy(first_refs[2 * j + i], firsts.at[to], sems.at[(0,) + to]))
+            copies.append(pltpu.make_async_copy(second_refs[2 * j + i], seconds.at[to], sems.at[(1,) + to]))
+        return copies
 
     @pl.when(step == 0)
     def _():
@@ -286,11 +382,11 @@
         res_sum[...] = jnp.zeros_like(res_sum)
         back_sum[...] = jnp.zeros_like(back_sum)
 
-    for j in range(parts):
+    for j in range(parts // 2):
 
         @pl.when(step == j)
         def _(j=j):
-            if j + 1 < parts:
+            if j + 1 < parts // 2:
                 for copy in fetch(j + 1):
                     copy.start()
             for copy in fetch(j):
@@ -301,19 +397,21 @@
         xt_ref[...] = rows[...].T
         lt_ref[...] = low[...].T
 
-    first = firsts[step % 2]
-    second = seconds[step % 2]
-    for start in range(0, count, tile):
-        span = pl.ds(start, tile)
-        active, slope = gelu_parts(dot_nn(rows[span, :], first))
+    slot = step % 2
+    spans = [pl.ds(start, tile) for start in range(0, count, tile)]
+    chains = [(i, span) for span in spans for i in range(2)]
+    values = [dot_nn(rows[span, :], firsts[slot, i]) for i, span in chains]
+    grads = [dot_nt(low[span, :], seconds[slot, i]) for i, span in chains]
+    for (i, span), value, grad in zip(chains, values, grads):
+        active, slope = gelu_parts(value)
         active = active.astype(jnp.bfloat16)
-        act_ref[0, span, :] = active
-        res_sum[span, :] += dot_nn(active, second)
-        pre = (dot_nt(low[span, :], second) * slope).astype(jnp.bfloat16)
-        pre_ref[0, span, :] = pre
-        back_sum[span, :] += dot_nt(pre, first)
-
-    @pl.when(step == parts - 1)
+        act_ref[i, span, :] = active
+        res_sum[span, :] += dot_nn(active, seconds[slot, i])
+        pre = (grad * slope).astype(jnp.bfloat16)
+        pre_ref[i, span, :] = pre
+        back_sum[span, :] += dot_nt(pre, firsts[slot, i])
+
+    @pl.when(step == parts // 2 - 1)
     def _():
         for e in range(pieces):
             span = pl.ds(e * capacity, capacity)
@@ -330,34 +428,23 @@
             back_refs[e][capacity : capacity + 8, :capacity] = pair.astype(jnp.bfloat16)
 
 
-PLACES = (
-    ((0, 0), (0, 0)),
-    ((1, 0), (1, 0)),
-    ((2, 0), (4, 0)),
-    ((3, 0), (5, 0)),
-    ((4, 0), (2, 0)),
-    ((4, 1), (4, 1)),
-    ((5, 0), (3, 0)),
-    ((5, 1), (5, 1)),
-)
-MINE = ((0, 4, 2, 5), (0, 2, 4, 5))
-OTHER = ((1, 6, 3, 7), (1, 3, 6, 7))
+MINE = ((0, 4, 2, 6), (0, 2, 4, 6))
+OTHER = ((1, 5, 3, 7), (1, 3, 5, 7))
 
 
 def expert_apply(arrived, grads, firsts, seconds):
     pieces = len(grads)
     capacity, width = grads[0].shape
     count = pieces * capacity
-    hidden = firsts[0].shape[2]
-    parts, arrays = len(PLACES), len(firsts)
+    parts, hidden = len(firsts), firsts[0].shape[1]
     sent = pl.BlockSpec(arrived[0].shape, lambda i: (0, 0))
     whole = pl.BlockSpec((capacity, width), lambda i: (0, 0))
-    kept = pl.BlockSpec((1, count, hidden), lambda i: (i, 0, 0))
+    kept = pl.BlockSpec((2, count, hidden), lambda i: (i, 0, 0))
     turned = pl.BlockSpec((width, count), lambda i: (0, 0))
     outs = pl.pallas_call(
-        functools.partial(expert_kernel, PLACES, arrays, pieces),
-        grid=(parts,),
-        in_specs=[sent] * pieces + [whole] * pieces + [pl.BlockSpec(memory_space=pl.ANY)] * (2 * arrays),
+        functools.partial(expert_kernel, parts, pieces),
+        grid=(parts // 2,),
+        in_specs=[sent] * pieces + [whole] * pieces + [pl.BlockSpec(memory_space=pl.ANY)] * (2 * parts),
         out_specs=[kept, kept, turned, turned] + [whole] * pieces + [sent] * pieces,
         out_shape=[
             jax.ShapeDtypeStruct((parts, count, hidden), jnp.bfloat16),
@@ -372,9 +459,9 @@
             pltpu.VMEM((count, width), jnp.bfloat16),
             pltpu.VMEM((count, width), jnp.float32),
             pltpu.VMEM((count, width), jnp.float32),
-            pltpu.VMEM((2, width, hidden), jnp.bfloat16),
-            pltpu.VMEM((2, hidden, width), jnp.bfloat16),
-            pltpu.SemaphoreType.DMA((2, 2)),
+            pltpu.VMEM((2, 2, width, hidden), jnp.bfloat16),
+            pltpu.VMEM((2, 2, hidden, width), jnp.bfloat16),
+            pltpu.SemaphoreType.DMA((2, 2, 2)),
         ],
         compiler_params=pltpu.CompilerParams(vmem_limit_bytes=52 * 2**20),
         cost_estimate=cost(12 * count * width * hidden * parts),
@@ -382,20 +469,29 @@
     return list(outs[:4]), list(outs[4 : 4 + pieces]), list(outs[4 + pieces :])
 
 
-def weight_kernel(groups, added, *refs):
+def weight_kernel(groups, *refs):
+    step = pl.program_id(0)
+    outs = refs[4 * groups :]
+    steps = pl.num_programs(0) // 2
     for out, (left, right) in enumerate(((2, 1), (3, 0))):
         total = 0.0
         for g in range(groups):
             total = total + dot_nn(refs[4 * g + left][...], refs[4 * g + right][0])
-        if added:
-            total = total + refs[4 * groups + out][0].astype(jnp.float32)
-        refs[4 * groups + 2 * added + out][0] = total.astype(jnp.bfloat16)
-
-
-def expert_weights(groups, chosen, added=()):
+        total = total.astype(jnp.bfloat16)
+
+        @pl.when(step < steps)
+        def _():
+            outs[out][0] = total
+
+        @pl.when(step >= steps)
+        def _():
+            outs[2 + out][0] = total
+
+
+def expert_weights(groups):
+    chosen = [OTHER[i] + MINE[i] for i in range(2)]
     steps, hidden = len(chosen[0]), groups[0][0].shape[2]
     width = groups[0][2].shape[0]
-    count = sum(group[2].shape[1] for group in groups)
     specs, arrays = [], []
 
     def pick(i, which):
@@ -411,16 +507,19 @@
             whole,
         ]
         arrays += [act, pre, xt, lt]
-    part = pl.BlockSpec((1, width, hidden), lambda i: (i, 0, 0))
+    half = steps // 2
+    early = pl.BlockSpec((1, width, hidden), lambda i: (jnp.minimum(i, half - 1), 0, 0))
+    late = pl.BlockSpec((1, width, hidden), lambda i: (jnp.maximum(i - half, 0), 0, 0))
+    count = sum(group[2].shape[1] for group in groups)
     return pl.pallas_call(
-        functools.partial(weight_kernel, len(groups), len(added) // 2),
+        functools.partial(weight_kernel, len(groups)),
         grid=(steps,),
-        in_specs=specs + [part] * len(added),
-        out_specs=[part, part],
-        out_shape=[jax.ShapeDtypeStruct((steps, width, hidden), jnp.bfloat16)] * 2,
+        in_specs=specs,
+        out_specs=[early, early, late, late],
+        out_shape=[jax.ShapeDtypeStruct((half, width, hidden), jnp.bfloat16)] * 4,
         compiler_params=pltpu.CompilerParams(vmem_limit_bytes=50 * 2**20),
         cost_estimate=cost(6 * count * width * hidden * steps),
-    )(*arrays, *added)
+    )(*arrays)
 
 
 def inverse_rms(rows):
@@ -441,28 +540,12 @@
     return lax.all_to_all(array, axis, 0, 0, tiled=True)
 
 
+def low_sum(*arrays):
+    return sum(array.astype(jnp.float32) for array in arrays).astype(jnp.bfloat16)
+
+
 def spread(array, axis):
     return trade(jnp.broadcast_to(array[None], (lax.axis_size(axis),) + array.shape), axis)
-
-
-def sum_copies(partial):
-    experts = lax.axis_size("expert")
-    rank = lax.axis_index("dp")
-    kept = partial.shape[0]
-    partial = jnp.pad(partial, ((0, -kept % (2 * experts)), (0, 0)))
-    rows, columns = partial.shape
-    half = rows // 2
-    mine = lax.dynamic_slice_in_dim(partial, rank * half, half, 0)
-    other = lax.dynamic_slice_in_dim(partial, (1 - rank) * half, half, 0).astype(jnp.bfloat16)
-    mine = (mine + swap(other, "dp", 1).astype(jnp.float32)).astype(jnp.bfloat16)
-    shares = trade(mine.reshape(experts, half // experts, columns), "expert")
-    share = jnp.sum(shares.astype(jnp.float32), axis=0).astype(jnp.bfloat16)
-    mine = spread(share, "expert").reshape(half, columns)
-    other = swap(mine, "dp", 1)
-    first = rank == 0
-    return jnp.concatenate(
-        [jnp.where(first, mine, other), jnp.where(first, other, mine)], axis=0
-    )[:kept].astype(jnp.float32)
 
 
 def on_device(
@@ -510,8 +593,7 @@
     slot = jnp.sum(before * own_hot, axis=-1).astype(jnp.int32)
     flat = (routes ^ lax.axis_index("expert")) * capacity + slot
     cot_low = lax.dynamic_slice_in_dim(cotangent, own_start, own_rows, 0)
-    cot_own = cot_low.astype(jnp.float32)
-    place_hot, grad_in = place_rows(flat, cot_low, experts, capacity)
+    place_hot, place_turned, grad_in = place_rows(flat, cot_low, experts, capacity)
     near = experts // 2
     far = near + experts // 4
     grad_in = [grad_in[0]] + [swap(grad_in[k], "expert", k) for k in range(1, far)] + grad_in[far:]
@@ -521,46 +603,44 @@
     high_bit = tensor_count // 2
     first_near = swap(first_mine, "tensor", 1)
     second_near = swap(second_mine, "tensor", high_bit)
+    first_far = [swap(first_mine, "tensor", high_bit)]
+    second_far = [swap(second_mine, "tensor", 1)]
     turned = jnp.concatenate([bucket[::-1], jnp.full((1,), -1, jnp.int32)])
     bucket_hot = jnp.arange(NUM_BUCKETS, dtype=jnp.int32)[:, None] == turned[None, :]
     vectors = dot_tn(bias_table, bucket_hot.astype(jnp.bfloat16))[:, None, :]
     mixed, logs = attend(projected, vectors, own_rows)
-    mixed, output_full, first_near, second_near, grad_in[1:far] = lax.optimization_barrier(
-        (mixed, output_full, first_near, second_near, grad_in[1:far])
+    mixed, output_full, first_near, second_near, first_far, second_far, grad_in[1:far] = (
+        lax.optimization_barrier(
+            (mixed, output_full, first_near, second_near, first_far, second_far, grad_in[1:far])
+        )
     )
     output_full = output_full.reshape(tensor_count * inner, width)
-    first_far = swap(jnp.stack([first_mine, first_near]), "tensor", high_bit)
-    second_far = swap(jnp.stack([second_mine, second_near]), "tensor", 1)
+    first_far.append(swap(first_near, "tensor", high_bit))
+    second_far.append(swap(second_near, "tensor", 1))
     grad_in[far:] = [swap(grad_in[k], "expert", k) for k in range(far, experts)]
     mixed_own = trade(mixed.reshape(tensor_count, inner, own_rows), "tensor").reshape(
         tensor_count * inner, own_rows
     )
 
     input_own = lax.dynamic_slice_in_dim(layer_input, own_start, own_rows, 0)
-    residual = input_own + dot_tn(mixed_own, output_full)
-    gain_two = norm2_gain.astype(jnp.float32)
-    inv_two = inverse_rms(residual)
-    hat_two = residual * inv_two
-    normed_two = hat_two * gain_two
-    router_wide = router.astype(jnp.float32)
-    router_probs = jax.nn.softmax(jnp.dot(normed_two, router_wide, precision=HIGHEST), axis=-1)
-    gate_full = jnp.sum(router_probs * own_hot, axis=-1)
-    gate_low = gate_full.astype(jnp.bfloat16)
-    send_rows = dot_nn(place_hot, normed_two.astype(jnp.bfloat16)).astype(jnp.bfloat16)
-    send_gates = dot_nn(place_hot, gate_low[:, None]).astype(jnp.bfloat16)
-    gate_rows = jnp.pad(send_gates.reshape(experts, 1, capacity), ((0, 0), (0, 7), (0, width - capacity)))
-    sent = jnp.concatenate([send_rows.reshape(experts, capacity, width), gate_rows], axis=1)
+    gain_two = norm2_gain.astype(jnp.float32)[None, :]
+    router_turned = router.astype(jnp.float32).T
+    hot_turned = own_hot.T
+    residual, router_probs, gate, sent = send_rows(
+        mixed_own, output_full, input_own, gain_two, router_turned, hot_turned, place_hot
+    )
     sent, grad_in[far:] = lax.optimization_barrier((sent, grad_in[far:]))
     arrived = [sent[0]] + [swap(sent[k], "expert", k) for k in range(1, experts)]
 
-    arrived[1:near], first_far, second_far = lax.optimization_barrier(
-        (arrived[1:near], first_far, second_far)
-    )
-    first_parts = [first_mine[None], first_other[None]]
-    second_parts = [second_mine[None], second_other[None]]
-    for first, second in ((first_near[None], second_near[None]), (first_far, second_far)):
+    first_parts, second_parts = [first_mine, first_other], [second_mine, second_other]
+    for first, second in ((first_near, second_far[0]), (first_far[0], second_near)):
         first_parts += [first, swap(first, "dp", 1)]
         second_parts += [second, swap(second, "dp", 1)]
+    arrived[1:near], first, second = lax.optimization_barrier(
+        (arrived[1:near], first_far[1], second_far[1])
+    )
+    first_parts += [first, swap(first, "dp", 1)]
+    second_parts += [second, swap(second, "dp", 1)]
     arrived[:near], first_parts, second_parts, joined = lax.optimization_barrier(
         (arrived[:near], first_parts, second_parts, w_joined)
     )
@@ -574,48 +654,47 @@
             )
             joined_parts.append(swap(joined, "tensor", tensor_count - 1))
         if low == far:
-            results, pieces, joined_parts = lax.optimization_barrier((results, pieces, joined_parts))
+            results, pieces = lax.optimization_barrier((results, pieces))
         kept, res, back = expert_apply(pieces, grad_in[low:high], first_parts, second_parts)
         groups.append(kept)
         results += res
         back_got += [
             back[k - low] if k == 0 else swap(back[k - low], "expert", k) for k in range(low, high)
         ]
-    others = expert_weights(groups, OTHER)
-    first_sum, second_sum = expert_weights(groups, MINE, [swap(part, "dp", 1) for part in others])
-    first_sum, second_sum, back_got = lax.optimization_barrier((first_sum, second_sum, back_got))
-    first_got = swap(first_sum[2:], "tensor", 1)
-    second_got = swap(second_sum[2:], "tensor", high_bit)
-
-    grad_normed_two = dot_tn(place_hot, jnp.concatenate([back[:capacity] for back in back_got]))
-    pair_got = jnp.concatenate([back[capacity : capacity + 2, :capacity].T for back in back_got])
-    grad_gate = jnp.sum(dot_tn(place_hot, pair_got), axis=-1)
-    grad_logits = router_probs * (own_hot - gate_full[:, None]) * grad_gate[:, None]
-    grad_router = jnp.einsum("td,te->ed", normed_two, grad_logits, precision=HIGHEST)
-    grad_normed_two = grad_normed_two + jnp.einsum(
-        "te,de->td", grad_logits, router_wide, precision=HIGHEST
-    )
-    grad_norm_two = jnp.sum(grad_normed_two * hat_two, axis=0)
-    grad_residual = cot_own + norm_backward(grad_normed_two, gain_two, hat_two, inv_two)
-    grad_low = grad_residual.astype(jnp.bfloat16)
-    grad_heads = dot_nt(output_full, grad_low).astype(jnp.bfloat16)
+    groups, joined_parts = lax.optimization_barrier((groups, joined_parts))
+    first_other, second_other, first_sum, second_sum = expert_weights(groups)
+    first_other, second_other, first_sum, second_sum, back_got = lax.optimization_barrier(
+        (first_other, second_other, first_sum, second_sum, back_got)
+    )
+    first_other, second_other = swap(first_other, "dp", 1), swap(second_other, "dp", 1)
+
+    grad_residual, grad_low, grad_heads, grad_router, grad_norm_two = receive_rows(
+        residual,
+        cot_low,
+        gain_two,
+        router_turned,
+        hot_turned,
+        router_probs,
+        gate,
+        place_hot,
+        place_turned,
+        output_full,
+        back_got,
+    )
     heads_got = trade(grad_heads.reshape(tensor_count, inner, own_rows), "tensor")
     grad_wo = dot_nn(mixed_own, grad_low).astype(jnp.bfloat16).reshape(tensor_count, inner, width)
-    shared = jnp.concatenate([grad_router, grad_norm_two[None]], axis=0).astype(jnp.bfloat16)
+    shared = jnp.concatenate([grad_router, grad_norm_two], axis=0).astype(jnp.bfloat16)
     shared = jnp.pad(shared, ((0, -shared.shape[0] % 8), (0, 0)))
     shared = jnp.broadcast_to(shared[None], (tensor_count,) + shared.shape)
     grad_wo = trade(jnp.concatenate([grad_wo, shared], axis=1), "tensor")
     _, *results = lax.optimization_barrier((grad_low, *results))
     returned = [results[0]] + [swap(results[k], "expert", k) for k in range(1, experts)]
 
-    heads_got, first_got, second_got = lax.optimization_barrier((heads_got, first_got, second_got))
-    first_pair = (first_sum[:2].astype(jnp.float32) + first_got.astype(jnp.float32)).astype(jnp.bfloat16)
-    second_pair = (second_sum[:2].astype(jnp.float32) + second_got.astype(jnp.float32)).astype(
-        jnp.bfloat16
-    )
-    first_got = swap(first_pair[1], "tensor", high_bit)
-    second_got = swap(second_pair[1], "tensor", 1)
-
+    heads_got, first_other, second_other = lax.optimization_barrier(
+        (heads_got, first_other, second_other)
+    )
+    first_got = swap(low_sum(first_sum[2:], first_other[2:]), "tensor", 1)
+    second_got = swap(low_sum(second_sum[2:], second_other[2:]), "tensor", high_bit)
     head_shape = (tensor_count, local_heads, HEAD_DIM, own_rows)
     grad_projected, diagonals = attend_back(
         projected, vectors, mixed, heads_got.reshape(head_shape), logs
@@ -625,27 +704,12 @@
         (grad_projected, first_got, second_got, returned, grad_wo)
     )
 
-    pairs = ((first_pair, first_got), (second_pair, second_got))
-    total = jnp.stack([pair[0].astype(jnp.float32) + got.astype(jnp.float32) for pair, got in pairs])
-    total = total.astype(jnp.bfloat16)
-    rest = swap(total, "dp", 1)
-    first = dp_rank == 0
-    both = jnp.concatenate(
-        [jnp.where(first, total, rest), jnp.where(first, rest, total)], axis=2
-    ).astype(jnp.float32)
-    output = residual + gate_low.astype(jnp.float32)[:, None] * dot_tn(
-        place_hot, jnp.concatenate(returned)
-    )
-
-    grad_normed_one = dot_tn(
-        lax.dynamic_index_in_dim(grad_projected, tensor_rank, 0, keepdims=False), w_joined
-    )
+    grad_got = [lax.dynamic_index_in_dim(grad_projected, tensor_rank, 0, keepdims=False)]
     for k in range(1, tensor_count):
         sent = lax.dynamic_index_in_dim(grad_projected, tensor_rank ^ k, 0, keepdims=False)
-        grad_normed_one = grad_normed_one + dot_tn(swap(sent, "tensor", k), joined_parts[k])
-    inv_own = inverse_rms(input_own)
-    input_grad = grad_residual + norm_backward(grad_normed_one, gain_one, input_own * inv_own, inv_own)
-
+        grad_got.append(swap(sent, "tensor", k))
+
+    grad_wo = jnp.sum(grad_wo.astype(jnp.float32), axis=0)
     grad_joined = jnp.einsum(
         "bcn,bnd->cd",
         grad_projected,
@@ -658,20 +722,51 @@
     ).reshape(-1)
     table_size = grad_table.shape[0]
     used = 3 * inner
-    joined = sum_copies(
-        jnp.concatenate(
-            [
-                grad_joined,
-                jnp.sum(grad_wo.astype(jnp.float32), axis=0),
-                norm_one[None],
-                jnp.pad(grad_table, (0, width - table_size))[None],
-            ],
-            axis=0,
-        )
-    )
+    main = jnp.concatenate(
+        [grad_joined, grad_wo, jnp.pad(grad_table, (0, width - table_size))[None]], axis=0
+    )
+    main = jnp.pad(main, ((0, -main.shape[0] % 16), (0, 0)))
+    rows = main.shape[0] // 2
+    main_mine = lax.dynamic_slice_in_dim(main, dp_rank * rows, rows, 0)
+    main_other = lax.dynamic_slice_in_dim(main, (1 - dp_rank) * rows, rows, 0)
+    extra = jnp.pad(norm_one[None], ((0, (-rows - 1) % max(8, experts)), (0, 0)))
+    main_mine = jnp.concatenate([main_mine, extra], axis=0)
+    main_other = jnp.concatenate([main_other, extra], axis=0).astype(jnp.bfloat16)
+    main_other, returned, first_got, second_got = lax.optimization_barrier(
+        (swap(main_other, "dp", 1), returned, first_got, second_got)
+    )
+    main_mine = (main_mine + main_other.astype(jnp.float32)).astype(jnp.bfloat16)
+    shares = trade(main_mine.reshape(experts, -1, width), "expert")
+
+    first_pair = low_sum(first_sum[:2], first_other[:2], first_got)
+    second_pair = low_sum(second_sum[:2], second_other[:2], second_got)
+    first_got = swap(first_pair[1], "tensor", high_bit)
+    second_got = swap(second_pair[1], "tensor", 1)
+    output = residual + gate[0].astype(jnp.bfloat16).astype(jnp.float32)[:, None] * dot_nn(
+        place_turned, jnp.concatenate(returned)
+    )
+    shares, grad_got, input_own = lax.optimization_barrier((shares, grad_got, input_own))
+    main_mine = spread(low_sum(*shares), "expert").reshape(main_mine.shape)
+    main_mine, first_got, second_got = lax.optimization_barrier((main_mine, first_got, second_got))
+    pairs = ((first_pair, first_got), (second_pair, second_got))
+    total = jnp.stack([low_sum(pair[0], got) for pair, got in pairs])
+    rest = swap(total, "dp", 1)
+    norm_one = main_mine[rows].astype(jnp.float32)
+    norm_one = norm_one + sum(swap(norm_one, "tensor", k) for k in range(1, tensor_count))
+    main_mine = main_mine[:rows]
+    main_other = swap(main_mine, "dp", 1)
+    first = dp_rank == 0
+    both = jnp.concatenate(
+        [jnp.where(first, total, rest), jnp.where(first, rest, total)], axis=2
+    ).astype(jnp.float32)
+    joined = jnp.concatenate(
+        [jnp.where(first, main_mine, main_other), jnp.where(first, main_other, main_mine)], axis=0
+    ).astype(jnp.float32)
     shared = joined[used + inner :]
-    norm_one = shared[-2]
-    norm_one = norm_one + sum(swap(norm_one, "tensor", k) for k in range(1, tensor_count))
+
+    grad_normed_one = sum(dot_tn(got, part) for got, part in zip(grad_got, joined_parts))
+    inv_own = inverse_rms(input_own)
+    input_grad = grad_residual + norm_backward(grad_normed_one, gain_one, input_own * inv_own, inv_own)
     return (
         output,
         input_grad,
@@ -679,7 +774,7 @@
         joined[inner : 2 * inner].T,
         joined[2 * inner : used].T,
         joined[used : used + inner],
-        shared[-1, :table_size].reshape(local_heads, NUM_BUCKETS).T,
+        shared[grad_wo.shape[0] - inner, :table_size].reshape(local_heads, NUM_BUCKETS).T,
         norm_one,
         shared[experts],
         shared[:experts].T,

time: 374 us -> 328 us (0.88)
  waiting for transfers between devices: 69 us -> 46.4 us
  matrix products: 38.2 us -> 15.9 us
  starting transfers between devices: 81.5 us -> 68.6 us
  local copies, waits for them, and re-layouts: 27.7 us -> 39.1 us
  Pallas kernels: 118 us -> 124 us
  other arithmetic: 30.7 us -> 26.1 us
    dot_general x9 -> x5, matrix products: 20.1 us -> 6.03 us  [dot_tn(): lax.dot_general(a, b, (((0,), (0,)), ((), ())), preferred_element_type=jn...]
    all_to_all x6, waiting for transfers between devices: 31.9 us -> 19 us  [trade(): return lax.all_to_all(array, axis, 0, 0, tiled=True)]
    ppermute x38 -> x42, waiting for transfers between devices: 37.1 us -> 27.5 us  [swap(): return lax.ppermute(array, axis, [(i, i ^ offset) for i in range(count)])]
    dot_general x4 -> x0, matrix products: 9.02 us -> none  [the longest x1 3.25 us: dot_nt(): lax.dot_general(a, b, (((1,), (1,)), ((), ())), preferred_element_type=jn...]
    unnamed x133 -> x128, local copies, waits for them, and re-layouts: 8.46 us -> 16.7 us
    all_to_all x6, starting transfers between devices: 32.4 us -> 25.3 us  [trade(): return lax.all_to_all(array, axis, 0, 0, tiled=True)]
    convert_element_type x8 -> x9, other arithmetic: 6.07 us -> 12.5 us  [the longest x4 10.4 us: low_sum(): sum((array.astype(jnp.float32) for array in arrays)).astype(jnp.bfloat16)]
    pallas_call x5 -> x6, Pallas kernels: 71.3 us -> 77.6 us  [the longest x3 44.5 us: expert_apply(): pl.pallas_call(functools.partial(expert_kernel, parts, pieces), grid=(par...]
  transfers between devices with their start and end apart: 44 -> 48, of which waited for: 12 -> 10; matrix products, arithmetic and copies ran while one was open for 21% -> 15% of each run, Pallas kernels for 26% -> 39%
where the time goes in v2:
time: 328 us; the launch traced here: 322 us
  Pallas kernels  124 us (38%)
  starting transfers between devices  68.6 us (21%)
  waiting for transfers between devices  46.4 us (14%)
  local copies, waits for them, and re-layouts  39.1 us (12%)
  other arithmetic  26.1 us (8%)
  matrix products  15.9 us (5%)
    pallas_call x3, Pallas kernels, expert_apply(): pl.pallas_call(functools.partial(expert_kernel, parts, pieces), grid=(par...  44.5 us
    ppermute x42, starting transfers between devices, swap(): return lax.ppermute(array, axis, [(i, i ^ offset) for i in range(count)])  43.3 us
    ppermute x42, waiting for transfers between devices, swap(): return lax.ppermute(array, axis, [(i, i ^ offset) for i in range(count)])  27.5 us
    all_to_all x6, starting transfers between devices, trade(): return lax.all_to_all(array, axis, 0, 0, tiled=True)  25.3 us
    pallas_call x1, Pallas kernels, attend_back(): pl.pallas_call(attend_back_kernel, grid=(heads, seqs), in_specs=[part(0),...  23.6 us
    pallas_call x1, Pallas kernels, expert_weights(): pl.pallas_call(functools.partial(weight_kernel, len(groups)), grid=(steps...  20.7 us
    all_to_all x6, waiting for transfers between devices, trade(): return lax.all_to_all(array, axis, 0, 0, tiled=True)  19 us
    unnamed x128, local copies, waits for them, and re-layouts  16.7 us
  transfers between devices with their start and end apart: 48, of which 10 were waited for; matrix products, arithmetic and copies ran while one was open for 15% of the time, Pallas kernels for 39%

profile of v2, /device:TPU:0, one launch (start us, length us, event | category | flops | bytes accessed | tf_op | source)
XLA Modules:
  0.0 321.9 jit_solution(14141756534513680308)
XLA Ops:
  3.2 2.9 collective-permute-start
  10.5 4.3 %all-to-all-start = ((bf16[4,192,768]{2,1,0:T(8,128)(2,1)}), bf16[4,192,768]{2,1,0:T(8,128)(2,1)}, u32[]{:S(2)}, u32[]{:S(2)}) async-start(bf16[4,192,768]{2,1,0:T(8,128)(2,1)} %broadcast_in_dim.24), calls=%async_computation | async-start | bytes 2359296 | tf_op jit(solution)/shard_map/all_to_all | solution.py:540
  24.9 6.6 %shard_map.229 = (bf16[576,2048]{1,0:T(8,128)(2,1)S(1)}, bf16[2048,768]{1,0:T(8,128)(2,1)}) custom-call(f32[2048,768]{1,0:T(8,128)} %x_ref.1, f32[1,768]{1,0:T(1,128)S(1)} %broadcast_in_dim.22.gain_ref, bf16[576,768]{1,0:T(8,128)(2,1)S(1)} %pad_maximum_fusion.2.weight_ref), custom_call_target="tpu_custom_call" | custom-call | flops 3623878656 | bytes 3538944 | tf_op jit(solution)/shard_map/pallas_call | solution.py:323
  31.6 2.8 collective-permute-start.5
  34.4 14.4 %shard_map.230 = (bf16[4,3,64,512]{3,2,1,0:T(8,128)(2,1)S(1)}, f32[3,2,1,1024]{3,2,1,0:T(1,128)S(1)}) custom-call(bf16[3,3,64,2048]{3,2,1,0:T(8,128)(2,1)S(1)} %bitcast.97, bf16[3,3,64,2048]{3,2,1,0:T(8,128)(2,1)S(1)} %bitcast.98, bf16[3,3,64,2048]{3,2,1,0:T(8,128)(2,1)S(1)} %bitcast.99, f32[3,1,2048]{2,1,0:T(1,128)S(1)} %broadcast_in_dim.23.vec_ref), custom_call_target="tpu_custom_call" | custom-call | flops 6442450944 | bytes 6291456 | tf_op jit(solution)/shard_map/pallas_call | solution.py:95
  51.1 3.2 collective-permute-start.6
  54.3 4.7 %all-to-all-start.1 = ((bf16[4,192,512]{2,1,0:T(8,128)(2,1)}), bf16[4,192,512]{2,1,0:T(8,128)(2,1)}, u32[]{:S(2)}, u32[]{:S(2)}) async-start(bf16[4,192,512]{2,1,0:T(8,128)(2,1)} %bitcast.94), calls=%async_computation.1 | async-start | bytes 1572864 | tf_op jit(solution)/shard_map/all_to_all | solution.py:540
  62.6 2.7 constant_dynamic-slice_fusion.1.rows_ref
  65.3 6.1 %all-to-all-done.1 = bf16[4,192,512]{2,1,0:T(8,128)(2,1)} async-done(((bf16[4,192,512]{2,1,0:T(8,128)(2,1)}), bf16[4,192,512]{2,1,0:T(8,128)(2,1)}, u32[]{:S(2)}, u32[]{:S(2)}) %all-to-all-start.1) | async-done | bytes 786464 | tf_op jit(solution)/shard_map/all_to_all | solution.py:540
  71.4 5.7 %shard_map.232 = (f32[512,768]{1,0:T(8,128)}, f32[4,512]{1,0:T(4,128)S(1)}, f32[1,512]{1,0:T(1,128)S(1)}, bf16[264,768]{1,0:T(8,128)(2,1)S(1)}, bf16[264,768]{1,...) custom-call(bf16[768,512]{1,0:T(8,128)(2,1)} %bitcast.10.mixed_ref, ...), custom_call_target="tpu_custom_call" | custom-call | flops 1811939328 | bytes 1769472 | tf_op jit(solution)/shard_map/pallas_call | solution.py:259
  77.8 4.5 %collective-permute-done.8.refs_10_.refs_8_ = bf16[768,384]{1,0:T(8,128)(2,1)} collective-permute-done((bf16[768,384]{1,0:T(8,128)(2,1)}, bf16[768,384]{1,0:T(8,128)(2,1)}, u32[]{:S(2)}, u32[]{:S(2)}) %collective-permute-start.8) | collective-permute-done | bytes 589856 | tf_op jit(solution)/shard_map/ppermute | solution.py:536
  82.8 3.6 %collective-permute-done.7.refs_1_ = bf16[264,768]{1,0:T(8,128)(2,1)S(1)} collective-permute-done((bf16[264,768]{1,0:T(8,128)(2,1)S(1)}, bf16[264,768]{1,0:T(8,128)(2,1)S(1)}, u32[]{:S(2)}, u32[]{:S(2)}) %collective-permute-start.7) | collective-permute-done | bytes 405536 | tf_op jit(solution)/shard_map/ppermute | solution.py:536
  91.2 20.5 %shard_map.233 = (bf16[8,512,384]{2,1,0:T(8,128)(2,1)}, bf16[8,512,384]{2,1,0:T(8,128)(2,1)}, bf16[768,512]{1,0:T(8,128)(2,1)}, bf16[768,512]{1,0:T(8,128)(2,1)}...) custom-call(bf16[264,768]{1,0:T(8,128)(2,1)} %copy-done.20, ...), custom_call_target="tpu_custom_call" | custom-call | flops 14495514624 | bytes 14155776 | tf_op jit(solution)/shard_map/pallas_call | solution.py:444
  113.3 3.2 %collective-permute-done.16.refs_0_ = bf16[264,768]{1,0:T(8,128)(2,1)} collective-permute-done((bf16[264,768]{1,0:T(8,128)(2,1)S(1)}, bf16[264,768]{1,0:T(8,128)(2,1)}, u32[]{:S(2)}, u32[]{:S(2)}) %collective-permute-start.16) | collective-permute-done | bytes 405536 | tf_op jit(solution)/shard_map/ppermute | solution.py:536
  118.6 11.8 %shard_map.234 = (bf16[8,256,384]{2,1,0:T(8,128)(2,1)}, bf16[8,256,384]{2,1,0:T(8,128)(2,1)}, bf16[768,256]{1,0:T(8,128)(2,1)S(1)}, bf16[768,256]{1,0:T(8,128)(2...) custom-call(bf16[264,768]{1,0:T(8,128)(2,1)} %collective-permute-done.16.refs_0_, ...), custom_call_target="tpu_custom_call" | custom-call | flops 7247757312 | bytes 7077888 | tf_op jit(solution)/shard_map/pallas_call | solution.py:444
  130.5 12.2 %shard_map.235 = (bf16[8,256,384]{2,1,0:T(8,128)(2,1)}, bf16[8,256,384]{2,1,0:T(8,128)(2,1)}, bf16[768,256]{1,0:T(8,128)(2,1)S(1)}, bf16[768,256]{1,0:T(8,128)(2...) custom-call(bf16[264,768]{1,0:T(8,128)(2,1)} %collective-permute-done.19.refs_0_, ...), custom_call_target="tpu_custom_call" | custom-call | flops 7247757312 | bytes 7077888 | tf_op jit(solution)/shard_map/pallas_call | solution.py:444
  144.3 20.7 %shard_map.236 = (bf16[4,768,384]{2,1,0:T(8,128)(2,1)}, bf16[4,768,384]{2,1,0:T(8,128)(2,1)}, bf16[4,768,384]{2,1,0:T(8,128)(2,1)}, bf16[4,768,384]{2,1,0:T(8,128)(2,1)}) custom-call(bf16[8,512,384]{2,1,0:T(8,128)(2,1)} %get-tuple-element.234.refs_0_, bf16[8,512,384]{2,1,0:T(8,128)(2,1)} %get-tuple-element.235.refs_1_, bf16[768,512]{1,0:T(8,128)(2,1)S(1)} %copy-done.23, ...), custom_call_target="tpu_custom_call" | custom-call | flops 14495514624 | bytes 14155776 | tf_op jit(solution)/shard_map/pallas_call | solution.py:514
  165.6 6.8 %shard_map.237 = (f32[512,768]{1,0:T(8,128)}, bf16[512,768]{1,0:T(8,128)(2,1)S(1)}, bf16[768,512]{1,0:T(8,128)(2,1)S(1)}, f32[4,768]{1,0:T(4,128)S(1)}, f32[1,768]{1,0:T(1,128)S(1)}) custom-call(f32[512,768]{1,0:T(8,128)} %get-tuple-element.168.residual_ref, bf16[512,768]{1,0:T(8,128)(2,1)S(1)} %copy-done.3, f32[1,768]{1,0:T(1,128)S(1)} %reshape.146.gain_ref, ...), custom_call_target="tpu_custom_call" | custom-call | flops 1811939328 | bytes 1769472 | tf_op jit(solution)/shard_map/pallas_call | solution.py:298
  174.2 3.6 %all-to-all-start.2 = ((bf16[4,192,512]{2,1,0:T(8,128)(2,1)}), bf16[4,192,512]{2,1,0:T(8,128)(2,1)S(1)}, u32[]{:S(2)}, u32[]{:S(2)}) async-start(bf16[4,192,512]{2,1,0:T(8,128)(2,1)} %bitcast.96), calls=%async_computation.2 | async-start | bytes 1572864 | tf_op jit(solution)/shard_map/all_to_all | solution.py:540
  185.4 3.8 %all-to-all-done.2 = bf16[4,192,512]{2,1,0:T(8,128)(2,1)S(1)} async-done(((bf16[4,192,512]{2,1,0:T(8,128)(2,1)}), bf16[4,192,512]{2,1,0:T(8,128)(2,1)S(1)}, u32[]{:S(2)}, u32[]{:S(2)}) %all-to-all-start.2) | async-done | bytes 786464 | tf_op jit(solution)/shard_map/all_to_all | solution.py:540
  189.1 4.5 %all-to-all-start.3 = ((bf16[4,200,768]{2,1,0:T(8,128)(2,1)}), bf16[4,200,768]{2,1,0:T(8,128)(2,1)}, u32[]{:S(2)}, u32[]{:S(2)}) async-start(bf16[4,200,768]{2,1,0:T(8,128)(2,1)} %pad_maximum_fusion), calls=%async_computation.3 | async-start | bytes 2457600 | tf_op jit(solution)/shard_map/all_to_all | solution.py:540
  193.7 3.1 add_convert_fusion.3
  198.8 2.7 add_convert_fusion.2
  202.9 23.6 %shard_map.238 = (bf16[4,3,3,64,512]{4,3,2,1,0:T(8,128)(2,1)S(1)}, f32[3,1,2048]{2,1,0:T(1,128)S(1)}) custom-call(bf16[3,3,64,2048]{3,2,1,0:T(8,128)(2,1)} %bitcast.100, bf16[3,3,64,2048]{3,2,1,0:T(8,128)(2,1)} %bitcast.101, bf16[3,3,64,2048]{3,2,1,0:T(8,128)(2,1)} %bitcast.102, bf16[4,3,64,512]{3,2,1,0:T(8,128)(2,1)S(1)} %copy-done.7, ...), custom_call_target="tpu_custom_call" | custom-call | flops 12884901888 | bytes 12582912 | tf_op jit(solution)/shard_map/pallas_call | solution.py:171
  226.8 7.5 %collective-permute-done.26 = bf16[2,768,384]{2,1,0:T(8,128)(2,1)} collective-permute-done((bf16[2,768,384]{2,1,0:T(8,128)(2,1)}, bf16[2,768,384]{2,1,0:T(8,128)(2,1)}, u32[]{:S(2)}, u32[]{:S(2)}) %collective-permute-start.26) | collective-permute-done | bytes 1179680 | tf_op jit(solution)/shard_map/ppermute | solution.py:536
  234.3 4.1 %multiply_reduce_fusion = (f32[768]{0:T(1024)S(1)}, f32[576,768]{1,0:T(8,128)S(1)}) fusion(bf16[192,768]{1,0:T(8,128)(2,1)} %bitcast.104, bf16[192,768]{1,0:T(8,128)(2,1)} %bitcast.107, bf16[192,768]{1,0:T(8,128)(2,1)} %bitcast.109, bf16[4,576,512]{2,1,0:T(8,128)(2,1)S(1)} %bitcast.92, bf16[4,512,768]{2,1,0:T(8,128)(2,1)} %bitcast.118), kind=kOutput, calls=%fused_computation.11 | convolution fusion | flops 1815477504 | bytes 8162304 | tf_op jit(solution)/shard_map/bcn,bnd->cd/dot_general | solution.py:713
  249.7 3.8 %all-to-all-start.4 = ((bf16[4,100,768]{2,1,0:T(8,128)(2,1)}), bf16[4,100,768]{2,1,0:T(8,128)(2,1)S(1)}, u32[]{:S(2)}, u32[]{:S(2)}) async-start(bf16[4,100,768]{2,1,0:T(8,128)(2,1)} %reshape.144), calls=%async_computation.4 | async-start | bytes 1277952 | tf_op jit(solution)/shard_map/all_to_all | solution.py:540
  263.4 3.4 %multiply_add_fusion.1 = f32[512,768]{1,0:T(8,128)} fusion(f32[512,768]{1,0:T(8,128)S(1)} %copy-done.40, bf16[512,1024]{1,0:T(8,128)(2,1)S(1)} %copy-done.5, bf16[256,768]{1,0:T(8,128)(2,1)} %collective-permute-done.30, bf16[256,768]{1,0:T(8,128)(2,1)} %collective-permute-done.29, bf16[256,768]{1,0:T(8,128)(2,1)} %collective-permute-done.28, ...), kind=kOutput, calls=%fused_computation.24 | convolution fusion | flops 812384256 | bytes 5769216 | tf_op jit(solution)/shard_map/dot_general | solution.py:27
  266.8 7.8 %collective-permute-done.33 = bf16[576,512]{1,0:T(8,128)(2,1)} collective-permute-done((bf16[576,512]{1,0:T(8,128)(2,1)}, bf16[576,512]{1,0:T(8,128)(2,1)}, u32[]{:S(2)}, u32[]{:S(2)}) %collective-permute-start.33) | collective-permute-done | bytes 589856 | tf_op jit(solution)/shard_map/ppermute | solution.py:536
  275.5 4.4 %all-to-all-start.5 = ((bf16[4,100,768]{2,1,0:T(8,128)(2,1)}), bf16[4,100,768]{2,1,0:T(8,128)(2,1)}, u32[]{:S(2)}, u32[]{:S(2)}) async-start(bf16[4,100,768]{2,1,0:T(8,128)(2,1)} %broadcast_in_dim.61), calls=%async_computation.5 | async-start | bytes 1277952 | tf_op jit(solution)/shard_map/all_to_all | solution.py:540
  287.0 9.1 %all-to-all-done.5 = bf16[4,100,768]{2,1,0:T(8,128)(2,1)} async-done(((bf16[4,100,768]{2,1,0:T(8,128)(2,1)}), bf16[4,100,768]{2,1,0:T(8,128)(2,1)}, u32[]{:S(2)}, u32[]{:S(2)}) %all-to-all-start.5) | async-done | bytes 614432 | tf_op jit(solution)/shard_map/all_to_all | solution.py:540
  318.4 3.2 copy.30
  (279 shorter events, 99.0 us)
Async XLA Ops:
  3.2 51.1 %collective-permute-start = (bf16[768,384]{1,0:T(8,128)(2,1)}, bf16[768,384]{1,0:T(8,128)(2,1)}, u32[]{:S(2)}, u32[]{:S(2)}) collective-permute-start(bf16[768,384]{1,0:T(8,128)(2,1)} %get-tuple-element.190.refs_4_.refs_2_), channel_id=1, source_target_pairs={{0,1},{1,0},{2,3},{3,2},{4,5},{5,4},{6,7},{7,6},{8,9},{9,8},{10,11... | collective-permute-start | bytes 1769480 | tf_op jit(solution)/shard_map/ppermute | solution.py:536
  6.2 48.1 %collective-permute-start.2 = (bf16[768,384]{1,0:T(8,128)(2,1)}, bf16[768,384]{1,0:T(8,128)(2,1)}, u32[]{:S(2)}, u32[]{:S(2)}) collective-permute-start(bf16[768,384]{1,0:T(8,128)(2,1)} %get-tuple-element.190.refs_4_.refs_2_), channel_id=1, source_target_pairs={{0,2},{1,3},{2,0},{3,1},{4,6},{5,7},{6,4},{7,5},{8,10},{9,11},{10,... | collective-permute-start | bytes 1769480 | tf_op jit(solution)/shard_map/ppermute | solution.py:536
  8.9 45.4 %collective-permute-start.1 = (bf16[384,768]{1,0:T(8,128)(2,1)}, bf16[384,768]{1,0:T(8,128)(2,1)}, u32[]{:S(2)}, u32[]{:S(2)}) collective-permute-start(bf16[384,768]{1,0:T(8,128)(2,1)} %get-tuple-element.198.refs_12_.refs_10_), channel_id=1, source_target_pairs={{0,2},{1,3},{2,0},{3,1},{4,6},{5,7},{6,4},{7,5},{8,10},{9,11},{10,... | collective-permute-start | bytes 1769480 | tf_op jit(solution)/shard_map/ppermute | solution.py:536
  9.4 44.9 %collective-permute-start.3 = (bf16[384,768]{1,0:T(8,128)(2,1)}, bf16[384,768]{1,0:T(8,128)(2,1)}, u32[]{:S(2)}, u32[]{:S(2)}) collective-permute-start(bf16[384,768]{1,0:T(8,128)(2,1)} %get-tuple-element.198.refs_12_.refs_10_), channel_id=1, source_target_pairs={{0,1},{1,0},{2,3},{3,2},{4,5},{5,4},{6,7},{7,6},{8,9},{9,8},{10,11... | collective-permute-start | bytes 1769480 | tf_op jit(solution)/shard_map/ppermute | solution.py:536
  10.5 43.8 %all-to-all-start = ((bf16[4,192,768]{2,1,0:T(8,128)(2,1)}), bf16[4,192,768]{2,1,0:T(8,128)(2,1)}, u32[]{:S(2)}, u32[]{:S(2)}) async-start(bf16[4,192,768]{2,1,0:T(8,128)(2,1)} %broadcast_in_dim.24), calls=%async_computation | async-start | bytes 2359296 | tf_op jit(solution)/shard_map/all_to_all | solution.py:540
  51.1 26.7 %collective-permute-start.6 = (bf16[256,768]{1,0:T(8,128)(2,1)}, bf16[256,768]{1,0:T(8,128)(2,1)}, u32[]{:S(2)}, u32[]{:S(2)}) collective-permute-start(bf16[256,768]{1,0:T(8,128)(2,1)} %get-tuple-element.176), channel_id=1, source_target_pairs={{0,12},{4,8},{8,4},{12,0},{1,13},{5,9},{9,5},{13,1},{2,14},{6,10},... | collective-permute-start | bytes 1179656 | tf_op jit(solution)/shard_map/ppermute | solution.py:536
  59.1 23.2 %collective-permute-start.8 = (bf16[768,384]{1,0:T(8,128)(2,1)}, bf16[768,384]{1,0:T(8,128)(2,1)}, u32[]{:S(2)}, u32[]{:S(2)}) collective-permute-start(bf16[768,384]{1,0:T(8,128)(2,1)} %collective-permute-done.refs_6_.refs_4_), channel_id=1, source_target_pairs={{0,2},{1,3},{2,0},{3,1},{4,6},{5,7},{6,4},{7,5},{8,10},{9,11},{10,... | collective-permute-start | bytes 1769480 | tf_op jit(solution)/shard_map/ppermute | solution.py:536
  61.2 25.3 %collective-permute-start.10 = (bf16[768,384]{1,0:T(8,128)(2,1)}, bf16[768,384]{1,0:T(8,128)(2,1)}, u32[]{:S(2)}, u32[]{:S(2)}) collective-permute-start(bf16[768,384]{1,0:T(8,128)(2,1)} %collective-permute-done.refs_6_.refs_4_), channel_id=1, source_target_pairs={{0,16},{16,0},{1,17},{17,1},{2,18},{18,2},{3,19},{19,3},{4,20},{20... | collective-permute-start | bytes 1769480 | tf_op jit(solution)/shard_map/ppermute | solution.py:536
  61.2 21.2 %collective-permute-start.9 = (bf16[384,768]{1,0:T(8,128)(2,1)}, bf16[384,768]{1,0:T(8,128)(2,1)}, u32[]{:S(2)}, u32[]{:S(2)}) collective-permute-start(bf16[384,768]{1,0:T(8,128)(2,1)} %collective-permute-done.1.refs_16_.refs_14_), channel_id=1, source_target_pairs={{0,1},{1,0},{2,3},{3,2},{4,5},{5,4},{6,7},{7,6},{8,9},{9,8},{10,11... | collective-permute-start | bytes 1769480 | tf_op jit(solution)/shard_map/ppermute | solution.py:536
  87.0 29.6 %collective-permute-start.16 = (bf16[264,768]{1,0:T(8,128)(2,1)S(1)}, bf16[264,768]{1,0:T(8,128)(2,1)}, u32[]{:S(2)}, u32[]{:S(2)}) collective-permute-start(bf16[264,768]{1,0:T(8,128)(2,1)S(1)} %get-tuple-element.212), channel_id=1, source_target_pairs={{0,8},{4,12},{8,0},{12,4},{1,9},{5,13},{9,1},{13,5},{2,10},{6,14},... | collective-permute-start | bytes 1216520 | tf_op jit(solution)/shard_map/ppermute | solution.py:536
  87.0 43.4 %collective-permute-start.19 = (bf16[264,768]{1,0:T(8,128)(2,1)S(1)}, bf16[264,768]{1,0:T(8,128)(2,1)}, u32[]{:S(2)}, u32[]{:S(2)}) collective-permute-start(bf16[264,768]{1,0:T(8,128)(2,1)S(1)} %get-tuple-element.223), channel_id=1, source_target_pairs={{0,12},{4,8},{8,4},{12,0},{1,13},{5,9},{9,5},{13,1},{2,14},{6,10},... | collective-permute-start | bytes 1216520 | tf_op jit(solution)/shard_map/ppermute | solution.py:536
  89.7 26.9 %collective-permute-start.17 = (bf16[576,768]{1,0:T(8,128)(2,1)S(1)}, bf16[576,768]{1,0:T(8,128)(2,1)S(1)}, u32[]{:S(2)}, u32[]{:S(2)}) collective-permute-start(bf16[576,768]{1,0:T(8,128)(2,1)S(1)} %pad_maximum_fusion.2.weight_ref), channel_id=1, source_target_pairs={{0,1},{1,0},{2,3},{3,2},{4,5},{5,4},{6,7},{7,6},{8,9},{9,8},{10,11... | collective-permute-start | bytes 2654216 | tf_op jit(solution)/shard_map/ppermute | solution.py:536
  90.5 26.0 %collective-permute-start.18 = (bf16[576,768]{1,0:T(8,128)(2,1)S(1)}, bf16[576,768]{1,0:T(8,128)(2,1)S(1)}, u32[]{:S(2)}, u32[]{:S(2)}) collective-permute-start(bf16[576,768]{1,0:T(8,128)(2,1)S(1)} %pad_maximum_fusion.2.weight_ref), channel_id=1, source_target_pairs={{0,2},{1,3},{2,0},{3,1},{4,6},{5,7},{6,4},{7,5},{8,10},{9,11},{10,... | collective-permute-start | bytes 2654216 | tf_op jit(solution)/shard_map/ppermute | solution.py:536
  112.5 52.5 %collective-permute-start.21 = (bf16[264,768]{1,0:T(8,128)(2,1)}, bf16[264,768]{1,0:T(8,128)(2,1)S(1)}, u32[]{:S(2)}, u32[]{:S(2)}) collective-permute-start(bf16[264,768]{1,0:T(8,128)(2,1)} %get-tuple-element.251), channel_id=1, source_target_pairs={{0,4},{4,0},{8,12},{12,8},{1,5},{5,1},{9,13},{13,9},{2,6},{6,2},{1... | collective-permute-start | bytes 1216520 | tf_op jit(solution)/shard_map/ppermute | solution.py:536
  117.8 26.5 %collective-permute-start.20 = (bf16[576,768]{1,0:T(8,128)(2,1)S(1)}, bf16[576,768]{1,0:T(8,128)(2,1)S(1)}, u32[]{:S(2)}, u32[]{:S(2)}) collective-permute-start(bf16[576,768]{1,0:T(8,128)(2,1)S(1)} %pad_maximum_fusion.2.weight_ref), channel_id=1, source_target_pairs={{0,3},{1,2},{2,1},{3,0},{4,7},{5,6},{6,5},{7,4},{8,11},{9,10},{10,... | collective-permute-start | bytes 2654216 | tf_op jit(solution)/shard_map/ppermute | solution.py:536
  130.5 34.6 %collective-permute-start.22 = (bf16[264,768]{1,0:T(8,128)(2,1)S(1)}, bf16[264,768]{1,0:T(8,128)(2,1)S(1)}, u32[]{:S(2)}, u32[]{:S(2)}) collective-permute-start(bf16[264,768]{1,0:T(8,128)(2,1)S(1)} %get-tuple-element.252), channel_id=1, source_target_pairs={{0,8},{4,12},{8,0},{12,4},{1,9},{5,13},{9,1},{13,5},{2,10},{6,14},... | collective-permute-start | bytes 1216520 | tf_op jit(solution)/shard_map/ppermute | solution.py:536
  142.8 22.2 %collective-permute-start.23 = (bf16[264,768]{1,0:T(8,128)(2,1)S(1)}, bf16[264,768]{1,0:T(8,128)(2,1)S(1)}, u32[]{:S(2)}, u32[]{:S(2)}) collective-permute-start(bf16[264,768]{1,0:T(8,128)(2,1)S(1)} %get-tuple-element.253), channel_id=1, source_target_pairs={{0,12},{4,8},{8,4},{12,0},{1,13},{5,9},{9,5},{13,1},{2,14},{6,10},... | collective-permute-start | bytes 1216520 | tf_op jit(solution)/shard_map/ppermute | solution.py:536
  165.0 28.6 %collective-permute-start.24 = (bf16[4,768,384]{2,1,0:T(8,128)(2,1)}, bf16[4,768,384]{2,1,0:T(8,128)(2,1)}, u32[]{:S(2)}, u32[]{:S(2)}) collective-permute-start(bf16[4,768,384]{2,1,0:T(8,128)(2,1)} %get-tuple-element.259), channel_id=1, source_target_pairs={{0,16},{16,0},{1,17},{17,1},{2,18},{18,2},{3,19},{19,3},{4,20},{20... | collective-permute-start | bytes 7077896 | tf_op jit(solution)/shard_map/ppermute | solution.py:536
  165.1 28.6 %collective-permute-start.25 = (bf16[4,768,384]{2,1,0:T(8,128)(2,1)}, bf16[4,768,384]{2,1,0:T(8,128)(2,1)}, u32[]{:S(2)}, u32[]{:S(2)}) collective-permute-start(bf16[4,768,384]{2,1,0:T(8,128)(2,1)} %get-tuple-element.260), channel_id=1, source_target_pairs={{0,16},{16,0},{1,17},{17,1},{2,18},{18,2},{3,19},{19,3},{4,20},{20... | collective-permute-start | bytes 7077896 | tf_op jit(solution)/shard_map/ppermute | solution.py:536
  177.8 49.0 %collective-permute-start.28 = (bf16[256,768]{1,0:T(8,128)(2,1)}, bf16[256,768]{1,0:T(8,128)(2,1)}, u32[]{:S(2)}, u32[]{:S(2)}) collective-permute-start(bf16[256,768]{1,0:T(8,128)(2,1)} %get-tuple-element.274), channel_id=1, source_target_pairs={{0,4},{4,0},{8,12},{12,8},{1,5},{5,1},{9,13},{13,9},{2,6},{6,2},{1... | collective-permute-start | bytes 1179656 | tf_op jit(solution)/shard_map/ppermute | solution.py:536
  179.7 47.1 %collective-permute-start.29 = (bf16[256,768]{1,0:T(8,128)(2,1)}, bf16[256,768]{1,0:T(8,128)(2,1)}, u32[]{:S(2)}, u32[]{:S(2)}) collective-permute-start(bf16[256,768]{1,0:T(8,128)(2,1)} %get-tuple-element.275), channel_id=1, source_target_pairs={{0,8},{4,12},{8,0},{12,4},{1,9},{5,13},{9,1},{13,5},{2,10},{6,14},... | collective-permute-start | bytes 1179656 | tf_op jit(solution)/shard_map/ppermute | solution.py:536
  180.8 46.0 %collective-permute-start.30 = (bf16[256,768]{1,0:T(8,128)(2,1)}, bf16[256,768]{1,0:T(8,128)(2,1)}, u32[]{:S(2)}, u32[]{:S(2)}) collective-permute-start(bf16[256,768]{1,0:T(8,128)(2,1)} %get-tuple-element.276), channel_id=1, source_target_pairs={{0,12},{4,8},{8,4},{12,0},{1,13},{5,9},{9,5},{13,1},{2,14},{6,10},... | collective-permute-start | bytes 1179656 | tf_op jit(solution)/shard_map/ppermute | solution.py:536
  189.1 37.7 %all-to-all-start.3 = ((bf16[4,200,768]{2,1,0:T(8,128)(2,1)}), bf16[4,200,768]{2,1,0:T(8,128)(2,1)}, u32[]{:S(2)}, u32[]{:S(2)}) async-start(bf16[4,200,768]{2,1,0:T(8,128)(2,1)} %pad_maximum_fusion), calls=%async_computation.3 | async-start | bytes 2457600 | tf_op jit(solution)/shard_map/all_to_all | solution.py:540
  196.8 37.6 %collective-permute-start.26 = (bf16[2,768,384]{2,1,0:T(8,128)(2,1)}, bf16[2,768,384]{2,1,0:T(8,128)(2,1)}, u32[]{:S(2)}, u32[]{:S(2)}) collective-permute-start(bf16[2,768,384]{2,1,0:T(8,128)(2,1)} %add_convert_fusion.3), channel_id=1, source_target_pairs={{0,1},{1,0},{2,3},{3,2},{4,5},{5,4},{6,7},{7,6},{8,9},{9,8},{10,11... | collective-permute-start | bytes 3538952 | tf_op jit(solution)/shard_map/ppermute | solution.py:536
  201.4 32.9 %collective-permute-start.27 = (bf16[2,768,384]{2,1,0:T(8,128)(2,1)}, bf16[2,768,384]{2,1,0:T(8,128)(2,1)}, u32[]{:S(2)}, u32[]{:S(2)}) collective-permute-start(bf16[2,768,384]{2,1,0:T(8,128)(2,1)} %add_convert_fusion.2), channel_id=1, source_target_pairs={{0,2},{1,3},{2,0},{3,1},{4,6},{5,7},{6,4},{7,5},{8,10},{9,11},{10,... | collective-permute-start | bytes 3538952 | tf_op jit(solution)/shard_map/ppermute | solution.py:536
  244.0 22.8 %collective-permute-start.32 = (bf16[576,512]{1,0:T(8,128)(2,1)}, bf16[576,512]{1,0:T(8,128)(2,1)S(1)}, u32[]{:S(2)}, u32[]{:S(2)}) collective-permute-start(bf16[576,512]{1,0:T(8,128)(2,1)} %get-tuple-element.346), channel_id=1, source_target_pairs={{0,1},{1,0},{2,3},{3,2},{4,5},{5,4},{6,7},{7,6},{8,9},{9,8},{10,11... | collective-permute-start | bytes 1769480 | tf_op jit(solution)/shard_map/ppermute | solution.py:536
  245.4 29.1 %collective-permute-start.33 = (bf16[576,512]{1,0:T(8,128)(2,1)}, bf16[576,512]{1,0:T(8,128)(2,1)}, u32[]{:S(2)}, u32[]{:S(2)}) collective-permute-start(bf16[576,512]{1,0:T(8,128)(2,1)} %get-tuple-element.345), channel_id=1, source_target_pairs={{0,2},{1,3},{2,0},{3,1},{4,6},{5,7},{6,4},{7,5},{8,10},{9,11},{10,... | collective-permute-start | bytes 1769480 | tf_op jit(solution)/shard_map/ppermute | solution.py:536
  246.0 28.5 %collective-permute-start.34 = (bf16[576,512]{1,0:T(8,128)(2,1)}, bf16[576,512]{1,0:T(8,128)(2,1)}, u32[]{:S(2)}, u32[]{:S(2)}) collective-permute-start(bf16[576,512]{1,0:T(8,128)(2,1)} %get-tuple-element.344), channel_id=1, source_target_pairs={{0,3},{1,2},{2,1},{3,0},{4,7},{5,6},{6,5},{7,4},{8,11},{9,10},{10,... | collective-permute-start | bytes 1769480 | tf_op jit(solution)/shard_map/ppermute | solution.py:536
  249.7 24.8 %all-to-all-start.4 = ((bf16[4,100,768]{2,1,0:T(8,128)(2,1)}), bf16[4,100,768]{2,1,0:T(8,128)(2,1)S(1)}, u32[]{:S(2)}, u32[]{:S(2)}) async-start(bf16[4,100,768]{2,1,0:T(8,128)(2,1)} %reshape.144), calls=%async_computation.4 | async-start | bytes 1277952 | tf_op jit(solution)/shard_map/all_to_all | solution.py:540
  258.0 40.3 %collective-permute-start.35 = (bf16[768,384]{1,0:T(8,128)(2,1)}, bf16[768,384]{1,0:T(8,128)(2,1)}, u32[]{:S(2)}, u32[]{:S(2)}) collective-permute-start(bf16[768,384]{1,0:T(8,128)(2,1)} %slice_bitcast_fusion.7), channel_id=1, source_target_pairs={{0,2},{1,3},{2,0},{3,1},{4,6},{5,7},{6,4},{7,5},{8,10},{9,11},{10,... | collective-permute-start | bytes 1769480 | tf_op jit(solution)/shard_map/ppermute | solution.py:536
  262.5 35.7 %collective-permute-start.36 = (bf16[768,384]{1,0:T(8,128)(2,1)}, bf16[768,384]{1,0:T(8,128)(2,1)}, u32[]{:S(2)}, u32[]{:S(2)}) collective-permute-start(bf16[768,384]{1,0:T(8,128)(2,1)} %slice_bitcast_fusion.6), channel_id=1, source_target_pairs={{0,1},{1,0},{2,3},{3,2},{4,5},{5,4},{6,7},{7,6},{8,9},{9,8},{10,11... | collective-permute-start | bytes 1769480 | tf_op jit(solution)/shard_map/ppermute | solution.py:536
  275.5 20.7 %all-to-all-start.5 = ((bf16[4,100,768]{2,1,0:T(8,128)(2,1)}), bf16[4,100,768]{2,1,0:T(8,128)(2,1)}, u32[]{:S(2)}, u32[]{:S(2)}) async-start(bf16[4,100,768]{2,1,0:T(8,128)(2,1)} %broadcast_in_dim.61), calls=%async_computation.5 | async-start | bytes 1277952 | tf_op jit(solution)/shard_map/all_to_all | solution.py:540
  (78 other events, 624.4 us)

commit v3 on v2

--- a/solution.py
+++ b/solution.py
@@ -522,6 +522,104 @@
     )(*arrays)
 
 
+def joined_kernel(rank_ref, grads_ref, normed_ref, weight_ref, gain_ref, wo_ref, table_ref, mine_ref, other_ref, main):
+    blocks, columns, own = grads_ref.shape
+    half = main.shape[0] // 2
+    extra = mine_ref.shape[0] - half
+    joined = 0.0
+    for b in range(blocks):
+        joined = joined + dot_nn(grads_ref[b], normed_ref[b * own : (b + 1) * own, :])
+    main[:columns, :] = joined
+    norm = jnp.sum(joined * weight_ref[...].astype(jnp.float32), axis=0, keepdims=True) / gain_ref[...]
+    output = 0.0
+    for b in range(blocks):
+        output = output + wo_ref[b].astype(jnp.float32)
+    end = columns + wo_ref.shape[1]
+    main[columns:end, :] = output
+    index = lax.broadcasted_iota(jnp.int32, (main.shape[0] - end, main.shape[1]), 0)
+    main[end:, :] = jnp.where(index == 0, table_ref[...], 0.0)
+    rank = rank_ref[0]
+    index = lax.broadcasted_iota(jnp.int32, (extra, main.shape[1]), 0)
+    norm = jnp.where(index == 0, norm, 0.0)
+    mine_ref[:half, :] = main[pl.ds(pl.multiple_of(rank * half, 8), half), :]
+    mine_ref[half:, :] = norm
+    other = main[pl.ds(pl.multiple_of((1 - rank) * half, 8), half), :]
+    other_ref[:half, :] = other.astype(jnp.bfloat16)
+    other_ref[half:, :] = norm.astype(jnp.bfloat16)
+
+
+def joined_halves(rank, grads, normed, weight, gain, wo, table, experts):
+    width = normed.shape[1]
+    rows = grads.shape[1] + wo.shape[1] + 1
+    half = (rows + 31) // 32 * 16
+    unit = max(16, experts)
+    total = (half + unit) // unit * unit
+    vmem = pl.BlockSpec(memory_space=pltpu.VMEM)
+    return half, pl.pallas_call(
+        joined_kernel,
+        in_specs=[pl.BlockSpec(memory_space=pltpu.SMEM)] + [vmem] * 6,
+        out_shape=[
+            jax.ShapeDtypeStruct((total, width), jnp.float32),
+            jax.ShapeDtypeStruct((total, width), jnp.bfloat16),
+        ],
+        scratch_shapes=[pltpu.VMEM((2 * half, width), jnp.float32)],
+        compiler_params=pltpu.CompilerParams(vmem_limit_bytes=48 * 2**20),
+        cost_estimate=cost(4 * rows * width * normed.shape[0]),
+    )(rank, grads, normed, weight, gain, wo, table)
+
+
+def halves_kernel(rank_ref, mine_ref, other_ref, query_ref, key_ref, value_ref, output_ref, rest_ref, main):
+    half = main.shape[0] // 2
+    rank = rank_ref[0]
+    main[pl.ds(pl.multiple_of(rank * half, 8), half), :] = mine_ref[:half, :].astype(jnp.float32)
+    main[pl.ds(pl.multiple_of((1 - rank) * half, 8), half), :] = other_ref[:half, :].astype(jnp.float32)
+    start = 0
+    for ref in (query_ref, key_ref, value_ref, output_ref, rest_ref):
+        ref[...] = main[start : start + ref.shape[0], :]
+        start += ref.shape[0]
+
+
+def joined_whole(rank, mine, other, half, inner):
+    width = mine.shape[1]
+    vmem = pl.BlockSpec(memory_space=pltpu.VMEM)
+    part = jax.ShapeDtypeStruct((inner, width), jnp.float32)
+    return pl.pallas_call(
+        halves_kernel,
+        in_specs=[pl.BlockSpec(memory_space=pltpu.SMEM), vmem, vmem],
+        out_shape=[part] * 4 + [jax.ShapeDtypeStruct((2 * half - 4 * inner, width), jnp.float32)],
+        scratch_shapes=[pltpu.VMEM((2 * half, width), jnp.float32)],
+        compiler_params=pltpu.CompilerParams(vmem_limit_bytes=48 * 2**20),
+        cost_estimate=cost(1000 * half * width),
+    )(rank, mine, other)
+
+
+def both_kernel(rank_ref, mine_ref, other_ref, first_ref, second_ref):
+    half = mine_ref.shape[2]
+    rank = rank_ref[0]
+    for place in range(2):
+
+        @pl.when(rank == place)
+        def _(place=place):
+            for ref, at in ((mine_ref, place * half), (other_ref, (1 - place) * half)):
+                first_ref[0, :, at : at + half] = ref[0].astype(jnp.float32)
+                second_ref[0, at : at + half, :] = ref[1].astype(jnp.float32).T
+
+
+def both_halves(rank, mine, other):
+    _, width, half = mine.shape
+    vmem = pl.BlockSpec(memory_space=pltpu.VMEM)
+    return pl.pallas_call(
+        both_kernel,
+        in_specs=[pl.BlockSpec(memory_space=pltpu.SMEM), vmem, vmem],
+        out_shape=[
+            jax.ShapeDtypeStruct((1, width, 2 * half), jnp.float32),
+            jax.ShapeDtypeStruct((1, 2 * half, width), jnp.float32),
+        ],
+        compiler_params=pltpu.CompilerParams(vmem_limit_bytes=48 * 2**20),
+        cost_estimate=cost(1000 * half * width),
+    )(rank, mine, other)
+
+
 def inverse_rms(rows):
     return lax.rsqrt(jnp.mean(rows * rows, axis=-1, keepdims=True) + EPSILON)
 
@@ -709,29 +807,21 @@
         sent = lax.dynamic_index_in_dim(grad_projected, tensor_rank ^ k, 0, keepdims=False)
         grad_got.append(swap(sent, "tensor", k))
 
-    grad_wo = jnp.sum(grad_wo.astype(jnp.float32), axis=0)
-    grad_joined = jnp.einsum(
-        "bcn,bnd->cd",
-        grad_projected,
-        normed_one.reshape(tensor_count, own_rows, width),
-        preferred_element_type=jnp.float32,
-    )
-    norm_one = jnp.sum(grad_joined * w_joined.astype(jnp.float32), axis=0) / gain_one
+    rank = dp_rank.reshape(1).astype(jnp.int32)
     grad_table = jnp.einsum(
         "br,hr->hb", bucket_hot.astype(jnp.float32), diagonals[:, 0], precision=HIGHEST
     ).reshape(-1)
     table_size = grad_table.shape[0]
-    used = 3 * inner
-    main = jnp.concatenate(
-        [grad_joined, grad_wo, jnp.pad(grad_table, (0, width - table_size))[None]], axis=0
-    )
-    main = jnp.pad(main, ((0, -main.shape[0] % 16), (0, 0)))
-    rows = main.shape[0] // 2
-    main_mine = lax.dynamic_slice_in_dim(main, dp_rank * rows, rows, 0)
-    main_other = lax.dynamic_slice_in_dim(main, (1 - dp_rank) * rows, rows, 0)
-    extra = jnp.pad(norm_one[None], ((0, (-rows - 1) % max(8, experts)), (0, 0)))
-    main_mine = jnp.concatenate([main_mine, extra], axis=0)
-    main_other = jnp.concatenate([main_other, extra], axis=0).astype(jnp.bfloat16)
+    rows, (main_mine, main_other) = joined_halves(
+        rank,
+        grad_projected,
+        normed_one,
+        w_joined,
+        gain_one[None, :],
+        grad_wo,
+        jnp.pad(grad_table, (0, width - table_size))[None],
+        experts,
+    )
     main_other, returned, first_got, second_got = lax.optimization_barrier(
         (swap(main_other, "dp", 1), returned, first_got, second_got)
     )
@@ -747,39 +837,32 @@
     )
     shares, grad_got, input_own = lax.optimization_barrier((shares, grad_got, input_own))
     main_mine = spread(low_sum(*shares), "expert").reshape(main_mine.shape)
+    grad_normed_one = sum(dot_tn(got, part) for got, part in zip(grad_got, joined_parts))
+    inv_own = inverse_rms(input_own)
+    input_grad = grad_residual + norm_backward(grad_normed_one, gain_one, input_own * inv_own, inv_own)
     main_mine, first_got, second_got = lax.optimization_barrier((main_mine, first_got, second_got))
     pairs = ((first_pair, first_got), (second_pair, second_got))
     total = jnp.stack([low_sum(pair[0], got) for pair, got in pairs])
-    rest = swap(total, "dp", 1)
+    grad_first, grad_second = both_halves(rank, total, swap(total, "dp", 1))
     norm_one = main_mine[rows].astype(jnp.float32)
     norm_one = norm_one + sum(swap(norm_one, "tensor", k) for k in range(1, tensor_count))
-    main_mine = main_mine[:rows]
-    main_other = swap(main_mine, "dp", 1)
-    first = dp_rank == 0
-    both = jnp.concatenate(
-        [jnp.where(first, total, rest), jnp.where(first, rest, total)], axis=2
-    ).astype(jnp.float32)
-    joined = jnp.concatenate(
-        [jnp.where(first, main_mine, main_other), jnp.where(first, main_other, main_mine)], axis=0
-    ).astype(jnp.float32)
-    shared = joined[used + inner :]
-
-    grad_normed_one = sum(dot_tn(got, part) for got, part in zip(grad_got, joined_parts))
-    inv_own = inverse_rms(input_own)
-    input_grad = grad_residual + norm_backward(grad_normed_one, gain_one, input_own * inv_own, inv_own)
+    grad_query, grad_key, grad_value, grad_output, shared = joined_whole(
+        rank, main_mine, swap(main_mine, "dp", 1), rows, inner
+    )
+
     return (
         output,
         input_grad,
-        joined[:inner].T,
-        joined[inner : 2 * inner].T,
-        joined[2 * inner : used].T,
-        joined[used : used + inner],
-        shared[grad_wo.shape[0] - inner, :table_size].reshape(local_heads, NUM_BUCKETS).T,
+        grad_query.T,
+        grad_key.T,
+        grad_value.T,
+        grad_output,
+        shared[grad_wo.shape[1] - inner, :table_size].reshape(local_heads, NUM_BUCKETS).T,
         norm_one,
         shared[experts],
         shared[:experts].T,
-        both[0][None],
-        both[1].T[None],
+        grad_first,
+        grad_second,
     )
 
 

time: 328 us -> 322 us (0.982)
  Pallas kernels: 124 us -> 137 us
  local copies, waits for them, and re-layouts: 39.1 us -> 31.2 us
  other arithmetic: 26.1 us -> 21.2 us
  waiting for transfers between devices: 46.4 us -> 43 us
    pallas_call x0 -> x3, Pallas kernels: none -> 13.3 us  [the longest x1 6 us: joined_halves(): pl.pallas_call(joined_kernel, in_specs=[pl.BlockSpec(memory_space=pltpu.S...]
    dot_general x1 -> x0, matrix products: 4.09 us -> none  [on_device(): jnp.einsum('bcn,bnd->cd', grad_projected, normed_one.reshape(tensor_count...]
    unnamed x128 -> x123, local copies, waits for them, and re-layouts: 16.7 us -> 15.9 us
  transfers between devices with their start and end apart: 48 -> 48, of which waited for: 10 -> 11; matrix products, arithmetic and copies ran while one was open for 15% -> 15% of each run, Pallas kernels for 39% -> 40%
where the time goes in v3:
time: 322 us; the launch traced here: 316 us
  Pallas kernels  137 us (43%)
  starting transfers between devices  67.7 us (21%)
  waiting for transfers between devices  43 us (13%)
  local copies, waits for them, and re-layouts  31.2 us (10%)
  other arithmetic  21.2 us (7%)
  matrix products  14.4 us (4%)
    pallas_call x3, Pallas kernels, expert_apply(): pl.pallas_call(functools.partial(expert_kernel, parts, pieces), grid=(par...  44.3 us
    ppermute x42, starting transfers between devices, swap(): return lax.ppermute(array, axis, [(i, i ^ offset) for i in range(count)])  43.3 us
    ppermute x42, waiting for transfers between devices, swap(): return lax.ppermute(array, axis, [(i, i ^ offset) for i in range(count)])  25.7 us
    all_to_all x6, starting transfers between devices, trade(): return lax.all_to_all(array, axis, 0, 0, tiled=True)  24.4 us
    pallas_call x1, Pallas kernels, attend_back(): pl.pallas_call(attend_back_kernel, grid=(heads, seqs), in_specs=[part(0),...  23.6 us
    pallas_call x1, Pallas kernels, expert_weights(): pl.pallas_call(functools.partial(weight_kernel, len(groups)), grid=(steps...  20.7 us
    all_to_all x6, waiting for transfers between devices, trade(): return lax.all_to_all(array, axis, 0, 0, tiled=True)  17.3 us
    unnamed x123, local copies, waits for them, and re-layouts  15.9 us
  transfers between devices with their start and end apart: 48, of which 11 were waited for; matrix products, arithmetic and copies ran while one was open for 15% of the time, Pallas kernels for 40%

profile of v3, /device:TPU:0, one launch (start us, length us, event | category | flops | bytes accessed | tf_op | source)
XLA Modules:
  0.0 316.3 jit_solution(15432216455540218106)
XLA Ops:
  3.2 2.9 collective-permute-start
  10.5 4.3 %all-to-all-start = ((bf16[4,192,768]{2,1,0:T(8,128)(2,1)}), bf16[4,192,768]{2,1,0:T(8,128)(2,1)}, u32[]{:S(2)}, u32[]{:S(2)}) async-start(bf16[4,192,768]{2,1,0:T(8,128)(2,1)} %broadcast_in_dim.20), calls=%async_computation | async-start | bytes 2359296 | tf_op jit(solution)/shard_map/all_to_all | solution.py:638
  24.9 6.6 %shard_map.229 = (bf16[576,2048]{1,0:T(8,128)(2,1)S(1)}, bf16[2048,768]{1,0:T(8,128)(2,1)}) custom-call(f32[2048,768]{1,0:T(8,128)} %x_ref.1, f32[1,768]{1,0:T(1,128)S(1)} %broadcast_in_dim.18.gain_ref, bf16[576,768]{1,0:T(8,128)(2,1)S(1)} %pad_maximum_fusion.2.weight_ref), custom_call_target="tpu_custom_call" | custom-call | flops 3623878656 | bytes 3538944 | tf_op jit(solution)/shard_map/pallas_call | solution.py:323
  31.6 2.8 collective-permute-start.5
  34.4 14.4 %shard_map.230 = (bf16[4,3,64,512]{3,2,1,0:T(8,128)(2,1)S(1)}, f32[3,2,1,1024]{3,2,1,0:T(1,128)S(1)}) custom-call(bf16[3,3,64,2048]{3,2,1,0:T(8,128)(2,1)S(1)} %bitcast.86, bf16[3,3,64,2048]{3,2,1,0:T(8,128)(2,1)S(1)} %bitcast.87, bf16[3,3,64,2048]{3,2,1,0:T(8,128)(2,1)S(1)} %bitcast.88, f32[3,1,2048]{2,1,0:T(1,128)S(1)} %broadcast_in_dim.19.vec_ref), custom_call_target="tpu_custom_call" | custom-call | flops 6442450944 | bytes 6291456 | tf_op jit(solution)/shard_map/pallas_call | solution.py:95
  51.2 3.1 collective-permute-start.6
  54.3 4.7 %all-to-all-start.1 = ((bf16[4,192,512]{2,1,0:T(8,128)(2,1)}), bf16[4,192,512]{2,1,0:T(8,128)(2,1)}, u32[]{:S(2)}, u32[]{:S(2)}) async-start(bf16[4,192,512]{2,1,0:T(8,128)(2,1)} %bitcast.83), calls=%async_computation.1 | async-start | bytes 1572864 | tf_op jit(solution)/shard_map/all_to_all | solution.py:638
  65.3 6.1 %all-to-all-done.1 = bf16[4,192,512]{2,1,0:T(8,128)(2,1)} async-done(((bf16[4,192,512]{2,1,0:T(8,128)(2,1)}), bf16[4,192,512]{2,1,0:T(8,128)(2,1)}, u32[]{:S(2)}, u32[]{:S(2)}) %all-to-all-start.1) | async-done | bytes 786464 | tf_op jit(solution)/shard_map/all_to_all | solution.py:638
  71.4 5.7 %shard_map.232 = (f32[512,768]{1,0:T(8,128)}, f32[4,512]{1,0:T(4,128)S(1)}, f32[1,512]{1,0:T(1,128)S(1)}, bf16[264,768]{1,0:T(8,128)(2,1)S(1)}, bf16[264,768]{1,...) custom-call(bf16[768,512]{1,0:T(8,128)(2,1)} %bitcast.10.mixed_ref, ...), custom_call_target="tpu_custom_call" | custom-call | flops 1811939328 | bytes 1769472 | tf_op jit(solution)/shard_map/pallas_call | solution.py:259
  77.8 4.5 %collective-permute-done.8.refs_10_.refs_8_ = bf16[768,384]{1,0:T(8,128)(2,1)} collective-permute-done((bf16[768,384]{1,0:T(8,128)(2,1)}, bf16[768,384]{1,0:T(8,128)(2,1)}, u32[]{:S(2)}, u32[]{:S(2)}) %collective-permute-start.8) | collective-permute-done | bytes 589856 | tf_op jit(solution)/shard_map/ppermute | solution.py:634
  82.9 3.6 %collective-permute-done.7.refs_1_ = bf16[264,768]{1,0:T(8,128)(2,1)S(1)} collective-permute-done((bf16[264,768]{1,0:T(8,128)(2,1)S(1)}, bf16[264,768]{1,0:T(8,128)(2,1)S(1)}, u32[]{:S(2)}, u32[]{:S(2)}) %collective-permute-start.7) | collective-permute-done | bytes 405536 | tf_op jit(solution)/shard_map/ppermute | solution.py:634
  91.2 20.5 %shard_map.233 = (bf16[8,512,384]{2,1,0:T(8,128)(2,1)}, bf16[8,512,384]{2,1,0:T(8,128)(2,1)}, bf16[768,512]{1,0:T(8,128)(2,1)}, bf16[768,512]{1,0:T(8,128)(2,1)}...) custom-call(bf16[264,768]{1,0:T(8,128)(2,1)} %copy-done.24, ...), custom_call_target="tpu_custom_call" | custom-call | flops 14495514624 | bytes 14155776 | tf_op jit(solution)/shard_map/pallas_call | solution.py:444
  113.4 3.1 collective-permute-done.16.refs_0_
  118.5 11.8 %shard_map.234 = (bf16[8,256,384]{2,1,0:T(8,128)(2,1)}, bf16[8,256,384]{2,1,0:T(8,128)(2,1)}, bf16[768,256]{1,0:T(8,128)(2,1)S(1)}, bf16[768,256]{1,0:T(8,128)(2...) custom-call(bf16[264,768]{1,0:T(8,128)(2,1)} %copy-done.58, bf16[256,768]{1,0:T(8,128)(2,1)S(1)} %copy-done.18, ...), custom_call_target="tpu_custom_call" | custom-call | flops 7247757312 | bytes 7077888 | tf_op jit(solution)/shard_map/pallas_call | solution.py:444
  131.1 12.0 %shard_map.235 = (bf16[8,256,384]{2,1,0:T(8,128)(2,1)}, bf16[8,256,384]{2,1,0:T(8,128)(2,1)}, bf16[768,256]{1,0:T(8,128)(2,1)S(1)}, bf16[768,256]{1,0:T(8,128)(2...) custom-call(bf16[264,768]{1,0:T(8,128)(2,1)} %copy-done.56, ...), custom_call_target="tpu_custom_call" | custom-call | flops 7247757312 | bytes 7077888 | tf_op jit(solution)/shard_map/pallas_call | solution.py:444
  144.7 20.7 %shard_map.236 = (bf16[4,768,384]{2,1,0:T(8,128)(2,1)}, bf16[4,768,384]{2,1,0:T(8,128)(2,1)}, bf16[4,768,384]{2,1,0:T(8,128)(2,1)}, bf16[4,768,384]{2,1,0:T(8,128)(2,1)}) custom-call(bf16[8,512,384]{2,1,0:T(8,128)(2,1)} %get-tuple-element.243.refs_0_, bf16[8,512,384]{2,1,0:T(8,128)(2,1)} %get-tuple-element.244.refs_1_, bf16[768,512]{1,0:T(8,128)(2,1)S(1)} %copy-done.27, ...), custom_call_target="tpu_custom_call" | custom-call | flops 14495514624 | bytes 14155776 | tf_op jit(solution)/shard_map/pallas_call | solution.py:514
  166.0 6.8 %shard_map.237 = (f32[512,768]{1,0:T(8,128)}, bf16[512,768]{1,0:T(8,128)(2,1)S(1)}, bf16[768,512]{1,0:T(8,128)(2,1)S(1)}, f32[4,768]{1,0:T(4,128)S(1)}, f32[1,768]{1,0:T(1,128)S(1)}) custom-call(f32[512,768]{1,0:T(8,128)} %get-tuple-element.177.residual_ref, bf16[512,768]{1,0:T(8,128)(2,1)S(1)} %copy-done.3, f32[1,768]{1,0:T(1,128)S(1)} %reshape.146.gain_ref, ...), custom_call_target="tpu_custom_call" | custom-call | flops 1811939328 | bytes 1769472 | tf_op jit(solution)/shard_map/pallas_call | solution.py:298
  174.6 3.6 %all-to-all-start.2 = ((bf16[4,192,512]{2,1,0:T(8,128)(2,1)}), bf16[4,192,512]{2,1,0:T(8,128)(2,1)S(1)}, u32[]{:S(2)}, u32[]{:S(2)}) async-start(bf16[4,192,512]{2,1,0:T(8,128)(2,1)} %bitcast.85), calls=%async_computation.2 | async-start | bytes 1572864 | tf_op jit(solution)/shard_map/all_to_all | solution.py:638
  185.8 3.8 %all-to-all-done.2 = bf16[4,192,512]{2,1,0:T(8,128)(2,1)S(1)} async-done(((bf16[4,192,512]{2,1,0:T(8,128)(2,1)}), bf16[4,192,512]{2,1,0:T(8,128)(2,1)S(1)}, u32[]{:S(2)}, u32[]{:S(2)}) %all-to-all-start.2) | async-done | bytes 786464 | tf_op jit(solution)/shard_map/all_to_all | solution.py:638
  189.5 3.7 %all-to-all-start.3 = ((bf16[4,200,768]{2,1,0:T(8,128)(2,1)}), bf16[4,200,768]{2,1,0:T(8,128)(2,1)S(1)}, u32[]{:S(2)}, u32[]{:S(2)}) async-start(bf16[4,200,768]{2,1,0:T(8,128)(2,1)} %pad_maximum_fusion), calls=%async_computation.3 | async-start | bytes 2457600 | tf_op jit(solution)/shard_map/all_to_all | solution.py:638
  193.3 3.1 add_convert_fusion.3
  202.5 23.6 %shard_map.238 = (bf16[4,3,3,64,512]{4,3,2,1,0:T(8,128)(2,1)S(1)}, f32[3,1,2048]{2,1,0:T(1,128)S(1)}) custom-call(bf16[3,3,64,2048]{3,2,1,0:T(8,128)(2,1)} %bitcast.89, bf16[3,3,64,2048]{3,2,1,0:T(8,128)(2,1)} %bitcast.90, bf16[3,3,64,2048]{3,2,1,0:T(8,128)(2,1)} %bitcast.91, bf16[4,3,64,512]{3,2,1,0:T(8,128)(2,1)S(1)} %copy-done.13, ...), custom_call_target="tpu_custom_call" | custom-call | flops 12884901888 | bytes 12582912 | tf_op jit(solution)/shard_map/pallas_call | solution.py:171
  228.8 5.1 %collective-permute-done.26 = bf16[2,768,384]{2,1,0:T(8,128)(2,1)} collective-permute-done((bf16[2,768,384]{2,1,0:T(8,128)(2,1)}, bf16[2,768,384]{2,1,0:T(8,128)(2,1)}, u32[]{:S(2)}, u32[]{:S(2)}) %collective-permute-start.26) | collective-permute-done | bytes 1179680 | tf_op jit(solution)/shard_map/ppermute | solution.py:634
  235.3 6.0 %shard_map.239 = (f32[416,768]{1,0:T(8,128)S(1)}, bf16[416,768]{1,0:T(8,128)(2,1)}) custom-call(s32[1]{0:T(128)} %bitcast.14.rank_ref, bf16[4,576,512]{2,1,0:T(8,128)(2,1)} %bitcast.81, bf16[2048,768]{1,0:T(8,128)(2,1)} %get-tuple-element.289.normed_ref, bf16[576,768]{1,0:T(8,128)(2,1)S(1)} %pad_maximum_fusion.2.weight_ref, ...), custom_call_target="tpu_custom_call" | custom-call | flops 4888461312 | bytes 4773888 | tf_op jit(solution)/shard_map/pallas_call | solution.py:558
  249.4 3.6 %all-to-all-start.4 = ((bf16[4,104,768]{2,1,0:T(8,128)(2,1)}), bf16[4,104,768]{2,1,0:T(8,128)(2,1)S(1)}, u32[]{:S(2)}, u32[]{:S(2)}) async-start(bf16[4,104,768]{2,1,0:T(8,128)(2,1)} %bitcast.21), calls=%async_computation.4 | async-start | bytes 1277952 | tf_op jit(solution)/shard_map/all_to_all | solution.py:638
  262.9 3.5 %multiply_add_fusion.1 = f32[512,768]{1,0:T(8,128)} fusion(f32[512,768]{1,0:T(8,128)S(1)} %copy-done.37, bf16[512,1024]{1,0:T(8,128)(2,1)S(1)} %copy-done.11, bf16[256,768]{1,0:T(8,128)(2,1)} %collective-permute-done.30, bf16[256,768]{1,0:T(8,128)(2,1)} %collective-permute-done.29, bf16[256,768]{1,0:T(8,128)(2,1)} %collective-permute-done.28, ...), kind=kOutput, calls=%fused_computation.17 | convolution fusion | flops 812384256 | bytes 5769216 | tf_op jit(solution)/shard_map/dot_general | solution.py:27
  266.4 8.0 %collective-permute-done.33 = bf16[576,512]{1,0:T(8,128)(2,1)} collective-permute-done((bf16[576,512]{1,0:T(8,128)(2,1)}, bf16[576,512]{1,0:T(8,128)(2,1)}, u32[]{:S(2)}, u32[]{:S(2)}) %collective-permute-start.33) | collective-permute-done | bytes 589856 | tf_op jit(solution)/shard_map/ppermute | solution.py:634
  275.5 4.4 %all-to-all-start.5 = ((bf16[4,104,768]{2,1,0:T(8,128)(2,1)}), bf16[4,104,768]{2,1,0:T(8,128)(2,1)}, u32[]{:S(2)}, u32[]{:S(2)}) async-start(bf16[4,104,768]{2,1,0:T(8,128)(2,1)} %broadcast_in_dim.26), calls=%async_computation.5 | async-start | bytes 1277952 | tf_op jit(solution)/shard_map/all_to_all | solution.py:638
  285.3 3.4 %multiply_reduce_fusion = (f32[512]{0:T(512)S(1)}, f32[512,768]{1,0:T(8,128)}) fusion(f32[512,768]{1,0:T(8,128)S(1)} %copy-done.29, f32[512]{0:T(512)S(1)} %add_rsqrt_fusion, f32[768]{0:T(1024)S(1)} %convert_element_type.160, f32[512,768]{1,0:T(8,128)S(1)} %fusion.31, f32[512,768]{1,0:T(8,128)S(1)} %fusion.29, f32[512,768]{1,0:T(8,128)S(1)} %fusion.30, ...), kind=kOutput, calls=%fused_computation.14 | convolution fusion | flops 455736832 | bytes 9346048 | tf_op jit(solution)/shard_map/dot_general | solution.py:31
  288.7 7.4 %all-to-all-done.5 = bf16[4,104,768]{2,1,0:T(8,128)(2,1)} async-done(((bf16[4,104,768]{2,1,0:T(8,128)(2,1)}), bf16[4,104,768]{2,1,0:T(8,128)(2,1)}, u32[]{:S(2)}, u32[]{:S(2)}) %all-to-all-start.5) | async-done | bytes 639008 | tf_op jit(solution)/shard_map/all_to_all | solution.py:638
  306.9 3.0 shard_map.240
  311.8 4.3 %shard_map.241 = (f32[1,768,768]{2,1,0:T(8,128)}, f32[1,768,768]{2,1,0:T(8,128)}) custom-call(s32[1]{0:T(128)} %bitcast.14.rank_ref, bf16[2,768,384]{2,1,0:T(8,128)(2,1)} %pad_maximum_fusion.1.mine_ref, bf16[2,768,384]{2,1,0:T(8,128)(2,1)} %collective-permute-done.41.other_ref), custom_call_target="tpu_custom_call" | custom-call | flops 294912000 | bytes 288000 | tf_op jit(solution)/shard_map/pallas_call | solution.py:611
  (258 shorter events, 94.4 us)
Async XLA Ops:
  3.2 51.1 %collective-permute-start = (bf16[768,384]{1,0:T(8,128)(2,1)}, bf16[768,384]{1,0:T(8,128)(2,1)}, u32[]{:S(2)}, u32[]{:S(2)}) collective-permute-start(bf16[768,384]{1,0:T(8,128)(2,1)} %get-tuple-element.199.refs_4_.refs_2_), channel_id=1, source_target_pairs={{0,1},{1,0},{2,3},{3,2},{4,5},{5,4},{6,7},{7,6},{8,9},{9,8},{10,11... | collective-permute-start | bytes 1769480 | tf_op jit(solution)/shard_map/ppermute | solution.py:634
  6.2 48.2 %collective-permute-start.2 = (bf16[768,384]{1,0:T(8,128)(2,1)}, bf16[768,384]{1,0:T(8,128)(2,1)}, u32[]{:S(2)}, u32[]{:S(2)}) collective-permute-start(bf16[768,384]{1,0:T(8,128)(2,1)} %get-tuple-element.199.refs_4_.refs_2_), channel_id=1, source_target_pairs={{0,2},{1,3},{2,0},{3,1},{4,6},{5,7},{6,4},{7,5},{8,10},{9,11},{10,... | collective-permute-start | bytes 1769480 | tf_op jit(solution)/shard_map/ppermute | solution.py:634
  8.9 45.5 %collective-permute-start.1 = (bf16[384,768]{1,0:T(8,128)(2,1)}, bf16[384,768]{1,0:T(8,128)(2,1)}, u32[]{:S(2)}, u32[]{:S(2)}) collective-permute-start(bf16[384,768]{1,0:T(8,128)(2,1)} %get-tuple-element.207.refs_12_.refs_10_), channel_id=1, source_target_pairs={{0,2},{1,3},{2,0},{3,1},{4,6},{5,7},{6,4},{7,5},{8,10},{9,11},{10,... | collective-permute-start | bytes 1769480 | tf_op jit(solution)/shard_map/ppermute | solution.py:634
  9.4 45.0 %collective-permute-start.3 = (bf16[384,768]{1,0:T(8,128)(2,1)}, bf16[384,768]{1,0:T(8,128)(2,1)}, u32[]{:S(2)}, u32[]{:S(2)}) collective-permute-start(bf16[384,768]{1,0:T(8,128)(2,1)} %get-tuple-element.207.refs_12_.refs_10_), channel_id=1, source_target_pairs={{0,1},{1,0},{2,3},{3,2},{4,5},{5,4},{6,7},{7,6},{8,9},{9,8},{10,11... | collective-permute-start | bytes 1769480 | tf_op jit(solution)/shard_map/ppermute | solution.py:634
  10.5 43.8 %all-to-all-start = ((bf16[4,192,768]{2,1,0:T(8,128)(2,1)}), bf16[4,192,768]{2,1,0:T(8,128)(2,1)}, u32[]{:S(2)}, u32[]{:S(2)}) async-start(bf16[4,192,768]{2,1,0:T(8,128)(2,1)} %broadcast_in_dim.20), calls=%async_computation | async-start | bytes 2359296 | tf_op jit(solution)/shard_map/all_to_all | solution.py:638
  51.2 26.6 %collective-permute-start.6 = (bf16[256,768]{1,0:T(8,128)(2,1)}, bf16[256,768]{1,0:T(8,128)(2,1)}, u32[]{:S(2)}, u32[]{:S(2)}) collective-permute-start(bf16[256,768]{1,0:T(8,128)(2,1)} %get-tuple-element.185), channel_id=1, source_target_pairs={{0,12},{4,8},{8,4},{12,0},{1,13},{5,9},{9,5},{13,1},{2,14},{6,10},... | collective-permute-start | bytes 1179656 | tf_op jit(solution)/shard_map/ppermute | solution.py:634
  59.1 23.2 %collective-permute-start.8 = (bf16[768,384]{1,0:T(8,128)(2,1)}, bf16[768,384]{1,0:T(8,128)(2,1)}, u32[]{:S(2)}, u32[]{:S(2)}) collective-permute-start(bf16[768,384]{1,0:T(8,128)(2,1)} %collective-permute-done.refs_6_.refs_4_), channel_id=1, source_target_pairs={{0,2},{1,3},{2,0},{3,1},{4,6},{5,7},{6,4},{7,5},{8,10},{9,11},{10,... | collective-permute-start | bytes 1769480 | tf_op jit(solution)/shard_map/ppermute | solution.py:634
  61.2 25.3 %collective-permute-start.10 = (bf16[768,384]{1,0:T(8,128)(2,1)}, bf16[768,384]{1,0:T(8,128)(2,1)}, u32[]{:S(2)}, u32[]{:S(2)}) collective-permute-start(bf16[768,384]{1,0:T(8,128)(2,1)} %collective-permute-done.refs_6_.refs_4_), channel_id=1, source_target_pairs={{0,16},{16,0},{1,17},{17,1},{2,18},{18,2},{3,19},{19,3},{4,20},{20... | collective-permute-start | bytes 1769480 | tf_op jit(solution)/shard_map/ppermute | solution.py:634
  61.2 21.2 %collective-permute-start.9 = (bf16[384,768]{1,0:T(8,128)(2,1)}, bf16[384,768]{1,0:T(8,128)(2,1)}, u32[]{:S(2)}, u32[]{:S(2)}) collective-permute-start(bf16[384,768]{1,0:T(8,128)(2,1)} %collective-permute-done.1.refs_16_.refs_14_), channel_id=1, source_target_pairs={{0,1},{1,0},{2,3},{3,2},{4,5},{5,4},{6,7},{7,6},{8,9},{9,8},{10,11... | collective-permute-start | bytes 1769480 | tf_op jit(solution)/shard_map/ppermute | solution.py:634
  87.0 29.5 %collective-permute-start.16 = (bf16[264,768]{1,0:T(8,128)(2,1)S(1)}, bf16[264,768]{1,0:T(8,128)(2,1)S(1)}, u32[]{:S(2)}, u32[]{:S(2)}) collective-permute-start(bf16[264,768]{1,0:T(8,128)(2,1)S(1)} %get-tuple-element.221), channel_id=1, source_target_pairs={{0,8},{4,12},{8,0},{12,4},{1,9},{5,13},{9,1},{13,5},{2,10},{6,14},... | collective-permute-start | bytes 1216520 | tf_op jit(solution)/shard_map/ppermute | solution.py:634
  87.0 43.3 %collective-permute-start.19 = (bf16[264,768]{1,0:T(8,128)(2,1)S(1)}, bf16[264,768]{1,0:T(8,128)(2,1)S(1)}, u32[]{:S(2)}, u32[]{:S(2)}) collective-permute-start(bf16[264,768]{1,0:T(8,128)(2,1)S(1)} %get-tuple-element.232), channel_id=1, source_target_pairs={{0,12},{4,8},{8,4},{12,0},{1,13},{5,9},{9,5},{13,1},{2,14},{6,10},... | collective-permute-start | bytes 1216520 | tf_op jit(solution)/shard_map/ppermute | solution.py:634
  89.7 26.8 %collective-permute-start.17 = (bf16[576,768]{1,0:T(8,128)(2,1)S(1)}, bf16[576,768]{1,0:T(8,128)(2,1)S(1)}, u32[]{:S(2)}, u32[]{:S(2)}) collective-permute-start(bf16[576,768]{1,0:T(8,128)(2,1)S(1)} %pad_maximum_fusion.2.weight_ref), channel_id=1, source_target_pairs={{0,1},{1,0},{2,3},{3,2},{4,5},{5,4},{6,7},{7,6},{8,9},{9,8},{10,11... | collective-permute-start | bytes 2654216 | tf_op jit(solution)/shard_map/ppermute | solution.py:634
  90.5 25.9 %collective-permute-start.18 = (bf16[576,768]{1,0:T(8,128)(2,1)S(1)}, bf16[576,768]{1,0:T(8,128)(2,1)S(1)}, u32[]{:S(2)}, u32[]{:S(2)}) collective-permute-start(bf16[576,768]{1,0:T(8,128)(2,1)S(1)} %pad_maximum_fusion.2.weight_ref), channel_id=1, source_target_pairs={{0,2},{1,3},{2,0},{3,1},{4,6},{5,7},{6,4},{7,5},{8,10},{9,11},{10,... | collective-permute-start | bytes 2654216 | tf_op jit(solution)/shard_map/ppermute | solution.py:634
  112.5 52.9 %collective-permute-start.21 = (bf16[264,768]{1,0:T(8,128)(2,1)}, bf16[264,768]{1,0:T(8,128)(2,1)S(1)}, u32[]{:S(2)}, u32[]{:S(2)}) collective-permute-start(bf16[264,768]{1,0:T(8,128)(2,1)} %get-tuple-element.260), channel_id=1, source_target_pairs={{0,4},{4,0},{8,12},{12,8},{1,5},{5,1},{9,13},{13,9},{2,6},{6,2},{1... | collective-permute-start | bytes 1216520 | tf_op jit(solution)/shard_map/ppermute | solution.py:634
  117.7 27.0 %collective-permute-start.20 = (bf16[576,768]{1,0:T(8,128)(2,1)S(1)}, bf16[576,768]{1,0:T(8,128)(2,1)S(1)}, u32[]{:S(2)}, u32[]{:S(2)}) collective-permute-start(bf16[576,768]{1,0:T(8,128)(2,1)S(1)} %pad_maximum_fusion.2.weight_ref), channel_id=1, source_target_pairs={{0,3},{1,2},{2,1},{3,0},{4,7},{5,6},{6,5},{7,4},{8,11},{9,10},{10,... | collective-permute-start | bytes 2654216 | tf_op jit(solution)/shard_map/ppermute | solution.py:634
  130.4 35.0 %collective-permute-start.22 = (bf16[264,768]{1,0:T(8,128)(2,1)S(1)}, bf16[264,768]{1,0:T(8,128)(2,1)S(1)}, u32[]{:S(2)}, u32[]{:S(2)}) collective-permute-start(bf16[264,768]{1,0:T(8,128)(2,1)S(1)} %get-tuple-element.261), channel_id=1, source_target_pairs={{0,8},{4,12},{8,0},{12,4},{1,9},{5,13},{9,1},{13,5},{2,10},{6,14},... | collective-permute-start | bytes 1216520 | tf_op jit(solution)/shard_map/ppermute | solution.py:634
  143.2 22.2 %collective-permute-start.23 = (bf16[264,768]{1,0:T(8,128)(2,1)S(1)}, bf16[264,768]{1,0:T(8,128)(2,1)S(1)}, u32[]{:S(2)}, u32[]{:S(2)}) collective-permute-start(bf16[264,768]{1,0:T(8,128)(2,1)S(1)} %get-tuple-element.262), channel_id=1, source_target_pairs={{0,12},{4,8},{8,4},{12,0},{1,13},{5,9},{9,5},{13,1},{2,14},{6,10},... | collective-permute-start | bytes 1216520 | tf_op jit(solution)/shard_map/ppermute | solution.py:634
  165.4 27.9 %collective-permute-start.24 = (bf16[4,768,384]{2,1,0:T(8,128)(2,1)}, bf16[4,768,384]{2,1,0:T(8,128)(2,1)}, u32[]{:S(2)}, u32[]{:S(2)}) collective-permute-start(bf16[4,768,384]{2,1,0:T(8,128)(2,1)} %get-tuple-element.268), channel_id=1, source_target_pairs={{0,16},{16,0},{1,17},{17,1},{2,18},{18,2},{3,19},{19,3},{4,20},{20... | collective-permute-start | bytes 7077896 | tf_op jit(solution)/shard_map/ppermute | solution.py:634
  165.5 27.8 %collective-permute-start.25 = (bf16[4,768,384]{2,1,0:T(8,128)(2,1)}, bf16[4,768,384]{2,1,0:T(8,128)(2,1)}, u32[]{:S(2)}, u32[]{:S(2)}) collective-permute-start(bf16[4,768,384]{2,1,0:T(8,128)(2,1)} %get-tuple-element.269), channel_id=1, source_target_pairs={{0,16},{16,0},{1,17},{17,1},{2,18},{18,2},{3,19},{19,3},{4,20},{20... | collective-permute-start | bytes 7077896 | tf_op jit(solution)/shard_map/ppermute | solution.py:634
  178.2 49.6 %collective-permute-start.28 = (bf16[256,768]{1,0:T(8,128)(2,1)}, bf16[256,768]{1,0:T(8,128)(2,1)}, u32[]{:S(2)}, u32[]{:S(2)}) collective-permute-start(bf16[256,768]{1,0:T(8,128)(2,1)} %get-tuple-element.283), channel_id=1, source_target_pairs={{0,4},{4,0},{8,12},{12,8},{1,5},{5,1},{9,13},{13,9},{2,6},{6,2},{1... | collective-permute-start | bytes 1179656 | tf_op jit(solution)/shard_map/ppermute | solution.py:634
  179.6 48.1 %collective-permute-start.29 = (bf16[256,768]{1,0:T(8,128)(2,1)}, bf16[256,768]{1,0:T(8,128)(2,1)}, u32[]{:S(2)}, u32[]{:S(2)}) collective-permute-start(bf16[256,768]{1,0:T(8,128)(2,1)} %get-tuple-element.284), channel_id=1, source_target_pairs={{0,8},{4,12},{8,0},{12,4},{1,9},{5,13},{9,1},{13,5},{2,10},{6,14},... | collective-permute-start | bytes 1179656 | tf_op jit(solution)/shard_map/ppermute | solution.py:634
  181.2 46.6 %collective-permute-start.30 = (bf16[256,768]{1,0:T(8,128)(2,1)}, bf16[256,768]{1,0:T(8,128)(2,1)}, u32[]{:S(2)}, u32[]{:S(2)}) collective-permute-start(bf16[256,768]{1,0:T(8,128)(2,1)} %get-tuple-element.285), channel_id=1, source_target_pairs={{0,12},{4,8},{8,4},{12,0},{1,13},{5,9},{9,5},{13,1},{2,14},{6,10},... | collective-permute-start | bytes 1179656 | tf_op jit(solution)/shard_map/ppermute | solution.py:634
  189.5 38.3 %all-to-all-start.3 = ((bf16[4,200,768]{2,1,0:T(8,128)(2,1)}), bf16[4,200,768]{2,1,0:T(8,128)(2,1)S(1)}, u32[]{:S(2)}, u32[]{:S(2)}) async-start(bf16[4,200,768]{2,1,0:T(8,128)(2,1)} %pad_maximum_fusion), calls=%async_computation.3 | async-start | bytes 2457600 | tf_op jit(solution)/shard_map/all_to_all | solution.py:638
  196.4 37.6 %collective-permute-start.26 = (bf16[2,768,384]{2,1,0:T(8,128)(2,1)}, bf16[2,768,384]{2,1,0:T(8,128)(2,1)}, u32[]{:S(2)}, u32[]{:S(2)}) collective-permute-start(bf16[2,768,384]{2,1,0:T(8,128)(2,1)} %add_convert_fusion.3), channel_id=1, source_target_pairs={{0,1},{1,0},{2,3},{3,2},{4,5},{5,4},{6,7},{7,6},{8,9},{9,8},{10,11... | collective-permute-start | bytes 3538952 | tf_op jit(solution)/shard_map/ppermute | solution.py:634
  201.0 33.0 %collective-permute-start.27 = (bf16[2,768,384]{2,1,0:T(8,128)(2,1)}, bf16[2,768,384]{2,1,0:T(8,128)(2,1)}, u32[]{:S(2)}, u32[]{:S(2)}) collective-permute-start(bf16[2,768,384]{2,1,0:T(8,128)(2,1)} %add_convert_fusion.2), channel_id=1, source_target_pairs={{0,2},{1,3},{2,0},{3,1},{4,6},{5,7},{6,4},{7,5},{8,10},{9,11},{10,... | collective-permute-start | bytes 3538952 | tf_op jit(solution)/shard_map/ppermute | solution.py:634
  243.8 22.6 %collective-permute-start.32 = (bf16[576,512]{1,0:T(8,128)(2,1)}, bf16[576,512]{1,0:T(8,128)(2,1)}, u32[]{:S(2)}, u32[]{:S(2)}) collective-permute-start(bf16[576,512]{1,0:T(8,128)(2,1)} %get-tuple-element.332), channel_id=1, source_target_pairs={{0,1},{1,0},{2,3},{3,2},{4,5},{5,4},{6,7},{7,6},{8,9},{9,8},{10,11... | collective-permute-start | bytes 1769480 | tf_op jit(solution)/shard_map/ppermute | solution.py:634
  245.2 29.1 %collective-permute-start.33 = (bf16[576,512]{1,0:T(8,128)(2,1)}, bf16[576,512]{1,0:T(8,128)(2,1)}, u32[]{:S(2)}, u32[]{:S(2)}) collective-permute-start(bf16[576,512]{1,0:T(8,128)(2,1)} %get-tuple-element.331), channel_id=1, source_target_pairs={{0,2},{1,3},{2,0},{3,1},{4,6},{5,7},{6,4},{7,5},{8,10},{9,11},{10,... | collective-permute-start | bytes 1769480 | tf_op jit(solution)/shard_map/ppermute | solution.py:634
  245.8 28.5 %collective-permute-start.34 = (bf16[576,512]{1,0:T(8,128)(2,1)}, bf16[576,512]{1,0:T(8,128)(2,1)}, u32[]{:S(2)}, u32[]{:S(2)}) collective-permute-start(bf16[576,512]{1,0:T(8,128)(2,1)} %get-tuple-element.330), channel_id=1, source_target_pairs={{0,3},{1,2},{2,1},{3,0},{4,7},{5,6},{6,5},{7,4},{8,11},{9,10},{10,... | collective-permute-start | bytes 1769480 | tf_op jit(solution)/shard_map/ppermute | solution.py:634
  249.4 25.0 %all-to-all-start.4 = ((bf16[4,104,768]{2,1,0:T(8,128)(2,1)}), bf16[4,104,768]{2,1,0:T(8,128)(2,1)S(1)}, u32[]{:S(2)}, u32[]{:S(2)}) async-start(bf16[4,104,768]{2,1,0:T(8,128)(2,1)} %bitcast.21), calls=%async_computation.4 | async-start | bytes 1277952 | tf_op jit(solution)/shard_map/all_to_all | solution.py:638
  257.5 31.2 %collective-permute-start.35 = (bf16[768,384]{1,0:T(8,128)(2,1)}, bf16[768,384]{1,0:T(8,128)(2,1)}, u32[]{:S(2)}, u32[]{:S(2)}) collective-permute-start(bf16[768,384]{1,0:T(8,128)(2,1)} %slice_bitcast_fusion.3), channel_id=1, source_target_pairs={{0,2},{1,3},{2,0},{3,1},{4,6},{5,7},{6,4},{7,5},{8,10},{9,11},{10,... | collective-permute-start | bytes 1769480 | tf_op jit(solution)/shard_map/ppermute | solution.py:634
  262.0 26.7 %collective-permute-start.36 = (bf16[768,384]{1,0:T(8,128)(2,1)}, bf16[768,384]{1,0:T(8,128)(2,1)}, u32[]{:S(2)}, u32[]{:S(2)}) collective-permute-start(bf16[768,384]{1,0:T(8,128)(2,1)} %slice_bitcast_fusion.2), channel_id=1, source_target_pairs={{0,1},{1,0},{2,3},{3,2},{4,5},{5,4},{6,7},{7,6},{8,9},{9,8},{10,11... | collective-permute-start | bytes 1769480 | tf_op jit(solution)/shard_map/ppermute | solution.py:634
  275.5 20.7 %all-to-all-start.5 = ((bf16[4,104,768]{2,1,0:T(8,128)(2,1)}), bf16[4,104,768]{2,1,0:T(8,128)(2,1)}, u32[]{:S(2)}, u32[]{:S(2)}) async-start(bf16[4,104,768]{2,1,0:T(8,128)(2,1)} %broadcast_in_dim.26), calls=%async_computation.5 | async-start | bytes 1277952 | tf_op jit(solution)/shard_map/all_to_all | solution.py:638
  (76 other events, 627.0 us)

commit v4 on v3

--- a/solution.py
+++ b/solution.py
@@ -840,9 +840,9 @@
     grad_normed_one = sum(dot_tn(got, part) for got, part in zip(grad_got, joined_parts))
     inv_own = inverse_rms(input_own)
     input_grad = grad_residual + norm_backward(grad_normed_one, gain_one, input_own * inv_own, inv_own)
-    main_mine, first_got, second_got = lax.optimization_barrier((main_mine, first_got, second_got))
     pairs = ((first_pair, first_got), (second_pair, second_got))
     total = jnp.stack([low_sum(pair[0], got) for pair, got in pairs])
+    main_mine, total = lax.optimization_barrier((main_mine, total))
     grad_first, grad_second = both_halves(rank, total, swap(total, "dp", 1))
     norm_one = main_mine[rows].astype(jnp.float32)
     norm_one = norm_one + sum(swap(norm_one, "tensor", k) for k in range(1, tensor_count))

time: 322 us -> 335 us (1.040)
  waiting for transfers between devices: 43 us -> 58.2 us
    ppermute x42, waiting for transfers between devices: 25.7 us -> 39.7 us  [swap(): return lax.ppermute(array, axis, [(i, i ^ offset) for i in range(count)])]
    unnamed x123 -> x115, local copies, waits for them, and re-layouts: 15.9 us -> 15.5 us
  transfers between devices with their start and end apart: 48 -> 48, of which waited for: 11 -> 11; matrix products, arithmetic and copies ran while one was open for 15% -> 14% of each run, Pallas kernels for 40% -> 39%
where the time goes in v4:
time: 335 us; the launch traced here: 329 us
  Pallas kernels  137 us (41%)
  starting transfers between devices  67.8 us (20%)
  waiting for transfers between devices  58.2 us (17%)
  local copies, waits for them, and re-layouts  29 us (9%)
  other arithmetic  21.3 us (6%)
  matrix products  14.3 us (4%)
    pallas_call x3, Pallas kernels, expert_apply(): pl.pallas_call(functools.partial(expert_kernel, parts, pieces), grid=(par...  44.3 us
    ppermute x42, starting transfers between devices, swap(): return lax.ppermute(array, axis, [(i, i ^ offset) for i in range(count)])  43.4 us
    ppermute x42, waiting for transfers between devices, swap(): return lax.ppermute(array, axis, [(i, i ^ offset) for i in range(count)])  39.7 us
    all_to_all x6, starting transfers between devices, trade(): return lax.all_to_all(array, axis, 0, 0, tiled=True)  24.4 us
    pallas_call x1, Pallas kernels, attend_back(): pl.pallas_call(attend_back_kernel, grid=(heads, seqs), in_specs=[part(0),...  23.6 us
    pallas_call x1, Pallas kernels, expert_weights(): pl.pallas_call(functools.partial(weight_kernel, len(groups)), grid=(steps...  20.6 us
    all_to_all x6, waiting for transfers between devices, trade(): return lax.all_to_all(array, axis, 0, 0, tiled=True)  18.5 us
    unnamed x115, local copies, waits for them, and re-layouts  15.5 us
  transfers between devices with their start and end apart: 48, of which 11 were waited for; matrix products, arithmetic and copies ran while one was open for 14% of the time, Pallas kernels for 39%

profile of v4, /device:TPU:0, one launch (start us, length us, event | category | flops | bytes accessed | tf_op | source)
XLA Modules:
  0.0 329.4 jit_solution(896680311099854988)
XLA Ops:
  3.2 2.9 collective-permute-start
  10.5 4.3 %all-to-all-start = ((bf16[4,192,768]{2,1,0:T(8,128)(2,1)}), bf16[4,192,768]{2,1,0:T(8,128)(2,1)}, u32[]{:S(2)}, u32[]{:S(2)}) async-start(bf16[4,192,768]{2,1,0:T(8,128)(2,1)} %broadcast_in_dim.20), calls=%async_computation | async-start | bytes 2359296 | tf_op jit(solution)/shard_map/all_to_all | solution.py:638
  24.9 6.6 %shard_map.229 = (bf16[576,2048]{1,0:T(8,128)(2,1)S(1)}, bf16[2048,768]{1,0:T(8,128)(2,1)}) custom-call(f32[2048,768]{1,0:T(8,128)} %x_ref.1, f32[1,768]{1,0:T(1,128)S(1)} %broadcast_in_dim.18.gain_ref, bf16[576,768]{1,0:T(8,128)(2,1)S(1)} %pad_maximum_fusion.2.weight_ref), custom_call_target="tpu_custom_call" | custom-call | flops 3623878656 | bytes 3538944 | tf_op jit(solution)/shard_map/pallas_call | solution.py:323
  34.4 14.4 %shard_map.230 = (bf16[4,3,64,512]{3,2,1,0:T(8,128)(2,1)S(1)}, f32[3,2,1,1024]{3,2,1,0:T(1,128)S(1)}) custom-call(bf16[3,3,64,2048]{3,2,1,0:T(8,128)(2,1)S(1)} %bitcast.86, bf16[3,3,64,2048]{3,2,1,0:T(8,128)(2,1)S(1)} %bitcast.87, bf16[3,3,64,2048]{3,2,1,0:T(8,128)(2,1)S(1)} %bitcast.88, f32[3,1,2048]{2,1,0:T(1,128)S(1)} %broadcast_in_dim.19.vec_ref), custom_call_target="tpu_custom_call" | custom-call | flops 6442450944 | bytes 6291456 | tf_op jit(solution)/shard_map/pallas_call | solution.py:95
  51.2 3.2 collective-permute-start.6
  54.3 4.7 %all-to-all-start.1 = ((bf16[4,192,512]{2,1,0:T(8,128)(2,1)}), bf16[4,192,512]{2,1,0:T(8,128)(2,1)}, u32[]{:S(2)}, u32[]{:S(2)}) async-start(bf16[4,192,512]{2,1,0:T(8,128)(2,1)} %bitcast.83), calls=%async_computation.1 | async-start | bytes 1572864 | tf_op jit(solution)/shard_map/all_to_all | solution.py:638
  65.3 6.1 %all-to-all-done.1 = bf16[4,192,512]{2,1,0:T(8,128)(2,1)} async-done(((bf16[4,192,512]{2,1,0:T(8,128)(2,1)}), bf16[4,192,512]{2,1,0:T(8,128)(2,1)}, u32[]{:S(2)}, u32[]{:S(2)}) %all-to-all-start.1) | async-done | bytes 786464 | tf_op jit(solution)/shard_map/all_to_all | solution.py:638
  71.4 5.7 %shard_map.232 = (f32[512,768]{1,0:T(8,128)}, f32[4,512]{1,0:T(4,128)S(1)}, f32[1,512]{1,0:T(1,128)S(1)}, bf16[264,768]{1,0:T(8,128)(2,1)S(1)}, bf16[264,768]{1,...) custom-call(bf16[768,512]{1,0:T(8,128)(2,1)} %bitcast.10.mixed_ref, ...), custom_call_target="tpu_custom_call" | custom-call | flops 1811939328 | bytes 1769472 | tf_op jit(solution)/shard_map/pallas_call | solution.py:259
  77.8 4.5 %collective-permute-done.8.refs_10_.refs_8_ = bf16[768,384]{1,0:T(8,128)(2,1)} collective-permute-done((bf16[768,384]{1,0:T(8,128)(2,1)}, bf16[768,384]{1,0:T(8,128)(2,1)}, u32[]{:S(2)}, u32[]{:S(2)}) %collective-permute-start.8) | collective-permute-done | bytes 589856 | tf_op jit(solution)/shard_map/ppermute | solution.py:634
  82.9 3.6 %collective-permute-done.7.refs_1_ = bf16[264,768]{1,0:T(8,128)(2,1)S(1)} collective-permute-done((bf16[264,768]{1,0:T(8,128)(2,1)S(1)}, bf16[264,768]{1,0:T(8,128)(2,1)S(1)}, u32[]{:S(2)}, u32[]{:S(2)}) %collective-permute-start.7) | collective-permute-done | bytes 405536 | tf_op jit(solution)/shard_map/ppermute | solution.py:634
  91.2 20.5 %shard_map.233 = (bf16[8,512,384]{2,1,0:T(8,128)(2,1)}, bf16[8,512,384]{2,1,0:T(8,128)(2,1)}, bf16[768,512]{1,0:T(8,128)(2,1)}, bf16[768,512]{1,0:T(8,128)(2,1)}...) custom-call(bf16[264,768]{1,0:T(8,128)(2,1)} %copy-done.24, ...), custom_call_target="tpu_custom_call" | custom-call | flops 14495514624 | bytes 14155776 | tf_op jit(solution)/shard_map/pallas_call | solution.py:444
  113.3 3.1 collective-permute-done.16.refs_0_
  118.6 11.8 %shard_map.234 = (bf16[8,256,384]{2,1,0:T(8,128)(2,1)}, bf16[8,256,384]{2,1,0:T(8,128)(2,1)}, bf16[768,256]{1,0:T(8,128)(2,1)S(1)}, bf16[768,256]{1,0:T(8,128)(2...) custom-call(bf16[264,768]{1,0:T(8,128)(2,1)} %copy-done.54, bf16[256,768]{1,0:T(8,128)(2,1)S(1)} %copy-done.18, ...), custom_call_target="tpu_custom_call" | custom-call | flops 7247757312 | bytes 7077888 | tf_op jit(solution)/shard_map/pallas_call | solution.py:444
  131.1 12.1 %shard_map.235 = (bf16[8,256,384]{2,1,0:T(8,128)(2,1)}, bf16[8,256,384]{2,1,0:T(8,128)(2,1)}, bf16[768,256]{1,0:T(8,128)(2,1)S(1)}, bf16[768,256]{1,0:T(8,128)(2...) custom-call(bf16[264,768]{1,0:T(8,128)(2,1)} %copy-done.52, ...), custom_call_target="tpu_custom_call" | custom-call | flops 7247757312 | bytes 7077888 | tf_op jit(solution)/shard_map/pallas_call | solution.py:444
  144.8 20.6 %shard_map.236 = (bf16[4,768,384]{2,1,0:T(8,128)(2,1)}, bf16[4,768,384]{2,1,0:T(8,128)(2,1)}, bf16[4,768,384]{2,1,0:T(8,128)(2,1)}, bf16[4,768,384]{2,1,0:T(8,128)(2,1)}) custom-call(bf16[8,512,384]{2,1,0:T(8,128)(2,1)} %get-tuple-element.242.refs_0_, bf16[8,512,384]{2,1,0:T(8,128)(2,1)} %get-tuple-element.243.refs_1_, bf16[768,512]{1,0:T(8,128)(2,1)S(1)} %copy-done.27, ...), custom_call_target="tpu_custom_call" | custom-call | flops 14495514624 | bytes 14155776 | tf_op jit(solution)/shard_map/pallas_call | solution.py:514
  166.0 6.8 %shard_map.237 = (f32[512,768]{1,0:T(8,128)}, bf16[512,768]{1,0:T(8,128)(2,1)S(1)}, bf16[768,512]{1,0:T(8,128)(2,1)S(1)}, f32[4,768]{1,0:T(4,128)S(1)}, f32[1,768]{1,0:T(1,128)S(1)}) custom-call(f32[512,768]{1,0:T(8,128)} %get-tuple-element.176.residual_ref, bf16[512,768]{1,0:T(8,128)(2,1)S(1)} %copy-done.3, f32[1,768]{1,0:T(1,128)S(1)} %reshape.146.gain_ref, ...), custom_call_target="tpu_custom_call" | custom-call | flops 1811939328 | bytes 1769472 | tf_op jit(solution)/shard_map/pallas_call | solution.py:298
  174.6 3.6 %all-to-all-start.2 = ((bf16[4,192,512]{2,1,0:T(8,128)(2,1)}), bf16[4,192,512]{2,1,0:T(8,128)(2,1)S(1)}, u32[]{:S(2)}, u32[]{:S(2)}) async-start(bf16[4,192,512]{2,1,0:T(8,128)(2,1)} %bitcast.85), calls=%async_computation.2 | async-start | bytes 1572864 | tf_op jit(solution)/shard_map/all_to_all | solution.py:638
  185.8 3.8 %all-to-all-done.2 = bf16[4,192,512]{2,1,0:T(8,128)(2,1)S(1)} async-done(((bf16[4,192,512]{2,1,0:T(8,128)(2,1)}), bf16[4,192,512]{2,1,0:T(8,128)(2,1)S(1)}, u32[]{:S(2)}, u32[]{:S(2)}) %all-to-all-start.2) | async-done | bytes 786464 | tf_op jit(solution)/shard_map/all_to_all | solution.py:638
  189.5 3.7 %all-to-all-start.3 = ((bf16[4,200,768]{2,1,0:T(8,128)(2,1)}), bf16[4,200,768]{2,1,0:T(8,128)(2,1)S(1)}, u32[]{:S(2)}, u32[]{:S(2)}) async-start(bf16[4,200,768]{2,1,0:T(8,128)(2,1)} %pad_maximum_fusion), calls=%async_computation.3 | async-start | bytes 2457600 | tf_op jit(solution)/shard_map/all_to_all | solution.py:638
  193.3 3.1 add_convert_fusion.3
  202.5 23.6 %shard_map.238 = (bf16[4,3,3,64,512]{4,3,2,1,0:T(8,128)(2,1)S(1)}, f32[3,1,2048]{2,1,0:T(1,128)S(1)}) custom-call(bf16[3,3,64,2048]{3,2,1,0:T(8,128)(2,1)} %bitcast.89, bf16[3,3,64,2048]{3,2,1,0:T(8,128)(2,1)} %bitcast.90, bf16[3,3,64,2048]{3,2,1,0:T(8,128)(2,1)} %bitcast.91, bf16[4,3,64,512]{3,2,1,0:T(8,128)(2,1)S(1)} %copy-done.13, ...), custom_call_target="tpu_custom_call" | custom-call | flops 12884901888 | bytes 12582912 | tf_op jit(solution)/shard_map/pallas_call | solution.py:171
  228.8 5.1 %collective-permute-done.26 = bf16[2,768,384]{2,1,0:T(8,128)(2,1)} collective-permute-done((bf16[2,768,384]{2,1,0:T(8,128)(2,1)}, bf16[2,768,384]{2,1,0:T(8,128)(2,1)}, u32[]{:S(2)}, u32[]{:S(2)}) %collective-permute-start.26) | collective-permute-done | bytes 1179680 | tf_op jit(solution)/shard_map/ppermute | solution.py:634
  235.3 6.0 %shard_map.239 = (f32[416,768]{1,0:T(8,128)S(1)}, bf16[416,768]{1,0:T(8,128)(2,1)}) custom-call(s32[1]{0:T(128)} %bitcast.14.rank_ref, bf16[4,576,512]{2,1,0:T(8,128)(2,1)} %bitcast.81, bf16[2048,768]{1,0:T(8,128)(2,1)} %get-tuple-element.288.normed_ref, bf16[576,768]{1,0:T(8,128)(2,1)S(1)} %pad_maximum_fusion.2.weight_ref, ...), custom_call_target="tpu_custom_call" | custom-call | flops 4888461312 | bytes 4773888 | tf_op jit(solution)/shard_map/pallas_call | solution.py:558
  249.3 3.6 %all-to-all-start.4 = ((bf16[4,104,768]{2,1,0:T(8,128)(2,1)}), bf16[4,104,768]{2,1,0:T(8,128)(2,1)S(1)}, u32[]{:S(2)}, u32[]{:S(2)}) async-start(bf16[4,104,768]{2,1,0:T(8,128)(2,1)} %bitcast.21), calls=%async_computation.4 | async-start | bytes 1277952 | tf_op jit(solution)/shard_map/all_to_all | solution.py:638
  260.2 3.4 %multiply_add_fusion.1 = f32[512,768]{1,0:T(8,128)} fusion(f32[512,768]{1,0:T(8,128)S(1)} %copy-done.33, bf16[512,1024]{1,0:T(8,128)(2,1)S(1)} %copy-done.11, bf16[256,768]{1,0:T(8,128)(2,1)} %collective-permute-done.30, bf16[256,768]{1,0:T(8,128)(2,1)} %collective-permute-done.29, bf16[256,768]{1,0:T(8,128)(2,1)} %collective-permute-done.28, ...), kind=kOutput, calls=%fused_computation.17 | convolution fusion | flops 812384256 | bytes 5769216 | tf_op jit(solution)/shard_map/dot_general | solution.py:27
  263.5 21.5 %collective-permute-done.36 = bf16[768,384]{1,0:T(8,128)(2,1)S(1)} collective-permute-done((bf16[768,384]{1,0:T(8,128)(2,1)S(1)}, bf16[768,384]{1,0:T(8,128)(2,1)S(1)}, u32[]{:S(2)}, u32[]{:S(2)}) %collective-permute-start.36) | collective-permute-done | bytes 589856 | tf_op jit(solution)/shard_map/ppermute | solution.py:634
  289.3 4.4 %all-to-all-start.5 = ((bf16[4,104,768]{2,1,0:T(8,128)(2,1)}), bf16[4,104,768]{2,1,0:T(8,128)(2,1)}, u32[]{:S(2)}, u32[]{:S(2)}) async-start(bf16[4,104,768]{2,1,0:T(8,128)(2,1)} %broadcast_in_dim.26), calls=%async_computation.5 | async-start | bytes 1277952 | tf_op jit(solution)/shard_map/all_to_all | solution.py:638
  299.1 3.4 %multiply_reduce_fusion = (f32[512]{0:T(512)S(1)}, f32[512,768]{1,0:T(8,128)}) fusion(f32[512,768]{1,0:T(8,128)S(1)} %copy-done.29, f32[512]{0:T(512)S(1)} %add_rsqrt_fusion, f32[768]{0:T(1024)S(1)} %convert_element_type.160, f32[512,768]{1,0:T(8,128)S(1)} %fusion.31, f32[512,768]{1,0:T(8,128)S(1)} %fusion.29, f32[512,768]{1,0:T(8,128)S(1)} %fusion.30, ...), kind=kOutput, calls=%fused_computation.14 | convolution fusion | flops 455736832 | bytes 9346048 | tf_op jit(solution)/shard_map/dot_general | solution.py:31
  302.5 8.7 %all-to-all-done.5 = bf16[4,104,768]{2,1,0:T(8,128)(2,1)} async-done(((bf16[4,104,768]{2,1,0:T(8,128)(2,1)}), bf16[4,104,768]{2,1,0:T(8,128)(2,1)}, u32[]{:S(2)}, u32[]{:S(2)}) %all-to-all-start.5) | async-done | bytes 639008 | tf_op jit(solution)/shard_map/all_to_all | solution.py:638
  316.0 3.4 %multiply_add_fusion = f32[512,768]{1,0:T(8,128)} fusion(f32[512,768]{1,0:T(8,128)} %get-tuple-element.302, f32[512,768]{1,0:T(8,128)} %get-tuple-element.327, f32[512,768]{1,0:T(8,128)S(1)} %copy-done.29, f32[512]{0:T(512)S(1)} %broadcast_multiply_fusion, f32[512]{0:T(512)S(1)} %add_rsqrt_fusion), kind=kLoop, calls=%fused_computation.13 | loop fusion | flops 1966080 | bytes 6295552 | tf_op jit(solution)/shard_map/add | solution.py:842
  320.0 3.0 shard_map.240
  324.8 4.3 %shard_map.241 = (f32[1,768,768]{2,1,0:T(8,128)}, f32[1,768,768]{2,1,0:T(8,128)}) custom-call(s32[1]{0:T(128)} %bitcast.14.rank_ref, bf16[2,768,384]{2,1,0:T(8,128)(2,1)} %pad_maximum_fusion.1.mine_ref, bf16[2,768,384]{2,1,0:T(8,128)(2,1)} %collective-permute-done.41.other_ref), custom_call_target="tpu_custom_call" | custom-call | flops 294912000 | bytes 288000 | tf_op jit(solution)/shard_map/pallas_call | solution.py:611
  (251 shorter events, 92.2 us)
Async XLA Ops:
  3.2 51.1 %collective-permute-start = (bf16[768,384]{1,0:T(8,128)(2,1)}, bf16[768,384]{1,0:T(8,128)(2,1)}, u32[]{:S(2)}, u32[]{:S(2)}) collective-permute-start(bf16[768,384]{1,0:T(8,128)(2,1)} %get-tuple-element.198.refs_4_.refs_2_), channel_id=1, source_target_pairs={{0,1},{1,0},{2,3},{3,2},{4,5},{5,4},{6,7},{7,6},{8,9},{9,8},{10,11... | collective-permute-start | bytes 1769480 | tf_op jit(solution)/shard_map/ppermute | solution.py:634
  6.2 48.2 %collective-permute-start.2 = (bf16[768,384]{1,0:T(8,128)(2,1)}, bf16[768,384]{1,0:T(8,128)(2,1)}, u32[]{:S(2)}, u32[]{:S(2)}) collective-permute-start(bf16[768,384]{1,0:T(8,128)(2,1)} %get-tuple-element.198.refs_4_.refs_2_), channel_id=1, source_target_pairs={{0,2},{1,3},{2,0},{3,1},{4,6},{5,7},{6,4},{7,5},{8,10},{9,11},{10,... | collective-permute-start | bytes 1769480 | tf_op jit(solution)/shard_map/ppermute | solution.py:634
  8.8 45.5 %collective-permute-start.1 = (bf16[384,768]{1,0:T(8,128)(2,1)}, bf16[384,768]{1,0:T(8,128)(2,1)}, u32[]{:S(2)}, u32[]{:S(2)}) collective-permute-start(bf16[384,768]{1,0:T(8,128)(2,1)} %get-tuple-element.206.refs_12_.refs_10_), channel_id=1, source_target_pairs={{0,2},{1,3},{2,0},{3,1},{4,6},{5,7},{6,4},{7,5},{8,10},{9,11},{10,... | collective-permute-start | bytes 1769480 | tf_op jit(solution)/shard_map/ppermute | solution.py:634
  9.4 45.0 %collective-permute-start.3 = (bf16[384,768]{1,0:T(8,128)(2,1)}, bf16[384,768]{1,0:T(8,128)(2,1)}, u32[]{:S(2)}, u32[]{:S(2)}) collective-permute-start(bf16[384,768]{1,0:T(8,128)(2,1)} %get-tuple-element.206.refs_12_.refs_10_), channel_id=1, source_target_pairs={{0,1},{1,0},{2,3},{3,2},{4,5},{5,4},{6,7},{7,6},{8,9},{9,8},{10,11... | collective-permute-start | bytes 1769480 | tf_op jit(solution)/shard_map/ppermute | solution.py:634
  10.5 43.9 %all-to-all-start = ((bf16[4,192,768]{2,1,0:T(8,128)(2,1)}), bf16[4,192,768]{2,1,0:T(8,128)(2,1)}, u32[]{:S(2)}, u32[]{:S(2)}) async-start(bf16[4,192,768]{2,1,0:T(8,128)(2,1)} %broadcast_in_dim.20), calls=%async_computation | async-start | bytes 2359296 | tf_op jit(solution)/shard_map/all_to_all | solution.py:638
  51.2 26.6 %collective-permute-start.6 = (bf16[256,768]{1,0:T(8,128)(2,1)}, bf16[256,768]{1,0:T(8,128)(2,1)}, u32[]{:S(2)}, u32[]{:S(2)}) collective-permute-start(bf16[256,768]{1,0:T(8,128)(2,1)} %get-tuple-element.184), channel_id=1, source_target_pairs={{0,12},{4,8},{8,4},{12,0},{1,13},{5,9},{9,5},{13,1},{2,14},{6,10},... | collective-permute-start | bytes 1179656 | tf_op jit(solution)/shard_map/ppermute | solution.py:634
  59.1 23.2 %collective-permute-start.8 = (bf16[768,384]{1,0:T(8,128)(2,1)}, bf16[768,384]{1,0:T(8,128)(2,1)}, u32[]{:S(2)}, u32[]{:S(2)}) collective-permute-start(bf16[768,384]{1,0:T(8,128)(2,1)} %collective-permute-done.refs_6_.refs_4_), channel_id=1, source_target_pairs={{0,2},{1,3},{2,0},{3,1},{4,6},{5,7},{6,4},{7,5},{8,10},{9,11},{10,... | collective-permute-start | bytes 1769480 | tf_op jit(solution)/shard_map/ppermute | solution.py:634
  61.2 25.3 %collective-permute-start.10 = (bf16[768,384]{1,0:T(8,128)(2,1)}, bf16[768,384]{1,0:T(8,128)(2,1)}, u32[]{:S(2)}, u32[]{:S(2)}) collective-permute-start(bf16[768,384]{1,0:T(8,128)(2,1)} %collective-permute-done.refs_6_.refs_4_), channel_id=1, source_target_pairs={{0,16},{16,0},{1,17},{17,1},{2,18},{18,2},{3,19},{19,3},{4,20},{20... | collective-permute-start | bytes 1769480 | tf_op jit(solution)/shard_map/ppermute | solution.py:634
  61.2 21.2 %collective-permute-start.9 = (bf16[384,768]{1,0:T(8,128)(2,1)}, bf16[384,768]{1,0:T(8,128)(2,1)}, u32[]{:S(2)}, u32[]{:S(2)}) collective-permute-start(bf16[384,768]{1,0:T(8,128)(2,1)} %collective-permute-done.1.refs_16_.refs_14_), channel_id=1, source_target_pairs={{0,1},{1,0},{2,3},{3,2},{4,5},{5,4},{6,7},{7,6},{8,9},{9,8},{10,11... | collective-permute-start | bytes 1769480 | tf_op jit(solution)/shard_map/ppermute | solution.py:634
  87.0 29.5 %collective-permute-start.16 = (bf16[264,768]{1,0:T(8,128)(2,1)S(1)}, bf16[264,768]{1,0:T(8,128)(2,1)S(1)}, u32[]{:S(2)}, u32[]{:S(2)}) collective-permute-start(bf16[264,768]{1,0:T(8,128)(2,1)S(1)} %get-tuple-element.220), channel_id=1, source_target_pairs={{0,8},{4,12},{8,0},{12,4},{1,9},{5,13},{9,1},{13,5},{2,10},{6,14},... | collective-permute-start | bytes 1216520 | tf_op jit(solution)/shard_map/ppermute | solution.py:634
  87.0 43.3 %collective-permute-start.19 = (bf16[264,768]{1,0:T(8,128)(2,1)S(1)}, bf16[264,768]{1,0:T(8,128)(2,1)S(1)}, u32[]{:S(2)}, u32[]{:S(2)}) collective-permute-start(bf16[264,768]{1,0:T(8,128)(2,1)S(1)} %get-tuple-element.231), channel_id=1, source_target_pairs={{0,12},{4,8},{8,4},{12,0},{1,13},{5,9},{9,5},{13,1},{2,14},{6,10},... | collective-permute-start | bytes 1216520 | tf_op jit(solution)/shard_map/ppermute | solution.py:634
  89.7 26.8 %collective-permute-start.17 = (bf16[576,768]{1,0:T(8,128)(2,1)S(1)}, bf16[576,768]{1,0:T(8,128)(2,1)S(1)}, u32[]{:S(2)}, u32[]{:S(2)}) collective-permute-start(bf16[576,768]{1,0:T(8,128)(2,1)S(1)} %pad_maximum_fusion.2.weight_ref), channel_id=1, source_target_pairs={{0,1},{1,0},{2,3},{3,2},{4,5},{5,4},{6,7},{7,6},{8,9},{9,8},{10,11... | collective-permute-start | bytes 2654216 | tf_op jit(solution)/shard_map/ppermute | solution.py:634
  90.5 25.9 %collective-permute-start.18 = (bf16[576,768]{1,0:T(8,128)(2,1)S(1)}, bf16[576,768]{1,0:T(8,128)(2,1)S(1)}, u32[]{:S(2)}, u32[]{:S(2)}) collective-permute-start(bf16[576,768]{1,0:T(8,128)(2,1)S(1)} %pad_maximum_fusion.2.weight_ref), channel_id=1, source_target_pairs={{0,2},{1,3},{2,0},{3,1},{4,6},{5,7},{6,4},{7,5},{8,10},{9,11},{10,... | collective-permute-start | bytes 2654216 | tf_op jit(solution)/shard_map/ppermute | solution.py:634
  112.5 52.9 %collective-permute-start.21 = (bf16[264,768]{1,0:T(8,128)(2,1)}, bf16[264,768]{1,0:T(8,128)(2,1)S(1)}, u32[]{:S(2)}, u32[]{:S(2)}) collective-permute-start(bf16[264,768]{1,0:T(8,128)(2,1)} %get-tuple-element.259), channel_id=1, source_target_pairs={{0,4},{4,0},{8,12},{12,8},{1,5},{5,1},{9,13},{13,9},{2,6},{6,2},{1... | collective-permute-start | bytes 1216520 | tf_op jit(solution)/shard_map/ppermute | solution.py:634
  117.7 27.0 %collective-permute-start.20 = (bf16[576,768]{1,0:T(8,128)(2,1)S(1)}, bf16[576,768]{1,0:T(8,128)(2,1)S(1)}, u32[]{:S(2)}, u32[]{:S(2)}) collective-permute-start(bf16[576,768]{1,0:T(8,128)(2,1)S(1)} %pad_maximum_fusion.2.weight_ref), channel_id=1, source_target_pairs={{0,3},{1,2},{2,1},{3,0},{4,7},{5,6},{6,5},{7,4},{8,11},{9,10},{10,... | collective-permute-start | bytes 2654216 | tf_op jit(solution)/shard_map/ppermute | solution.py:634
  130.4 35.0 %collective-permute-start.22 = (bf16[264,768]{1,0:T(8,128)(2,1)S(1)}, bf16[264,768]{1,0:T(8,128)(2,1)S(1)}, u32[]{:S(2)}, u32[]{:S(2)}) collective-permute-start(bf16[264,768]{1,0:T(8,128)(2,1)S(1)} %get-tuple-element.260), channel_id=1, source_target_pairs={{0,8},{4,12},{8,0},{12,4},{1,9},{5,13},{9,1},{13,5},{2,10},{6,14},... | collective-permute-start | bytes 1216520 | tf_op jit(solution)/shard_map/ppermute | solution.py:634
  143.2 22.2 %collective-permute-start.23 = (bf16[264,768]{1,0:T(8,128)(2,1)S(1)}, bf16[264,768]{1,0:T(8,128)(2,1)S(1)}, u32[]{:S(2)}, u32[]{:S(2)}) collective-permute-start(bf16[264,768]{1,0:T(8,128)(2,1)S(1)} %get-tuple-element.261), channel_id=1, source_target_pairs={{0,12},{4,8},{8,4},{12,0},{1,13},{5,9},{9,5},{13,1},{2,14},{6,10},... | collective-permute-start | bytes 1216520 | tf_op jit(solution)/shard_map/ppermute | solution.py:634
  165.4 27.9 %collective-permute-start.24 = (bf16[4,768,384]{2,1,0:T(8,128)(2,1)}, bf16[4,768,384]{2,1,0:T(8,128)(2,1)}, u32[]{:S(2)}, u32[]{:S(2)}) collective-permute-start(bf16[4,768,384]{2,1,0:T(8,128)(2,1)} %get-tuple-element.267), channel_id=1, source_target_pairs={{0,16},{16,0},{1,17},{17,1},{2,18},{18,2},{3,19},{19,3},{4,20},{20... | collective-permute-start | bytes 7077896 | tf_op jit(solution)/shard_map/ppermute | solution.py:634
  165.5 27.8 %collective-permute-start.25 = (bf16[4,768,384]{2,1,0:T(8,128)(2,1)}, bf16[4,768,384]{2,1,0:T(8,128)(2,1)}, u32[]{:S(2)}, u32[]{:S(2)}) collective-permute-start(bf16[4,768,384]{2,1,0:T(8,128)(2,1)} %get-tuple-element.268), channel_id=1, source_target_pairs={{0,16},{16,0},{1,17},{17,1},{2,18},{18,2},{3,19},{19,3},{4,20},{20... | collective-permute-start | bytes 7077896 | tf_op jit(solution)/shard_map/ppermute | solution.py:634
  178.2 49.6 %collective-permute-start.28 = (bf16[256,768]{1,0:T(8,128)(2,1)}, bf16[256,768]{1,0:T(8,128)(2,1)}, u32[]{:S(2)}, u32[]{:S(2)}) collective-permute-start(bf16[256,768]{1,0:T(8,128)(2,1)} %get-tuple-element.282), channel_id=1, source_target_pairs={{0,4},{4,0},{8,12},{12,8},{1,5},{5,1},{9,13},{13,9},{2,6},{6,2},{1... | collective-permute-start | bytes 1179656 | tf_op jit(solution)/shard_map/ppermute | solution.py:634
  179.6 48.2 %collective-permute-start.29 = (bf16[256,768]{1,0:T(8,128)(2,1)}, bf16[256,768]{1,0:T(8,128)(2,1)}, u32[]{:S(2)}, u32[]{:S(2)}) collective-permute-start(bf16[256,768]{1,0:T(8,128)(2,1)} %get-tuple-element.283), channel_id=1, source_target_pairs={{0,8},{4,12},{8,0},{12,4},{1,9},{5,13},{9,1},{13,5},{2,10},{6,14},... | collective-permute-start | bytes 1179656 | tf_op jit(solution)/shard_map/ppermute | solution.py:634
  181.2 46.6 %collective-permute-start.30 = (bf16[256,768]{1,0:T(8,128)(2,1)}, bf16[256,768]{1,0:T(8,128)(2,1)}, u32[]{:S(2)}, u32[]{:S(2)}) collective-permute-start(bf16[256,768]{1,0:T(8,128)(2,1)} %get-tuple-element.284), channel_id=1, source_target_pairs={{0,12},{4,8},{8,4},{12,0},{1,13},{5,9},{9,5},{13,1},{2,14},{6,10},... | collective-permute-start | bytes 1179656 | tf_op jit(solution)/shard_map/ppermute | solution.py:634
  189.5 38.3 %all-to-all-start.3 = ((bf16[4,200,768]{2,1,0:T(8,128)(2,1)}), bf16[4,200,768]{2,1,0:T(8,128)(2,1)S(1)}, u32[]{:S(2)}, u32[]{:S(2)}) async-start(bf16[4,200,768]{2,1,0:T(8,128)(2,1)} %pad_maximum_fusion), calls=%async_computation.3 | async-start | bytes 2457600 | tf_op jit(solution)/shard_map/all_to_all | solution.py:638
  196.4 37.5 %collective-permute-start.26 = (bf16[2,768,384]{2,1,0:T(8,128)(2,1)}, bf16[2,768,384]{2,1,0:T(8,128)(2,1)}, u32[]{:S(2)}, u32[]{:S(2)}) collective-permute-start(bf16[2,768,384]{2,1,0:T(8,128)(2,1)} %add_convert_fusion.3), channel_id=1, source_target_pairs={{0,1},{1,0},{2,3},{3,2},{4,5},{5,4},{6,7},{7,6},{8,9},{9,8},{10,11... | collective-permute-start | bytes 3538952 | tf_op jit(solution)/shard_map/ppermute | solution.py:634
  201.0 33.0 %collective-permute-start.27 = (bf16[2,768,384]{2,1,0:T(8,128)(2,1)}, bf16[2,768,384]{2,1,0:T(8,128)(2,1)}, u32[]{:S(2)}, u32[]{:S(2)}) collective-permute-start(bf16[2,768,384]{2,1,0:T(8,128)(2,1)} %add_convert_fusion.2), channel_id=1, source_target_pairs={{0,2},{1,3},{2,0},{3,1},{4,6},{5,7},{6,4},{7,5},{8,10},{9,11},{10,... | collective-permute-start | bytes 3538952 | tf_op jit(solution)/shard_map/ppermute | solution.py:634
  243.8 43.7 %collective-permute-start.32 = (bf16[576,512]{1,0:T(8,128)(2,1)}, bf16[576,512]{1,0:T(8,128)(2,1)}, u32[]{:S(2)}, u32[]{:S(2)}) collective-permute-start(bf16[576,512]{1,0:T(8,128)(2,1)} %get-tuple-element.330), channel_id=1, source_target_pairs={{0,1},{1,0},{2,3},{3,2},{4,5},{5,4},{6,7},{7,6},{8,9},{9,8},{10,11... | collective-permute-start | bytes 1769480 | tf_op jit(solution)/shard_map/ppermute | solution.py:634
  245.2 42.3 %collective-permute-start.33 = (bf16[576,512]{1,0:T(8,128)(2,1)}, bf16[576,512]{1,0:T(8,128)(2,1)}, u32[]{:S(2)}, u32[]{:S(2)}) collective-permute-start(bf16[576,512]{1,0:T(8,128)(2,1)} %get-tuple-element.329), channel_id=1, source_target_pairs={{0,2},{1,3},{2,0},{3,1},{4,6},{5,7},{6,4},{7,5},{8,10},{9,11},{10,... | collective-permute-start | bytes 1769480 | tf_op jit(solution)/shard_map/ppermute | solution.py:634
  245.8 41.7 %collective-permute-start.34 = (bf16[576,512]{1,0:T(8,128)(2,1)}, bf16[576,512]{1,0:T(8,128)(2,1)}, u32[]{:S(2)}, u32[]{:S(2)}) collective-permute-start(bf16[576,512]{1,0:T(8,128)(2,1)} %get-tuple-element.328), channel_id=1, source_target_pairs={{0,3},{1,2},{2,1},{3,0},{4,7},{5,6},{6,5},{7,4},{8,11},{9,10},{10,... | collective-permute-start | bytes 1769480 | tf_op jit(solution)/shard_map/ppermute | solution.py:634
  249.3 38.2 %all-to-all-start.4 = ((bf16[4,104,768]{2,1,0:T(8,128)(2,1)}), bf16[4,104,768]{2,1,0:T(8,128)(2,1)S(1)}, u32[]{:S(2)}, u32[]{:S(2)}) async-start(bf16[4,104,768]{2,1,0:T(8,128)(2,1)} %bitcast.21), calls=%async_computation.4 | async-start | bytes 1277952 | tf_op jit(solution)/shard_map/all_to_all | solution.py:638
  255.6 29.4 %collective-permute-start.36 = (bf16[768,384]{1,0:T(8,128)(2,1)S(1)}, bf16[768,384]{1,0:T(8,128)(2,1)S(1)}, u32[]{:S(2)}, u32[]{:S(2)}) collective-permute-start(bf16[768,384]{1,0:T(8,128)(2,1)S(1)} %slice_bitcast_fusion), channel_id=1, source_target_pairs={{0,1},{1,0},{2,3},{3,2},{4,5},{5,4},{6,7},{7,6},{8,9},{9,8},{10,11... | collective-permute-start | bytes 1769480 | tf_op jit(solution)/shard_map/ppermute | solution.py:634
  259.3 26.9 %collective-permute-start.35 = (bf16[768,384]{1,0:T(8,128)(2,1)S(1)}, bf16[768,384]{1,0:T(8,128)(2,1)S(1)}, u32[]{:S(2)}, u32[]{:S(2)}) collective-permute-start(bf16[768,384]{1,0:T(8,128)(2,1)S(1)} %slice_bitcast_fusion.2), channel_id=1, source_target_pairs={{0,2},{1,3},{2,0},{3,1},{4,6},{5,7},{6,4},{7,5},{8,10},{9,11},{10,... | collective-permute-start | bytes 1769480 | tf_op jit(solution)/shard_map/ppermute | solution.py:634
  289.3 21.9 %all-to-all-start.5 = ((bf16[4,104,768]{2,1,0:T(8,128)(2,1)}), bf16[4,104,768]{2,1,0:T(8,128)(2,1)}, u32[]{:S(2)}, u32[]{:S(2)}) async-start(bf16[4,104,768]{2,1,0:T(8,128)(2,1)} %broadcast_in_dim.26), calls=%async_computation.5 | async-start | bytes 1277952 | tf_op jit(solution)/shard_map/all_to_all | solution.py:638
  (72 other events, 597.2 us)
